TPU v7x, 512 devices: a whole 4x4x16 slice. The times are simulated.
512 devices in a mesh: gx: 16 (over y, x_hi, core), gy: 32 (over x_lo, z).
Axes of the slice: x: 4 (x_hi: 2, x_lo: 2; x = x_hi * 2 + x_lo), y: 4, z: 16, core: 2. Of those that a mesh axis runs over, the one named last changes fastest.
Arguments:
- abundance_start: float32 [1, 12, 1024, 4096], P(None, None, 'gx', 'gy'), may hold values from 0 to 1
- measured: bfloat16 [1, 32, 1024, 4096], P(None, None, 'gx', 'gy'), may hold values from 0 to 11, as said below
- spectra: float32 [32, 12], replicated, may hold values from 0.02 to 0.3
- taps_x: float32 [33], replicated, may hold values from 0.01 to 0.05
- taps_y: float32 [33], replicated, may hold values from 0.01 to 0.05
Outputs:
- abundance: float32 [1, 12, 1024, 4096], P(None, None, 'gx', 'gy')
Inputs may be any that keep to these rules, and one draw needn't show every extreme that they name: `measured`: nonnegative intensities.
All inputs are finite; a program needn't handle non-finite values.
Results may differ from a plain program's by a relative error of at most 0.0003.
Values sent between devices are 32-bit elements; how exact they have to be, the bound alone decides.
No kernel may reach another device: no remote copies, remote signals or barrier semaphores. Data moves between devices by JAX's collectives and lax.ppermute only.
A program may use at most 64 MiB of HBM per device.

v0:
```python
import jax
import jax.numpy as jnp
from jax import lax
from jax.sharding import PartitionSpec as P

TAPS = 33
ITERS = 2


precise = lax.Precision.HIGHEST
tiny_floor = 1e-06


def extended(block, sides, width):
    for axis, dim in sides:
        count = lax.axis_size(axis)
        forward = [(i, i + 1) for i in range(count - 1)]
        backward = [(target, source) for source, target in forward]
        low = lax.ppermute(
            lax.slice_in_dim(block, block.shape[dim] - width, None, axis=dim), axis, forward
        )
        high = lax.ppermute(lax.slice_in_dim(block, 0, width, axis=dim), axis, backward)
        block = jnp.concatenate([low, block, high], axis=dim)
    return block


def banded(profile, length):
    reach = profile.shape[0]
    in_index = jnp.arange(length + reach - 1)[:, None]
    out_index = jnp.arange(length)[None, :]
    offset = in_index - out_index
    matches = (offset[:, :, None] == jnp.arange(reach)[None, None, :]).astype(profile.dtype)
    return jnp.einsum("abt,t->ab", matches, profile, precision=precise)


def smear(padded, band_x, band_y):
    along_x = jnp.einsum("zfay,ab->zfby", padded, band_x, precision=precise)
    return jnp.einsum("zfxa,ab->zfxb", along_x, band_y, precision=precise)


def fetch_rim(fields, margin):
    return extended(fields, (("gx", 2), ("gy", 3)), margin)


def local(abundance_start, measured, spectra, taps_x, taps_y):
    size_x = abundance_start.shape[2]
    size_y = abundance_start.shape[3]
    margin = TAPS // 2
    fwd_x = banded(taps_x, size_x)
    fwd_y = banded(taps_y, size_y)
    observed = measured.astype(jnp.float32)
    back_x = banded(taps_x[::-1], size_x)
    back_y = banded(taps_y[::-1], size_y)
    abundance = abundance_start
    for iteration in range(ITERS):
        padded = fetch_rim(abundance, margin)
        image = smear(padded, fwd_x, fwd_y)
        mixed_image = jnp.einsum("cf,zfxy->zcxy", spectra, image, precision=precise)
        misfit = mixed_image - observed
        projected = jnp.einsum("cf,zcxy->zfxy", spectra, misfit, precision=precise)
        adjoint_pad = extended(projected, (("gx", 2), ("gy", 3)), margin)
        gradient = smear(adjoint_pad, back_x, back_y)
        grad_pad = extended(gradient, (("gx", 2), ("gy", 3)), margin)
        grad_local = jnp.sum(gradient * gradient)
        grad_sq = lax.psum(grad_local, ("gx", "gy"))
        probe_image = jnp.einsum(
            "cf,zfxy->zcxy", spectra, smear(grad_pad, fwd_x, fwd_y), precision=precise
        )
        image_local = jnp.sum(probe_image * probe_image)
        image_sq = lax.psum(image_local, ("gx", "gy"))
        step_length = grad_sq / (image_sq + tiny_floor)
        abundance = jnp.maximum(abundance - step_length * gradient, 0.0)
    return abundance


def solution(mesh):
    in_specs = (P(None, None, "gx", "gy"), P(None, None, "gx", "gy"), P(), P(), P())
    out_specs = P(None, None, "gx", "gy")
    return jax.shard_map(local, mesh=mesh, in_specs=in_specs, out_specs=out_specs, check_vma=False)
```

profile of v0, /device:TPU:1, one launch (start us, length us, event | category | flops | bytes accessed | tf_op | source)
XLA Modules:
  0.0 381.7 jit_solution(7507737955583656348)
XLA Ops:
  0.0 1.0 fusion.76
  1.0 6.0 %collective-permute-start = (f32[1,12,16,128]{3,2,1,0:T(8,128)S(1)}, f32[1,12,16,128]{3,2,1,0:T(8,128)S(1)}, u32[]{:S(2)}, u32[]{:S(2)}) collective-permute-start(f32[1,12,16,128]{3,2,1,0:T(8,128)S(1)} %get-tuple-element.31), channel_id=1, source_target_pairs={{0,32},{32,64},{64,96},{96,128},{128,160},{160,192},{192,224},{224... | collective-permute-start | bytes 294920 | tf_op jit(solution)/shard_map/ppermute | solution.py:19
  7.0 4.0 %collective-permute-start.1 = (f32[1,12,16,128]{3,2,1,0:T(8,128)S(1)}, f32[1,12,16,128]{3,2,1,0:T(8,128)S(1)}, u32[]{:S(2)}, u32[]{:S(2)}) collective-permute-start(f32[1,12,16,128]{3,2,1,0:T(8,128)S(1)} %get-tuple-element.32), channel_id=1, source_target_pairs={{32,0},{64,32},{96,64},{128,96},{160,128},{192,160},{224,192},{256... | collective-permute-start | bytes 294920 | tf_op jit(solution)/shard_map/ppermute | solution.py:22
  11.5 1.3 fusion.2
  13.2 1.2 collective-permute-done.1
  15.0 0.8 pad_maximum_fusion.7
  15.8 3.5 collective-permute-start.2
  19.4 1.3 collective-permute-start.3
  21.4 3.7 collective-permute-done.3
  25.0 3.2 convolution_bitcast_fusion.7
  28.2 0.8 fusion.77
  29.3 1.5 fusion.5
  30.8 0.7 convolution_bitcast_fusion.9
  31.5 3.1 collective-permute-start.4
  34.5 1.9 collective-permute-start.5
  36.5 1.3 fusion
  37.9 4.5 %collective-permute-done.5 = f32[1,12,16,128]{3,1,2,0:T(8,128)S(1)} collective-permute-done((f32[1,12,16,128]{3,1,2,0:T(8,128)S(1)}, f32[1,12,16,128]{3,1,2,0:T(8,128)S(1)}, u32[]{:S(2)}, u32[]{:S(2)}) %collective-permute-start.5) | collective-permute-done | bytes 98336 | tf_op jit(solution)/shard_map/ppermute | solution.py:22
  42.7 0.9 copy.82
  43.8 1.3 collective-permute-start.7
  45.1 4.4 %collective-permute-start.6 = (f32[1,12,96,16]{2,3,1,0:T(8,128)}, f32[1,12,96,16]{2,3,1,0:T(8,128)S(1)}, u32[]{:S(2)}, u32[]{:S(2)}) collective-permute-start(f32[1,12,96,16]{2,3,1,0:T(8,128)} %copy.82), channel_id=1, source_target_pairs={{0,1},{1,2},{2,3},{3,4},{4,5},{5,6},{6,7},{7,8},{8,9},{9,10},{10,1... | collective-permute-start | bytes 221192 | tf_op jit(solution)/shard_map/ppermute | solution.py:19
  49.5 1.4 fusion.43
  51.6 1.3 copy.85
  52.9 0.7 maximum_bitcast_fusion
  53.6 1.5 convolution_bitcast_fusion.6
  55.1 1.4 multiply_reduce_fusion.1
  56.5 2.7 collective-permute-start.8
  59.2 1.9 collective-permute-start.9
  61.2 5.8 %collective-permute-done.9 = f32[1,12,16,128]{3,2,1,0:T(8,128)S(1)} collective-permute-done((f32[1,12,16,128]{3,2,1,0:T(8,128)S(1)}, f32[1,12,16,128]{3,2,1,0:T(8,128)S(1)}, u32[]{:S(2)}, u32[]{:S(2)}) %collective-permute-start.9) | collective-permute-done | bytes 98336 | tf_op jit(solution)/shard_map/ppermute | solution.py:22
  67.5 4.2 %collective-permute-start.10 = (f32[1,12,96,16]{2,3,1,0:T(8,128)S(1)}, f32[1,12,96,16]{2,3,1,0:T(8,128)S(1)}, u32[]{:S(2)}, u32[]{:S(2)}) collective-permute-start(f32[1,12,96,16]{2,3,1,0:T(8,128)S(1)} %copy.87), channel_id=1, source_target_pairs={{0,1},{1,2},{2,3},{3,4},{4,5},{5,6},{6,7},{7,8},{8,9},{9,10},{10,1... | collective-permute-start | bytes 221192 | tf_op jit(solution)/shard_map/ppermute | solution.py:19
  71.9 1.3 collective-permute-start.11
  73.6 5.2 %collective-permute-done.11 = f32[1,12,96,16]{2,3,1,0:T(8,128)S(1)} collective-permute-done((f32[1,12,96,16]{2,3,1,0:T(8,128)S(1)}, f32[1,12,96,16]{2,3,1,0:T(8,128)S(1)}, u32[]{:S(2)}, u32[]{:S(2)}) %collective-permute-start.11) | collective-permute-done | bytes 73760 | tf_op jit(solution)/shard_map/ppermute | solution.py:22
  79.0 1.2 convolution_bitcast_fusion.5
  80.2 0.8 fusion.78
  81.0 2.0 fusion.44
  83.0 115.5 %all-reduce.1 = (f32[]{:T(128)}, f32[]{:T(128)}) all-reduce(f32[]{:T(128)} %get-tuple-element.33, f32[]{:T(128)} %fusion.44), channel_id=1, replica_groups=mesh['gx'=16,'gy'=32] {'gx','gy'}, use_global_device_ids=true, to_apply=%region_1.0 | all-reduce | flops 2 | bytes 16 | tf_op jit(solution)/shard_map/psum | solution.py:65
  199.9 3.6 collective-permute-start.12
  203.5 1.9 collective-permute-start.13
  205.5 5.5 %collective-permute-done.13 = f32[1,12,16,128]{3,2,1,0:T(8,128)S(1)} collective-permute-done((f32[1,12,16,128]{3,2,1,0:T(8,128)S(1)}, f32[1,12,16,128]{3,2,1,0:T(8,128)S(1)}, u32[]{:S(2)}, u32[]{:S(2)}) %collective-permute-start.13) | collective-permute-done | bytes 98336 | tf_op jit(solution)/shard_map/ppermute | solution.py:22
  211.4 1.7 collective-permute-start.14
  213.3 1.5 collective-permute-start.15
  215.0 3.6 collective-permute-done.15
  218.9 1.3 convolution_bitcast_fusion.4
  220.1 0.8 fusion.79
  220.9 1.5 fusion.7
  223.1 3.3 collective-permute-start.16
  226.4 1.9 collective-permute-start.17
  228.3 5.9 %collective-permute-done.17 = f32[1,12,16,128]{3,1,2,0:T(8,128)S(1)} collective-permute-done((f32[1,12,16,128]{3,1,2,0:T(8,128)S(1)}, f32[1,12,16,128]{3,1,2,0:T(8,128)S(1)}, u32[]{:S(2)}, u32[]{:S(2)}) %collective-permute-start.17) | collective-permute-done | bytes 98336 | tf_op jit(solution)/shard_map/ppermute | solution.py:22
  234.8 2.4 collective-permute-start.18
  237.4 1.3 collective-permute-start.19
  239.2 3.6 collective-permute-done.19
  243.1 0.7 maximum_bitcast_fusion.1
  243.8 1.5 convolution_bitcast_fusion.3
  245.3 1.4 multiply_reduce_fusion
  246.7 3.2 collective-permute-start.20
  249.9 1.9 collective-permute-start.21
  251.9 5.5 %collective-permute-done.21 = f32[1,12,16,128]{3,2,1,0:T(8,128)S(1)} collective-permute-done((f32[1,12,16,128]{3,2,1,0:T(8,128)S(1)}, f32[1,12,16,128]{3,2,1,0:T(8,128)S(1)}, u32[]{:S(2)}, u32[]{:S(2)}) %collective-permute-start.21) | collective-permute-done | bytes 98336 | tf_op jit(solution)/shard_map/ppermute | solution.py:22
  257.8 4.1 %collective-permute-start.22 = (f32[1,12,96,16]{2,3,1,0:T(8,128)S(1)}, f32[1,12,96,16]{2,3,1,0:T(8,128)S(1)}, u32[]{:S(2)}, u32[]{:S(2)}) collective-permute-start(f32[1,12,96,16]{2,3,1,0:T(8,128)S(1)} %copy.104), channel_id=1, source_target_pairs={{0,1},{1,2},{2,3},{3,4},{4,5},{5,6},{6,7},{7,8},{8,9},{9,10},{10,1... | collective-permute-start | bytes 221192 | tf_op jit(solution)/shard_map/ppermute | solution.py:19
  262.1 1.6 collective-permute-start.23
  263.9 3.8 %collective-permute-done.23 = f32[1,12,96,16]{2,3,1,0:T(8,128)S(1)} collective-permute-done((f32[1,12,96,16]{2,3,1,0:T(8,128)S(1)}, f32[1,12,96,16]{2,3,1,0:T(8,128)S(1)}, u32[]{:S(2)}, u32[]{:S(2)}) %collective-permute-start.23) | collective-permute-done | bytes 73760 | tf_op jit(solution)/shard_map/ppermute | solution.py:22
  268.0 1.3 convolution_bitcast_fusion.2
  269.2 0.8 fusion.80
  270.0 2.0 fusion.45
  272.0 107.6 %all-reduce = (f32[]{:T(128)}, f32[]{:T(128)}) all-reduce(f32[]{:T(128)} %get-tuple-element.35, f32[]{:T(128)} %fusion.45), channel_id=1, replica_groups=mesh['gx'=16,'gy'=32] {'gx','gy'}, use_global_device_ids=true, to_apply=%region_5.0 | all-reduce | flops 2 | bytes 16 | tf_op jit(solution)/shard_map/psum | solution.py:65
  380.9 0.8 fusion.50
  (74 shorter events, 9.5 us)
Async XLA Ops:
  0.0 29.0 %copy-start = (f32[32,12]{0,1:T(8,128)S(1)}, f32[32,12]{0,1:T(8,128)}, u32[]{:S(2)}) copy-start(f32[32,12]{0,1:T(8,128)} %param.7) | copy-start | bytes 4612
  0.0 11.5 %copy-start.6 = (f32[33]{0:T(128)S(1)}, f32[33]{0:T(128)}, u32[]{:S(2)}) copy-start(f32[33]{0:T(128)} %param.9) | copy-start | bytes 400
  1.0 13.8 %collective-permute-start = (f32[1,12,16,128]{3,2,1,0:T(8,128)S(1)}, f32[1,12,16,128]{3,2,1,0:T(8,128)S(1)}, u32[]{:S(2)}, u32[]{:S(2)}) collective-permute-start(f32[1,12,16,128]{3,2,1,0:T(8,128)S(1)} %get-tuple-element.31), channel_id=1, source_target_pairs={{0,32},{32,64},{64,96},{96,128},{128,160},{160,192},{192,224},{224... | collective-permute-start | bytes 294920 | tf_op jit(solution)/shard_map/ppermute | solution.py:19
  7.0 7.4 %collective-permute-start.1 = (f32[1,12,16,128]{3,2,1,0:T(8,128)S(1)}, f32[1,12,16,128]{3,2,1,0:T(8,128)S(1)}, u32[]{:S(2)}, u32[]{:S(2)}) collective-permute-start(f32[1,12,16,128]{3,2,1,0:T(8,128)S(1)} %get-tuple-element.32), channel_id=1, source_target_pairs={{32,0},{64,32},{96,64},{128,96},{160,128},{192,160},{224,192},{256... | collective-permute-start | bytes 294920 | tf_op jit(solution)/shard_map/ppermute | solution.py:22
  11.5 1.3 copy-start.3
  11.5 1.4 copy-start.1
  12.9 7.7 %copy-start.5 = (pred[96,64,33]{0,1,2:T(32,128)(4,1)}, pred[96,64,33]{0,1,2:T(32,128)(4,1)S(1)}, u32[]{:S(2)}) copy-start(pred[96,64,33]{0,1,2:T(32,128)(4,1)S(1)} %iota_compare_fusion.1) | copy-start | bytes 608260
  15.0 5.7 %copy-start.7 = (f32[33]{0:T(128)S(1)}, f32[33]{0:T(128)}, u32[]{:S(2)}) copy-start(f32[33]{0:T(128)} %param.8) | copy-start | bytes 400
  15.8 5.5 %collective-permute-start.2 = (f32[1,12,96,16]{2,3,1,0:T(8,128)}, f32[1,12,96,16]{2,3,1,0:T(8,128)S(1)}, u32[]{:S(2)}, u32[]{:S(2)}) collective-permute-start(f32[1,12,96,16]{2,3,1,0:T(8,128)} %get-tuple-element.9), channel_id=1, source_target_pairs={{0,1},{1,2},{2,3},{3,4},{4,5},{5,6},{6,7},{7,8},{8,9},{9,10},{10,1... | collective-permute-start | bytes 221192 | tf_op jit(solution)/shard_map/ppermute | solution.py:19
  19.4 5.7 %collective-permute-start.3 = (f32[1,12,96,16]{2,3,1,0:T(8,128)S(1)}, f32[1,12,96,16]{2,3,1,0:T(8,128)}, u32[]{:S(2)}, u32[]{:S(2)}) collective-permute-start(f32[1,12,96,16]{2,3,1,0:T(8,128)S(1)} %get-tuple-element.10), channel_id=1, source_target_pairs={{1,0},{2,1},{3,2},{4,3},{5,4},{6,5},{7,6},{8,7},{9,8},{10,9},{11,1... | collective-permute-start | bytes 221192 | tf_op jit(solution)/shard_map/ppermute | solution.py:22
  28.2 1.0 copy-start.2
  30.8 5.7 %copy-start.4 = (pred[160,128,33]{1,0,2:T(32,128)(4,1)S(1)}, pred[160,128,33]{1,0,2:T(32,128)(4,1)}, u32[]{:S(2)}) copy-start(pred[160,128,33]{1,0,2:T(32,128)(4,1)} %copy-done.3) | copy-start | bytes 2027524
  31.5 6.4 %collective-permute-start.4 = (f32[1,12,16,128]{3,1,2,0:T(8,128)S(1)}, f32[1,12,16,128]{3,1,2,0:T(8,128)S(1)}, u32[]{:S(2)}, u32[]{:S(2)}) collective-permute-start(f32[1,12,16,128]{3,1,2,0:T(8,128)S(1)} %get-tuple-element.23), channel_id=1, source_target_pairs={{0,32},{32,64},{64,96},{96,128},{128,160},{160,192},{192,224},{224... | collective-permute-start | bytes 294920 | tf_op jit(solution)/shard_map/ppermute | solution.py:19
  34.5 7.8 %collective-permute-start.5 = (f32[1,12,16,128]{3,1,2,0:T(8,128)S(1)}, f32[1,12,16,128]{3,1,2,0:T(8,128)S(1)}, u32[]{:S(2)}, u32[]{:S(2)}) collective-permute-start(f32[1,12,16,128]{3,1,2,0:T(8,128)S(1)} %get-tuple-element.24), channel_id=1, source_target_pairs={{32,0},{64,32},{96,64},{128,96},{160,128},{192,160},{224,192},{256... | collective-permute-start | bytes 294920 | tf_op jit(solution)/shard_map/ppermute | solution.py:22
  43.8 7.8 %collective-permute-start.7 = (f32[1,12,96,16]{2,3,1,0:T(8,128)S(1)}, f32[1,12,96,16]{2,3,1,0:T(8,128)}, u32[]{:S(2)}, u32[]{:S(2)}) collective-permute-start(f32[1,12,96,16]{2,3,1,0:T(8,128)S(1)} %copy.83), channel_id=1, source_target_pairs={{1,0},{2,1},{3,2},{4,3},{5,4},{6,5},{7,6},{8,7},{9,8},{10,9},{11,1... | collective-permute-start | bytes 221192 | tf_op jit(solution)/shard_map/ppermute | solution.py:22
  45.1 6.1 %collective-permute-start.6 = (f32[1,12,96,16]{2,3,1,0:T(8,128)}, f32[1,12,96,16]{2,3,1,0:T(8,128)S(1)}, u32[]{:S(2)}, u32[]{:S(2)}) collective-permute-start(f32[1,12,96,16]{2,3,1,0:T(8,128)} %copy.82), channel_id=1, source_target_pairs={{0,1},{1,2},{2,3},{3,4},{4,5},{5,6},{6,7},{7,8},{8,9},{9,10},{10,1... | collective-permute-start | bytes 221192 | tf_op jit(solution)/shard_map/ppermute | solution.py:19
  56.5 4.7 %collective-permute-start.8 = (f32[1,12,16,128]{3,2,1,0:T(8,128)S(1)}, f32[1,12,16,128]{3,2,1,0:T(8,128)S(1)}, u32[]{:S(2)}, u32[]{:S(2)}) collective-permute-start(f32[1,12,16,128]{3,2,1,0:T(8,128)S(1)} %get-tuple-element.29), channel_id=1, source_target_pairs={{0,32},{32,64},{64,96},{96,128},{128,160},{160,192},{192,224},{224... | collective-permute-start | bytes 294920 | tf_op jit(solution)/shard_map/ppermute | solution.py:19
  59.2 7.8 %collective-permute-start.9 = (f32[1,12,16,128]{3,2,1,0:T(8,128)S(1)}, f32[1,12,16,128]{3,2,1,0:T(8,128)S(1)}, u32[]{:S(2)}, u32[]{:S(2)}) collective-permute-start(f32[1,12,16,128]{3,2,1,0:T(8,128)S(1)} %get-tuple-element.30), channel_id=1, source_target_pairs={{32,0},{64,32},{96,64},{128,96},{160,128},{192,160},{224,192},{256... | collective-permute-start | bytes 294920 | tf_op jit(solution)/shard_map/ppermute | solution.py:22
  67.5 5.8 %collective-permute-start.10 = (f32[1,12,96,16]{2,3,1,0:T(8,128)S(1)}, f32[1,12,96,16]{2,3,1,0:T(8,128)S(1)}, u32[]{:S(2)}, u32[]{:S(2)}) collective-permute-start(f32[1,12,96,16]{2,3,1,0:T(8,128)S(1)} %copy.87), channel_id=1, source_target_pairs={{0,1},{1,2},{2,3},{3,4},{4,5},{5,6},{6,7},{7,8},{8,9},{9,10},{10,1... | collective-permute-start | bytes 221192 | tf_op jit(solution)/shard_map/ppermute | solution.py:19
  71.9 6.8 %collective-permute-start.11 = (f32[1,12,96,16]{2,3,1,0:T(8,128)S(1)}, f32[1,12,96,16]{2,3,1,0:T(8,128)S(1)}, u32[]{:S(2)}, u32[]{:S(2)}) collective-permute-start(f32[1,12,96,16]{2,3,1,0:T(8,128)S(1)} %copy.88), channel_id=1, source_target_pairs={{1,0},{2,1},{3,2},{4,3},{5,4},{6,5},{7,6},{8,7},{9,8},{10,9},{11,1... | collective-permute-start | bytes 221192 | tf_op jit(solution)/shard_map/ppermute | solution.py:22
  199.9 5.6 %collective-permute-start.12 = (f32[1,12,16,128]{3,2,1,0:T(8,128)S(1)}, f32[1,12,16,128]{3,2,1,0:T(8,128)S(1)}, u32[]{:S(2)}, u32[]{:S(2)}) collective-permute-start(f32[1,12,16,128]{3,2,1,0:T(8,128)S(1)} %get-tuple-element.27), channel_id=1, source_target_pairs={{0,32},{32,64},{64,96},{96,128},{128,160},{160,192},{192,224},{224... | collective-permute-start | bytes 294920 | tf_op jit(solution)/shard_map/ppermute | solution.py:19
  203.5 7.4 %collective-permute-start.13 = (f32[1,12,16,128]{3,2,1,0:T(8,128)S(1)}, f32[1,12,16,128]{3,2,1,0:T(8,128)S(1)}, u32[]{:S(2)}, u32[]{:S(2)}) collective-permute-start(f32[1,12,16,128]{3,2,1,0:T(8,128)S(1)} %get-tuple-element.28), channel_id=1, source_target_pairs={{32,0},{64,32},{96,64},{128,96},{160,128},{192,160},{224,192},{256... | collective-permute-start | bytes 294920 | tf_op jit(solution)/shard_map/ppermute | solution.py:22
  211.4 3.4 collective-permute-start.14
  213.3 5.4 %collective-permute-start.15 = (f32[1,12,96,16]{2,3,1,0:T(8,128)S(1)}, f32[1,12,96,16]{2,3,1,0:T(8,128)S(1)}, u32[]{:S(2)}, u32[]{:S(2)}) collective-permute-start(f32[1,12,96,16]{2,3,1,0:T(8,128)S(1)} %copy.94), channel_id=1, source_target_pairs={{1,0},{2,1},{3,2},{4,3},{5,4},{6,5},{7,6},{8,7},{9,8},{10,9},{11,1... | collective-permute-start | bytes 221192 | tf_op jit(solution)/shard_map/ppermute | solution.py:22
  223.1 5.2 %collective-permute-start.16 = (f32[1,12,16,128]{3,1,2,0:T(8,128)S(1)}, f32[1,12,16,128]{3,1,2,0:T(8,128)S(1)}, u32[]{:S(2)}, u32[]{:S(2)}) collective-permute-start(f32[1,12,16,128]{3,1,2,0:T(8,128)S(1)} %get-tuple-element.21), channel_id=1, source_target_pairs={{0,32},{32,64},{64,96},{96,128},{128,160},{160,192},{192,224},{224... | collective-permute-start | bytes 294920 | tf_op jit(solution)/shard_map/ppermute | solution.py:19
  226.4 7.8 %collective-permute-start.17 = (f32[1,12,16,128]{3,1,2,0:T(8,128)S(1)}, f32[1,12,16,128]{3,1,2,0:T(8,128)S(1)}, u32[]{:S(2)}, u32[]{:S(2)}) collective-permute-start(f32[1,12,16,128]{3,1,2,0:T(8,128)S(1)} %get-tuple-element.22), channel_id=1, source_target_pairs={{32,0},{64,32},{96,64},{128,96},{160,128},{192,160},{224,192},{256... | collective-permute-start | bytes 294920 | tf_op jit(solution)/shard_map/ppermute | solution.py:22
  234.8 4.0 %collective-permute-start.18 = (f32[1,12,96,16]{2,3,1,0:T(8,128)S(1)}, f32[1,12,96,16]{2,3,1,0:T(8,128)S(1)}, u32[]{:S(2)}, u32[]{:S(2)}) collective-permute-start(f32[1,12,96,16]{2,3,1,0:T(8,128)S(1)} %copy.99), channel_id=1, source_target_pairs={{0,1},{1,2},{2,3},{3,4},{4,5},{5,6},{6,7},{7,8},{8,9},{9,10},{10,1... | collective-permute-start | bytes 221192 | tf_op jit(solution)/shard_map/ppermute | solution.py:19
  237.4 5.3 %collective-permute-start.19 = (f32[1,12,96,16]{2,3,1,0:T(8,128)S(1)}, f32[1,12,96,16]{2,3,1,0:T(8,128)S(1)}, u32[]{:S(2)}, u32[]{:S(2)}) collective-permute-start(f32[1,12,96,16]{2,3,1,0:T(8,128)S(1)} %copy.100), channel_id=1, source_target_pairs={{1,0},{2,1},{3,2},{4,3},{5,4},{6,5},{7,6},{8,7},{9,8},{10,9},{11,1... | collective-permute-start | bytes 221192 | tf_op jit(solution)/shard_map/ppermute | solution.py:22
  246.7 5.2 %collective-permute-start.20 = (f32[1,12,16,128]{3,2,1,0:T(8,128)S(1)}, f32[1,12,16,128]{3,2,1,0:T(8,128)S(1)}, u32[]{:S(2)}, u32[]{:S(2)}) collective-permute-start(f32[1,12,16,128]{3,2,1,0:T(8,128)S(1)} %get-tuple-element.25), channel_id=1, source_target_pairs={{0,32},{32,64},{64,96},{96,128},{128,160},{160,192},{192,224},{224... | collective-permute-start | bytes 294920 | tf_op jit(solution)/shard_map/ppermute | solution.py:19
  249.9 7.4 %collective-permute-start.21 = (f32[1,12,16,128]{3,2,1,0:T(8,128)S(1)}, f32[1,12,16,128]{3,2,1,0:T(8,128)S(1)}, u32[]{:S(2)}, u32[]{:S(2)}) collective-permute-start(f32[1,12,16,128]{3,2,1,0:T(8,128)S(1)} %get-tuple-element.26), channel_id=1, source_target_pairs={{32,0},{64,32},{96,64},{128,96},{160,128},{192,160},{224,192},{256... | collective-permute-start | bytes 294920 | tf_op jit(solution)/shard_map/ppermute | solution.py:22
  257.8 5.8 %collective-permute-start.22 = (f32[1,12,96,16]{2,3,1,0:T(8,128)S(1)}, f32[1,12,96,16]{2,3,1,0:T(8,128)S(1)}, u32[]{:S(2)}, u32[]{:S(2)}) collective-permute-start(f32[1,12,96,16]{2,3,1,0:T(8,128)S(1)} %copy.104), channel_id=1, source_target_pairs={{0,1},{1,2},{2,3},{3,4},{4,5},{5,6},{6,7},{7,8},{8,9},{9,10},{10,1... | collective-permute-start | bytes 221192 | tf_op jit(solution)/shard_map/ppermute | solution.py:19
  262.1 5.6 %collective-permute-start.23 = (f32[1,12,96,16]{2,3,1,0:T(8,128)S(1)}, f32[1,12,96,16]{2,3,1,0:T(8,128)S(1)}, u32[]{:S(2)}, u32[]{:S(2)}) collective-permute-start(f32[1,12,96,16]{2,3,1,0:T(8,128)S(1)} %copy.105), channel_id=1, source_target_pairs={{1,0},{2,1},{3,2},{4,3},{5,4},{6,5},{7,6},{8,7},{9,8},{10,9},{11,1... | collective-permute-start | bytes 221192 | tf_op jit(solution)/shard_map/ppermute | solution.py:22
where the time goes:
time: 383 us; the launch traced here: 382 us
  blocking collectives  223 us (58%)
  starting transfers between devices  64.1 us (17%)
  waiting for transfers between devices  48.9 us (13%)
  matrix products  28.6 us (7%)
  local copies, waits for them, and re-layouts  10.1 us (3%)
    psum x2, blocking collectives, local(): grad_sq = lax.psum(grad_local, ('gx', 'gy'))  223 us
    ppermute x12, waiting for transfers between devices, extended(): lax.ppermute(lax.slice_in_dim(block, 0, width, axis=dim), axis, backward)  48.4 us
    ppermute x12, starting transfers between devices, extended(): lax.ppermute(lax.slice_in_dim(block, block.shape[dim] - width, None, axis...  42.2 us
    ppermute x12, starting transfers between devices, extended(): lax.ppermute(lax.slice_in_dim(block, 0, width, axis=dim), axis, backward)  21.9 us
    dot_general x6, matrix products, smear(): along_x = jnp.einsum('zfay,ab->zfby', padded, band_x, precision=precise)  9.93 us
  transfers between devices with their start and end apart: 24, of which 14 were waited for; matrix products, arithmetic and copies ran while one was open for 2% of the time, Pallas kernels for 0%

commit v1 on v0

v1 whole, which is shorter than its diff:
```python
import functools

import jax
import jax.numpy as jnp
from jax import lax
from jax.experimental import pallas as pl
from jax.experimental.pallas import tpu as pltpu
from jax.sharding import Mesh
from jax.sharding import PartitionSpec as P

TAPS = 33
ITERS = 2
FLUOR = 12
CHAN = 32
ROWS = 64
COLS = 128

HALF = TAPS // 2
A_HALO = 3 * HALF
P_HALO = 2 * HALF
G_HALO = HALF
A_ROWS = ROWS + 2 * A_HALO
P_ROWS = ROWS + 2 * P_HALO
G_ROWS = ROWS + 2 * G_HALO

GX = ("y", "x_hi", "core")
GY = ("x_lo", "z")
NEAR = ("y", "x_hi", "core", "x_lo")
FAR = "z"

tiny_floor = 1e-06
f32 = jnp.float32
bf16 = jnp.bfloat16


def smem():
    return pl.BlockSpec(memory_space=pltpu.SMEM)


def vmem():
    return pl.BlockSpec(memory_space=pltpu.VMEM)


def kernel(body, ins, outs, cost, scratch=()):
    return pl.pallas_call(
        body,
        in_specs=[smem() if kind == "s" else vmem() for kind in ins],
        out_specs=[vmem() for _ in outs],
        out_shape=[jax.ShapeDtypeStruct(shape, dtype) for shape, dtype in outs],
        scratch_shapes=list(scratch),
        compiler_params=pltpu.CompilerParams(vmem_limit_bytes=32 * 2**20),
        cost_estimate=pl.CostEstimate(flops=cost, bytes_accessed=cost // 100, transcendentals=0),
    )


def roll(x, by):
    by = by % 128
    return x if by == 0 else pltpu.roll(x, by, axis=x.ndim - 1)


def lane_of(shape):
    return lax.broadcasted_iota(jnp.int32, shape, len(shape) - 1)


def split(x):
    high = x.astype(bf16)
    return high, (x - high.astype(f32)).astype(bf16)


def dot(a, b):
    return jnp.dot(a, b, preferred_element_type=f32)


def dot_right(x, high, low):
    x_high, x_low = split(x)
    return dot(x_high, high) + dot(x_low, high) + dot(x_high, low)


def stacked(x, depth):
    high, low = split(x)
    parts = [high, low, high]
    spare = depth - 3 * x.shape[0]
    if spare:
        parts.append(jnp.zeros((spare, x.shape[1]), bf16))
    return jnp.concatenate(parts, axis=0)


def side_position(index, halo):
    left = index - COLS - halo
    right = index - halo
    position = jnp.where(index < COLS, index, jnp.where(index < COLS + halo, left, right))
    return jnp.where(index < COLS + 2 * halo, position, 1 << 20)


def tap_matrix(taps_ref, offset):
    out = jnp.zeros(offset.shape, f32)
    for t in range(TAPS):
        out = jnp.where(offset == t, taps_ref[t], out)
    return out


def inside(position, base, size):
    where = position + base
    return jnp.logical_and(where >= 0, where < size)


def exact_dot(a, b):
    return lax.dot_general(a, b, (((1,), (0,)), ((), ())), precision=lax.Precision.HIGHEST, preferred_element_type=f32)


def rows_cols(shape):
    return lax.broadcasted_iota(jnp.int32, shape, 0), lax.broadcasted_iota(jnp.int32, shape, 1)


def put_pair(x, high_ref, low_ref):
    high, low = split(x)
    high_ref[...] = high
    low_ref[...] = low


def put_left(x, part, ref):
    high, low = split(x)
    ref[...] = jnp.where(part < 2, high.astype(f32), low.astype(f32)).astype(bf16)


def matrices_body(sizes, at_ref, tx_ref, ty_ref, myh, myl, pyh, pyl, byh, byl, mx, px, bx):
    size_x, size_y = sizes
    base_x = at_ref[0] * ROWS
    base_y = at_ref[1] * COLS
    r, c = rows_cols((256, 256))
    source = side_position(r, P_HALO)
    target = side_position(c, G_HALO)
    okay = jnp.logical_and(inside(source, base_y, size_y), inside(target, base_y, size_y))
    put_pair(jnp.where(okay, tap_matrix(ty_ref, target - source + HALF), 0.0), pyh, pyl)
    source = side_position(r, A_HALO)
    middle = c - P_HALO
    okay = jnp.logical_and(inside(source, base_y, size_y), inside(middle, base_y, size_y))
    first = jnp.where(okay, tap_matrix(ty_ref, source - middle + HALF), 0.0)
    middle = r - P_HALO
    second = jnp.where(inside(target, base_y, size_y), tap_matrix(ty_ref, target - middle + HALF), 0.0)
    put_pair(exact_dot(first, second), myh, myl)
    r, c = rows_cols((256, 128))
    source = side_position(r, G_HALO)
    okay = inside(source, base_y, size_y)
    put_pair(jnp.where(okay, tap_matrix(ty_ref, source - c + HALF), 0.0), byh, byl)
    r, c = rows_cols((128, 512))
    part = c // A_ROWS
    source = c - part * A_ROWS - A_HALO
    middle = r - P_HALO
    okay = jnp.logical_and(inside(source, base_x, size_x), inside(middle, base_x, size_x))
    okay = jnp.logical_and(okay, part < 3)
    first = jnp.where(okay, tap_matrix(tx_ref, source - middle + HALF), 0.0)
    r, c = rows_cols((G_ROWS, 128))
    target = r - G_HALO
    middle = c - P_HALO
    second = jnp.where(inside(target, base_x, size_x), tap_matrix(tx_ref, target - middle + HALF), 0.0)
    r, c = rows_cols((G_ROWS, 512))
    put_left(exact_dot(second, first), c // A_ROWS, mx)
    r, c = rows_cols((G_ROWS, 384))
    part = c // P_ROWS
    source = c - part * P_ROWS - P_HALO
    target = r - G_HALO
    okay = jnp.logical_and(inside(source, base_x, size_x), inside(target, base_x, size_x))
    put_left(jnp.where(okay, tap_matrix(tx_ref, target - source + HALF), 0.0), part, px)
    r, c = rows_cols((ROWS, 384))
    part = c // G_ROWS
    source = c - part * G_ROWS - G_HALO
    okay = jnp.logical_and(inside(source, base_x, size_x), part < 3)
    put_left(jnp.where(okay, tap_matrix(tx_ref, source - r + HALF), 0.0), part, bx)


def project_body(spectra_ref, a_ref, m_ref, p_ref, left_ref, right_ref):
    step = 16
    for start in range(0, ROWS, step):
        acc = [jnp.zeros((step, COLS), f32) for _ in range(FLUOR)]
        for c in range(CHAN):
            seen = m_ref[c, start : start + step, :].astype(f32)
            for f in range(FLUOR):
                acc[f] = acc[f] + spectra_ref[c, f] * seen
        for f in range(FLUOR):
            p_ref[f, start : start + step, :] = acc[f]
    lane = lane_of((32, 128))
    lane8 = lane_of((8, 128))
    for f in range(FLUOR):
        for ref, a_from, p_from in ((left_ref, 0, 0), (right_ref, COLS - A_HALO, COLS - P_HALO)):
            top = roll(a_ref[f, :32, :], -a_from)
            low = roll(a_ref[f, 32:, :], A_HALO - a_from)
            side = roll(p_ref[f, :32, :], 2 * A_HALO - p_from)
            ref[f, :32, :] = jnp.where(lane < A_HALO, top, jnp.where(lane < 2 * A_HALO, low, side))
            rest = roll(p_ref[f, 32:40, :], -p_from)
            for k in range(1, 4):
                piece = roll(p_ref[f, 32 + 8 * k : 40 + 8 * k, :], 32 * k - p_from)
                rest = jnp.where(lane8 < 32 * k, rest, piece)
            ref[f, 32:, :] = rest


def widen_body(a_ref, p_ref, left_ref, right_ref, pyh, pyl, side_ref, w_ref, up_ref, down_ref, ps_ref):
    lane = lane_of((32, 128))
    lane8 = lane_of((8, 128))
    for f in range(FLUOR):
        left = left_ref[f, :32, :]
        right = right_ref[f, :32, :]
        side_ref[f, :32, :] = jnp.where(
            lane < A_HALO, left, jnp.where(lane < 2 * A_HALO, roll(right, A_HALO), 0.0)
        )
        side_ref[f, 32:, :] = jnp.where(
            lane < A_HALO, roll(left, -A_HALO), jnp.where(lane < 2 * A_HALO, right, 0.0)
        )
        ps_ref[:32, :] = jnp.where(
            lane < P_HALO, roll(left, -2 * A_HALO), jnp.where(lane < 2 * P_HALO, roll(right, P_HALO - 2 * A_HALO), 0.0)
        )
        left = left_ref[f, 32:, :]
        right = right_ref[f, 32:, :]
        for k in range(4):
            ps_ref[32 + 8 * k : 40 + 8 * k, :] = jnp.where(
                lane8 < P_HALO, roll(left, -32 * k), jnp.where(lane8 < 2 * P_HALO, roll(right, P_HALO - 32 * k), 0.0)
            )
        w = dot_right(jnp.concatenate([p_ref[f], ps_ref[...]], axis=1), pyh[...], pyl[...])
        w_ref[f] = w
        for ref, a_from, w_from in ((up_ref, 0, 0), (down_ref, ROWS - A_HALO, ROWS - P_HALO)):
            ref[f, :A_HALO, :] = a_ref[f, a_from : a_from + A_HALO, :]
            ref[f, A_HALO : 2 * A_HALO, :] = side_ref[f, a_from : a_from + A_HALO, :]
            w_side = roll(w[w_from : w_from + P_HALO, COLS:], 2 * A_HALO)
            ref[f, A_HALO : A_HALO + P_HALO, :] = jnp.where(
                lane < 2 * A_HALO, side_ref[f, a_from : a_from + P_HALO, :], w_side
            )
            ref[f, 2 * A_HALO :, :] = w[w_from : w_from + P_HALO, :COLS]


def gradient(f, abundance, myh, myl, mx, v_ref):
    u = dot_right(abundance, myh[...], myl[...])
    v_ref[f] = dot(mx[...], stacked(u, 512))


def mix(gram_ref, v_ref, d_ref, g_ref):
    step = 8
    for start in range(0, G_ROWS, step):
        part = [v_ref[f, start : start + step, :] for f in range(FLUOR)]
        for f in range(FLUOR):
            acc = -d_ref[f, start : start + step, :]
            for k in range(FLUOR):
                acc = acc + gram_ref[f, k] * part[k]
            g_ref[f, start : start + step, :] = acc


def sums(gram_ref, g_ref, byh, byl, bx, z_ref, sum_ref):
    for f in range(FLUOR):
        y = dot(bx[...], stacked(g_ref[f], 384))
        z_ref[f] = dot_right(y, byh[...], byl[...])
    grad = jnp.zeros((8, 128), f32)
    image = jnp.zeros((8, 128), f32)
    for start in range(0, ROWS, 8):
        part = [z_ref[f, start : start + 8, :] for f in range(FLUOR)]
        for f in range(FLUOR):
            acc = gram_ref[f, 0] * part[0]
            for k in range(1, FLUOR):
                acc = acc + gram_ref[f, k] * part[k]
            image = image + acc * part[f]
            g = g_ref[f, G_HALO + start : G_HALO + start + 8, :COLS]
            grad = grad + g * g
    grad = jnp.sum(grad, axis=0, keepdims=True)
    image = jnp.sum(image, axis=0, keepdims=True)
    lane = lane_of((1, 128))
    sum_ref[...] = jnp.where(lane < 64, grad + roll(grad, 64), image + roll(image, 64))


def step_length(total_ref):
    total = jnp.sum(total_ref[...], axis=0, keepdims=True)
    lane = lane_of((1, 128))
    grad = jnp.sum(jnp.where(lane < 64, total, 0.0), axis=1, keepdims=True)
    image = jnp.sum(jnp.where(lane < 64, 0.0, total), axis=1, keepdims=True)
    return grad / (image + tiny_floor)


def first_body(
    gram_ref, a_ref, side_ref, w_ref, above_ref, below_ref, myh, myl, mx, px,
    ext_ref, d_ref, g_ref, left_ref, right_ref, v_ref, we_ref,
):
    lane = lane_of((P_HALO, 128))
    for f in range(FLUOR):
        top = slice(0, A_HALO)
        mid = slice(A_HALO, A_HALO + ROWS)
        low = slice(A_HALO + ROWS, A_ROWS)
        ext_ref[f, top, :COLS] = above_ref[f, :A_HALO, :]
        ext_ref[f, mid, :COLS] = a_ref[f]
        ext_ref[f, low, :COLS] = below_ref[f, :A_HALO, :]
        ext_ref[f, top, COLS:] = above_ref[f, A_HALO : 2 * A_HALO, :]
        ext_ref[f, mid, COLS:] = side_ref[f]
        ext_ref[f, low, COLS:] = below_ref[f, A_HALO : 2 * A_HALO, :]
        for ref, at in ((above_ref, 0), (below_ref, P_HALO + ROWS)):
            we_ref[at : at + P_HALO, :COLS] = ref[f, 2 * A_HALO :, :]
            w_side = roll(ref[f, A_HALO : A_HALO + P_HALO, :], -2 * A_HALO)
            we_ref[at : at + P_HALO, COLS:] = jnp.where(lane < 2 * G_HALO, w_side, 0.0)
        we_ref[P_HALO : P_HALO + ROWS, :] = w_ref[f]
        d_ref[f] = dot(px[...], stacked(we_ref[...], 384))
        gradient(f, ext_ref[f], myh, myl, mx, v_ref)
    mix(gram_ref, v_ref, d_ref, g_ref)
    lane = lane_of((24, 128))
    for f in range(FLUOR):
        for ref, start in ((left_ref, G_HALO), (right_ref, COLS - G_HALO - 32)):
            out = roll(g_ref[f, :24, :COLS], -start)
            for k in range(1, 4):
                piece = roll(g_ref[f, 24 * k : 24 * k + 24, :COLS], 32 * k - start)
                out = jnp.where(lane < 32 * k, out, piece)
            ref[f] = out


def probe_body(gram_ref, g_ref, byh, byl, bx, sum_ref, z_ref):
    sums(gram_ref, g_ref, byh, byl, bx, z_ref, sum_ref)


def outer_body(g_ref, left_ref, right_ref, side_ref, send_ref):
    lane = lane_of((24, 128))
    for f in range(FLUOR):
        for k in range(4):
            own = roll(g_ref[f, 24 * k : 24 * k + 24, COLS:], 32)
            left = roll(left_ref[f], -32 * k)
            right = roll(right_ref[f], 64 - 32 * k)
            side_ref[f, 24 * k : 24 * k + 24, :] = jnp.where(
                lane < 32, left, jnp.where(lane < 64, own, jnp.where(lane < 96, right, 0.0))
            )
        send_ref[f, :32, :] = g_ref[f, 2 * G_HALO : 2 * G_HALO + 32, :COLS]
        send_ref[f, 32:, :] = side_ref[f, 2 * G_HALO : 2 * G_HALO + 32, :]


def second_body(
    gram_ref, total_ref, ext_ref, d_ref, g_ref, side_ref, above_ref, below_ref, myh, myl, mx, byh, byl, bx,
    a_out, g_out, sum_ref, v_ref, n_ref, z_ref, x_ref,
):
    t = step_length(total_ref)
    for f in range(FLUOR):
        for rows, main, side in (
            (slice(0, 32), above_ref[f, :32, :], above_ref[f, 32:, :]),
            (slice(32, 32 + G_ROWS), g_ref[f, :, :COLS], side_ref[f]),
            (slice(32 + G_ROWS, A_ROWS), below_ref[f, :32, :], below_ref[f, 32:, :]),
        ):
            x_ref[rows, :COLS] = jnp.maximum(ext_ref[f, rows, :COLS] - t * main, 0.0)
            x_ref[rows, COLS:] = jnp.maximum(ext_ref[f, rows, COLS:] - t * side, 0.0)
        a_out[f] = x_ref[A_HALO : A_HALO + ROWS, :COLS]
        gradient(f, x_ref[...], myh, myl, mx, v_ref)
    mix(gram_ref, v_ref, d_ref, n_ref)
    sums(gram_ref, n_ref, byh, byl, bx, z_ref, sum_ref)
    for f in range(FLUOR):
        g_out[f] = n_ref[f, G_HALO : G_HALO + ROWS, :COLS]


def last_body(total_ref, a_ref, g_ref, out_ref):
    t = step_length(total_ref)
    for f in range(FLUOR):
        out_ref[f] = jnp.maximum(a_ref[f] - t * g_ref[f], 0.0)


def both_ways(to_low, to_high, axes):
    count = 1
    for axis in axes:
        count *= lax.axis_size(axis)
    up = [(i, (i + 1) % count) for i in range(count)]
    down = [(i, (i - 1) % count) for i in range(count)]
    return lax.ppermute(to_high, axes, up), lax.ppermute(to_low, axes, down)


def spread(row, axes):
    names = axes if isinstance(axes, tuple) else (axes,)
    count = 1
    for axis in names:
        count *= lax.axis_size(axis)
    sent = jnp.broadcast_to(row.reshape(1, 1, 128), (count, 1, 128))
    return lax.all_to_all(sent, axes, 0, 0, tiled=True)


def local(sizes, abundance_start, measured, spectra, taps_x, taps_y):
    a0 = abundance_start[0]
    at = jnp.stack([lax.axis_index(GX), lax.axis_index(GY)]).astype(jnp.int32)
    wide = (256, 256)
    half = (256, 128)
    tile = (FLUOR, ROWS, COLS)

    p, left, right = kernel(
        project_body, "svv", [(tile, f32)] + [((FLUOR, 40, 128), f32)] * 2, 10**8
    )(spectra, a0, measured[0])
    from_left, from_right = both_ways(left, right, GY)
    gram = jnp.einsum("cf,cg->fg", spectra, spectra, precision=lax.Precision.HIGHEST)
    myh, myl, pyh, pyl, byh, byl, mx, px, bx = kernel(
        functools.partial(matrices_body, sizes),
        "sss",
        [(wide, bf16)] * 4 + [(half, bf16)] * 2
        + [((G_ROWS, 512), bf16), ((G_ROWS, 384), bf16), ((ROWS, 384), bf16)],
        10**9,
    )(at, taps_x, taps_y)
    side, w, up, down = kernel(
        widen_body,
        "vvvvvv",
        [(tile, f32), ((FLUOR, ROWS, 256), f32)] + [((FLUOR, 128, 128), f32)] * 2,
        10**8,
        [pltpu.VMEM((ROWS, 128), f32)],
    )(a0, p, from_left, from_right, pyh, pyl)
    from_above, from_below = both_ways(up, down, GX)
    ext, d, g, left, right = kernel(
        first_body,
        "s" + "v" * 9,
        [((FLUOR, A_ROWS, 256), f32)] + [((FLUOR, G_ROWS, 256), f32)] * 2 + [((FLUOR, 24, 128), f32)] * 2,
        10**9,
        [pltpu.VMEM((FLUOR, G_ROWS, 256), f32), pltpu.VMEM((P_ROWS, 256), f32)],
    )(gram, a0, side, w, from_above, from_below, myh, myl, mx, px)
    from_left, from_right = both_ways(left, right, GY)
    (partial,) = kernel(probe_body, "svvvv", [((1, 128), f32)], 10**9, [pltpu.VMEM(tile, f32)])(
        gram, g, byh, byl, bx
    )
    near = jnp.sum(spread(partial, NEAR), axis=0)
    g_side, send = kernel(
        outer_body, "vvv", [((FLUOR, G_ROWS, 128), f32), ((FLUOR, 64, 128), f32)], 10**8
    )(g, from_left, from_right)
    from_above, from_below = both_ways(send, send, GX)
    total = spread(near, FAR)
    a1, g1, partial = kernel(
        second_body,
        "s" + "v" * 13,
        [(tile, f32)] * 2 + [((1, 128), f32)],
        10**9,
        [
            pltpu.VMEM((FLUOR, G_ROWS, 256), f32),
            pltpu.VMEM((FLUOR, G_ROWS, 256), f32),
            pltpu.VMEM(tile, f32),
            pltpu.VMEM((A_ROWS, 256), f32),
        ],
    )(gram, total.reshape(-1, 128), ext, d, g, g_side, from_above, from_below, myh, myl, mx, byh, byl, bx)
    near = jnp.sum(spread(partial, NEAR), axis=0)
    total = spread(near, FAR)
    (out,) = kernel(last_body, "vvv", [(tile, f32)], 10**7)(total.reshape(-1, 128), a1, g1)
    return out[None]


def solution(mesh):
    count_x, count_y = mesh.shape["gx"], mesh.shape["gy"]
    parts = Mesh(
        mesh.devices.reshape(count_x // 4, 2, 2, 2, count_y // 2), ("y", "x_hi", "core", "x_lo", "z")
    )
    sizes = (count_x * ROWS, count_y * COLS)
    tiles = P(None, None, GX, GY)
    return jax.shard_map(
        functools.partial(local, sizes),
        mesh=parts,
        in_specs=(tiles, tiles, P(), P(), P()),
        out_specs=tiles,
        check_vma=False,
    )
```

time: 383 us -> 155 us (0.40)
  blocking collectives: 223 us -> 58.7 us
  waiting for transfers between devices: 48.9 us -> 20.1 us
  matrix products: 28.6 us -> 0.13 us
  starting transfers between devices: 64.1 us -> 36.4 us
  Pallas kernels: 0 us -> 22.1 us
  local copies, waits for them, and re-layouts: 10.1 us -> 15.2 us
    psum x2 -> x0, blocking collectives: 223 us -> none  [local(): grad_sq = lax.psum(grad_local, ('gx', 'gy'))]
    all_to_all x0 -> x4, blocking collectives: none -> 58.7 us  [spread(): return lax.all_to_all(sent, axes, 0, 0, tiled=True)]
    ppermute x24 -> x8, waiting for transfers between devices: 48.9 us -> 20.1 us  [both_ways(): return (lax.ppermute(to_high, axes, up), lax.ppermute(to_low, axes, down))]
    dot_general x22 -> x1, matrix products: 28.6 us -> 0.13 us  [local(): jnp.einsum('cf,cg->fg', spectra, spectra, precision=lax.Precision.HIGHEST)]
    ppermute x24 -> x8, starting transfers between devices: 64.1 us -> 36.4 us  [both_ways(): return (lax.ppermute(to_high, axes, up), lax.ppermute(to_low, axes, down))]
    pallas_call x0 -> x8, Pallas kernels: none -> 22.1 us  [the longest x1 6.63 us: local(): kernel(second_body, 's' + 'v' * 13, [(tile, f32)] * 2 + [((1, 128), f32)]...]
    unnamed x17 -> x53, local copies, waits for them, and re-layouts: 0.56 us -> 15.2 us
    slice x21 -> x0, local copies, waits for them, and re-layouts: 5.1 us -> none  [the longest x16 4.01 us: extended(): lax.slice_in_dim(block, block.shape[dim] - width, None, axis=dim)]
  transfers between devices with their start and end apart: 24 -> 8, of which waited for: 14 -> 4; matrix products, arithmetic and copies ran while one was open for 2% -> 1% of each run, Pallas kernels for 0% -> 4%
where the time goes in v1:
time: 155 us; the launch traced here: 154 us
  blocking collectives  58.7 us (38%)
  starting transfers between devices  36.4 us (23%)
  Pallas kernels  22.1 us (14%)
  waiting for transfers between devices  20.1 us (13%)
  local copies, waits for them, and re-layouts  15.2 us (10%)
    all_to_all x4, blocking collectives, spread(): return lax.all_to_all(sent, axes, 0, 0, tiled=True)  58.7 us
    ppermute x8, starting transfers between devices, both_ways(): return (lax.ppermute(to_high, axes, up), lax.ppermute(to_low, axes, down))  36.4 us
    ppermute x8, waiting for transfers between devices, both_ways(): return (lax.ppermute(to_high, axes, up), lax.ppermute(to_low, axes, down))  20.1 us
    unnamed x53, local copies, waits for them, and re-layouts  15.2 us
    pallas_call x1, Pallas kernels, local(): kernel(second_body, 's' + 'v' * 13, [(tile, f32)] * 2 + [((1, 128), f32)]...  6.63 us
    pallas_call x1, Pallas kernels, local(): kernel(functools.partial(matrices_body, sizes), 'sss', [(wide, bf16)] * 4...  4.98 us
    pallas_call x1, Pallas kernels, local(): kernel(first_body, 's' + 'v' * 9, [((FLUOR, A_ROWS, 256), f32)] + [((FLUO...  3.62 us
  transfers between devices with their start and end apart: 8, of which 4 were waited for; matrix products, arithmetic and copies ran while one was open for 1% of the time, Pallas kernels for 4%

profile of v1, /device:TPU:1, one launch (start us, length us, event | category | flops | bytes accessed | tf_op | source)
XLA Modules:
  0.0 153.6 jit_solution(13453223585757982286)
XLA Ops:
  0.0 0.8 copy.9.spectra_ref
  0.8 1.0 copy-done
  1.8 1.0 copy-done.6
  2.8 1.9 %shard_map.55 = (f32[12,64,128]{2,1,0:T(8,128)S(1)}, f32[12,40,128]{2,1,0:T(8,128)S(1)}, f32[12,40,128]{2,1,0:T(8,128)S(1)}) custom-call(f32[32,12]{1,0:T(8,128)S(1)} %copy.9.spectra_ref, f32[12,64,128]{2,1,0:T(8,128)S(1)} %bitcast.13, bf16[32,64,128]{2,1,0:T(8,128)(2,1)S(1)} %bitcast.16), custom_call_target="tpu_custom_call" | custom-call | flops 100000000 | bytes 1000000 | tf_op jit(solution)/shard_map/pallas_call | solution.py:378
  4.7 4.4 %collective-permute-start = (f32[12,40,128]{2,1,0:T(8,128)S(1)}, f32[12,40,128]{2,1,0:T(8,128)S(1)}, u32[]{:S(2)}, u32[]{:S(2)}) collective-permute-start(f32[12,40,128]{2,1,0:T(8,128)S(1)} %get-tuple-element.32), channel_id=1, source_target_pairs={{0,1},{1,2},{2,3},{3,4},{4,5},{5,6},{6,7},{7,8},{8,9},{9,10},{10,1... | collective-permute-start | bytes 737288 | tf_op jit(solution)/shard_map/ppermute | solution.py:359
  9.1 10.4 %collective-permute-start.1 = (f32[12,40,128]{2,1,0:T(8,128)S(1)}, f32[12,40,128]{2,1,0:T(8,128)S(1)}, u32[]{:S(2)}, u32[]{:S(2)}) collective-permute-start(f32[12,40,128]{2,1,0:T(8,128)S(1)} %get-tuple-element.33), channel_id=1, source_target_pairs={{0,31},{1,0},{2,1},{3,2},{4,3},{5,4},{6,5},{7,6},{8,7},{9,8},{10,9... | collective-permute-start | bytes 737288 | tf_op jit(solution)/shard_map/ppermute | solution.py:359
  19.6 0.1 pad_add_fusion.at_ref
  19.6 0.7 copy-done.23
  20.3 0.7 copy-done.24
  20.9 5.0 %shard_map.56 = (bf16[256,256]{1,0:T(8,128)(2,1)S(1)}, bf16[256,256]{1,0:T(8,128)(2,1)S(1)}, bf16[256,256]{1,0:T(8,128)(2,1)S(1)}, bf16[256,256]{1,0:T(8,128)(2,...) custom-call(s32[2]{0:T(128)S(1)} %pad_add_fusion.at_ref, ...), custom_call_target="tpu_custom_call" | custom-call | flops 1000000000 | bytes 10000000 | tf_op jit(solution)/shard_map/pallas_call | solution.py:383
  25.9 0.0 copy-start.11
  25.9 0.0 copy-start.13
  26.0 0.0 copy-start.15
  26.0 0.0 copy-start.17
  26.0 0.0 copy-start.19
  26.0 0.0 copy-start.21
  26.0 0.0 copy-start.25
  26.0 0.0 collective-permute-done.left_ref
  26.0 0.0 collective-permute-done.1.right_ref
  26.0 0.0 copy-done.1
  26.0 1.1 shard_map.57
  27.1 5.2 %collective-permute-start.2 = (f32[12,128,128]{2,1,0:T(8,128)S(1)}, f32[12,128,128]{2,1,0:T(8,128)S(1)}, u32[]{:S(2)}, u32[]{:S(2)}) collective-permute-start(f32[12,128,128]{2,1,0:T(8,128)S(1)} %get-tuple-element.38), channel_id=1, source_target_pairs={{0,32},{32,64},{64,96},{96,128},{128,160},{160,192},{192,224},{224... | collective-permute-start | bytes 2359304 | tf_op jit(solution)/shard_map/ppermute | solution.py:359
  32.3 1.9 %collective-permute-start.3 = (f32[12,128,128]{2,1,0:T(8,128)S(1)}, f32[12,128,128]{2,1,0:T(8,128)S(1)}, u32[]{:S(2)}, u32[]{:S(2)}) collective-permute-start(f32[12,128,128]{2,1,0:T(8,128)S(1)} %get-tuple-element.39), channel_id=1, source_target_pairs={{0,480},{32,0},{64,32},{96,64},{128,96},{160,128},{192,160},{224,1... | collective-permute-start | bytes 2359304 | tf_op jit(solution)/shard_map/ppermute | solution.py:359
  34.2 0.0 copy-done.25
  34.2 0.1 fusion.gram_ref
  34.4 10.1 %collective-permute-done.2.above_ref = f32[12,128,128]{2,1,0:T(8,128)S(1)} collective-permute-done((f32[12,128,128]{2,1,0:T(8,128)S(1)}, f32[12,128,128]{2,1,0:T(8,128)S(1)}, u32[]{:S(2)}, u32[]{:S(2)}) %collective-permute-start.2) | collective-permute-done | bytes 786464 | tf_op jit(solution)/shard_map/ppermute | solution.py:359
  44.5 7.2 %collective-permute-done.3.below_ref = f32[12,128,128]{2,1,0:T(8,128)S(1)} collective-permute-done((f32[12,128,128]{2,1,0:T(8,128)S(1)}, f32[12,128,128]{2,1,0:T(8,128)S(1)}, u32[]{:S(2)}, u32[]{:S(2)}) %collective-permute-start.3) | collective-permute-done | bytes 786464 | tf_op jit(solution)/shard_map/ppermute | solution.py:359
  51.6 3.6 %shard_map.58 = (f32[12,160,256]{2,1,0:T(8,128)S(1)}, f32[12,96,256]{2,1,0:T(8,128)S(1)}, f32[12,96,256]{2,1,0:T(8,128)S(1)}, f32[12,24,128]{2,1,0:T(8,128)S(1)}, f32[12,24,128]{2,1,0:T(8,128)S(1)}) custom-call(f32[12,12]{1,0:T(8,128)S(1)} %fusion.gram_ref, f32[12,64,128]{2,1,0:T(8,128)S(1)} %bitcast.15, f32[12,64,128]{2,1,0:T(8,128)S(1)} %get-tuple-element.36.side_ref, ...), custom_call_target="tpu_custom_call" | custom-call | flops 1000000000 | bytes 10000000 | tf_op jit(solution)/shard_map/pallas_call | solution.py:398
  55.2 0.0 copy-done.11
  55.3 0.0 copy-done.13
  55.3 0.0 copy-done.15
  55.3 1.9 %collective-permute-start.4 = (f32[12,24,128]{2,1,0:T(8,128)S(1)}, f32[12,24,128]{2,1,0:T(8,128)S(1)}, u32[]{:S(2)}, u32[]{:S(2)}) collective-permute-start(f32[12,24,128]{2,1,0:T(8,128)S(1)} %get-tuple-element.50), channel_id=1, source_target_pairs={{0,1},{1,2},{2,3},{3,4},{4,5},{5,6},{6,7},{7,8},{8,9},{9,10},{10,1... | collective-permute-start | bytes 442376 | tf_op jit(solution)/shard_map/ppermute | solution.py:359
  57.2 5.5 %collective-permute-start.5 = (f32[12,24,128]{2,1,0:T(8,128)S(1)}, f32[12,24,128]{2,1,0:T(8,128)S(1)}, u32[]{:S(2)}, u32[]{:S(2)}) collective-permute-start(f32[12,24,128]{2,1,0:T(8,128)S(1)} %get-tuple-element.51), channel_id=1, source_target_pairs={{0,31},{1,0},{2,1},{3,2},{4,3},{5,4},{6,5},{7,6},{8,7},{9,8},{10,9... | collective-permute-start | bytes 442376 | tf_op jit(solution)/shard_map/ppermute | solution.py:359
  62.7 1.1 collective-permute-done.4.left_ref
  63.7 1.8 %collective-permute-done.5.right_ref = f32[12,24,128]{2,1,0:T(8,128)S(1)} collective-permute-done((f32[12,24,128]{2,1,0:T(8,128)S(1)}, f32[12,24,128]{2,1,0:T(8,128)S(1)}, u32[]{:S(2)}, u32[]{:S(2)}) %collective-permute-start.5) | collective-permute-done | bytes 147488 | tf_op jit(solution)/shard_map/ppermute | solution.py:359
  65.5 1.2 shard_map.60
  66.7 1.9 %collective-permute-start.7 = (f32[12,64,128]{2,1,0:T(8,128)}, f32[12,64,128]{2,1,0:T(8,128)S(1)}, u32[]{:S(2)}, u32[]{:S(2)}) collective-permute-start(f32[12,64,128]{2,1,0:T(8,128)} %get-tuple-element.53), channel_id=1, source_target_pairs={{0,480},{32,0},{64,32},{96,64},{128,96},{160,128},{192,160},{224,1... | collective-permute-start | bytes 1179656 | tf_op jit(solution)/shard_map/ppermute | solution.py:359
  68.6 5.1 %collective-permute-start.6 = (f32[12,64,128]{2,1,0:T(8,128)}, f32[12,64,128]{2,1,0:T(8,128)}, u32[]{:S(2)}, u32[]{:S(2)}) collective-permute-start(f32[12,64,128]{2,1,0:T(8,128)} %get-tuple-element.53), channel_id=1, source_target_pairs={{0,32},{32,64},{64,96},{96,128},{128,160},{160,192},{192,224},{224... | collective-permute-start | bytes 1179656 | tf_op jit(solution)/shard_map/ppermute | solution.py:359
  73.7 0.0 copy-done.17
  73.7 0.0 copy-done.19
  73.8 0.0 copy-done.21
  73.8 1.9 %shard_map.59 = f32[1,128]{1,0:T(1,128)S(1)} custom-call(f32[12,12]{1,0:T(8,128)S(1)} %fusion.gram_ref, f32[12,96,256]{2,1,0:T(8,128)S(1)} %get-tuple-element.44.g_ref, bf16[256,128]{1,0:T(8,128)(2,1)S(1)} %get-tuple-element.45.byh, bf16[256,128]{1,0:T(8,128)(2,1)S(1)} %get-tuple-element.46.byl, bf16[64,384]{1,0:T(8,128)(2,1)S(1)} %get-tuple-element.47.bx), custom_call_target="tpu_custom_call" | custom-call | flops 1000000000 | bytes 10000000 | tf_op jit(solution)/shard_map/pallas_call | solution.py:406
  75.6 0.0 copy-done.4
  75.6 13.6 %all_to_all.20 = f32[32,1,128]{2,1,0:T(1,128)} all-to-all(f32[32,1,128]{2,1,0:T(1,128)S(1)} %broadcast_in_dim.28), channel_id=1, replica_groups=mesh['y'=4,'x_hi'=2,'core'=2,'x_lo'=2,'z'=16] {'y','x_hi','core','x_lo'}, dimensions={0} | all-to-all | bytes 32768 | tf_op jit(solution)/shard_map/all_to_all | solution.py:368
  89.3 0.7 reduce_sum.18
  90.0 19.1 %all_to_all.21 = f32[16,1,128]{2,1,0:T(1,128)S(1)} all-to-all(f32[16,1,128]{2,1,0:T(1,128)S(1)} %broadcast_in_dim.29), channel_id=1, replica_groups=mesh['y'=4,'x_hi'=2,'core'=2,'x_lo'=2,'z'=16] {'z'}, dimensions={0} | all-to-all | bytes 16384 | tf_op jit(solution)/shard_map/all_to_all | solution.py:368
  109.1 0.0 collective-permute-done.7.below_ref
  109.1 0.0 collective-permute-done.6.above_ref
  109.1 1.3 copy-done.3
  110.4 1.1 copy-done.5
  111.4 0.9 copy-done.12
  112.3 0.9 copy-done.14
  113.2 0.9 copy-done.16
  114.1 0.8 copy-done.18
  115.0 0.8 copy-done.20
  115.8 0.8 copy-done.22
  116.6 6.6 %shard_map.61 = (f32[12,64,128]{2,1,0:T(8,128)S(1)}, f32[12,64,128]{2,1,0:T(8,128)S(1)}, f32[1,128]{1,0:T(1,128)S(1)}) custom-call(f32[12,12]{1,0:T(8,128)S(1)} %fusion.gram_ref, f32[16,128]{1,0:T(8,128)S(1)} %bitcast.17, f32[12,160,256]{2,1,0:T(8,128)S(1)} %get-tuple-element.48.ext_ref, f32[12,96,256]{2,1,0:T(8,128)S(1)} %copy-done.3, ...), custom_call_target="tpu_custom_call" | custom-call | flops 1000000000 | bytes 10000000 | tf_op jit(solution)/shard_map/pallas_call | solution.py:415
  123.2 0.7 copy-done.7
  124.0 0.7 copy-done.9
  124.7 12.2 %all_to_all.22 = f32[32,1,128]{2,1,0:T(1,128)S(1)} all-to-all(f32[32,1,128]{2,1,0:T(1,128)S(1)} %broadcast_in_dim.31), channel_id=1, replica_groups=mesh['y'=4,'x_hi'=2,'core'=2,'x_lo'=2,'z'=16] {'y','x_hi','core','x_lo'}, dimensions={0} | all-to-all | bytes 32768 | tf_op jit(solution)/shard_map/all_to_all | solution.py:368
  137.0 13.8 %all_to_all.23 = f32[16,1,128]{2,1,0:T(1,128)S(1)} all-to-all(f32[16,1,128]{2,1,0:T(1,128)S(1)} %broadcast_in_dim.32), channel_id=1, replica_groups=mesh['y'=4,'x_hi'=2,'core'=2,'x_lo'=2,'z'=16] {'z'}, dimensions={0} | all-to-all | bytes 16384 | tf_op jit(solution)/shard_map/all_to_all | solution.py:368
  150.8 1.0 copy-done.8
  151.8 1.0 copy-done.10
  152.8 0.9 shard_map.62
  (25 shorter events, 0.1 us)
Async XLA Ops:
  0.8 1.0 copy-start
  1.8 1.0 copy-start.6
  4.7 21.3 %collective-permute-start = (f32[12,40,128]{2,1,0:T(8,128)S(1)}, f32[12,40,128]{2,1,0:T(8,128)S(1)}, u32[]{:S(2)}, u32[]{:S(2)}) collective-permute-start(f32[12,40,128]{2,1,0:T(8,128)S(1)} %get-tuple-element.32), channel_id=1, source_target_pairs={{0,1},{1,2},{2,3},{3,4},{4,5},{5,6},{6,7},{7,8},{8,9},{9,10},{10,1... | collective-permute-start | bytes 737288 | tf_op jit(solution)/shard_map/ppermute | solution.py:359
  9.1 16.9 %collective-permute-start.1 = (f32[12,40,128]{2,1,0:T(8,128)S(1)}, f32[12,40,128]{2,1,0:T(8,128)S(1)}, u32[]{:S(2)}, u32[]{:S(2)}) collective-permute-start(f32[12,40,128]{2,1,0:T(8,128)S(1)} %get-tuple-element.33), channel_id=1, source_target_pairs={{0,31},{1,0},{2,1},{3,2},{4,3},{5,4},{6,5},{7,6},{8,7},{9,8},{10,9... | collective-permute-start | bytes 737288 | tf_op jit(solution)/shard_map/ppermute | solution.py:359
  19.6 0.7 copy-start.23
  20.3 0.7 copy-start.24
  20.9 5.1 %copy-start.1 = (f32[1,12,64,128]{3,2,1,0:T(8,128)S(1)}, f32[1,12,64,128]{3,2,1,0:T(8,128)}, u32[]{:S(2)}) copy-start(f32[1,12,64,128]{3,2,1,0:T(8,128)} %param.5) | copy-start | bytes 1179652
  25.9 29.3 %copy-start.11 = (bf16[256,256]{1,0:T(8,128)(2,1)}, bf16[256,256]{1,0:T(8,128)(2,1)S(1)}, u32[]{:S(2)}) copy-start(bf16[256,256]{1,0:T(8,128)(2,1)S(1)} %get-tuple-element.40.myh) | copy-start | bytes 393220
  25.9 29.3 %copy-start.13 = (bf16[256,256]{1,0:T(8,128)(2,1)}, bf16[256,256]{1,0:T(8,128)(2,1)S(1)}, u32[]{:S(2)}) copy-start(bf16[256,256]{1,0:T(8,128)(2,1)S(1)} %get-tuple-element.41.myl) | copy-start | bytes 393220
  26.0 29.3 %copy-start.15 = (bf16[96,512]{1,0:T(8,128)(2,1)}, bf16[96,512]{1,0:T(8,128)(2,1)S(1)}, u32[]{:S(2)}) copy-start(bf16[96,512]{1,0:T(8,128)(2,1)S(1)} %get-tuple-element.42.mx) | copy-start | bytes 294916
  26.0 47.8 %copy-start.17 = (bf16[256,128]{1,0:T(8,128)(2,1)}, bf16[256,128]{1,0:T(8,128)(2,1)S(1)}, u32[]{:S(2)}) copy-start(bf16[256,128]{1,0:T(8,128)(2,1)S(1)} %get-tuple-element.45.byh) | copy-start | bytes 196612
  26.0 47.8 %copy-start.19 = (bf16[256,128]{1,0:T(8,128)(2,1)}, bf16[256,128]{1,0:T(8,128)(2,1)S(1)}, u32[]{:S(2)}) copy-start(bf16[256,128]{1,0:T(8,128)(2,1)S(1)} %get-tuple-element.46.byl) | copy-start | bytes 196612
  26.0 47.8 %copy-start.21 = (bf16[64,384]{1,0:T(8,128)(2,1)}, bf16[64,384]{1,0:T(8,128)(2,1)S(1)}, u32[]{:S(2)}) copy-start(bf16[64,384]{1,0:T(8,128)(2,1)S(1)} %get-tuple-element.47.bx) | copy-start | bytes 147460
  26.0 8.2 %copy-start.25 = (f32[32,12]{0,1:T(8,128)S(1)}, f32[32,12]{0,1:T(8,128)}, u32[]{:S(2)}) copy-start(f32[32,12]{0,1:T(8,128)} %param.7) | copy-start | bytes 4612
  27.1 17.4 %collective-permute-start.2 = (f32[12,128,128]{2,1,0:T(8,128)S(1)}, f32[12,128,128]{2,1,0:T(8,128)S(1)}, u32[]{:S(2)}, u32[]{:S(2)}) collective-permute-start(f32[12,128,128]{2,1,0:T(8,128)S(1)} %get-tuple-element.38), channel_id=1, source_target_pairs={{0,32},{32,64},{64,96},{96,128},{128,160},{160,192},{192,224},{224... | collective-permute-start | bytes 2359304 | tf_op jit(solution)/shard_map/ppermute | solution.py:359
  32.3 19.3 %collective-permute-start.3 = (f32[12,128,128]{2,1,0:T(8,128)S(1)}, f32[12,128,128]{2,1,0:T(8,128)S(1)}, u32[]{:S(2)}, u32[]{:S(2)}) collective-permute-start(f32[12,128,128]{2,1,0:T(8,128)S(1)} %get-tuple-element.39), channel_id=1, source_target_pairs={{0,480},{32,0},{64,32},{96,64},{128,96},{160,128},{192,160},{224,1... | collective-permute-start | bytes 2359304 | tf_op jit(solution)/shard_map/ppermute | solution.py:359
  55.3 20.4 %copy-start.2 = (f32[12,96,256]{2,1,0:T(8,128)}, f32[12,96,256]{2,1,0:T(8,128)S(1)}, u32[]{:S(2)}) copy-start(f32[12,96,256]{2,1,0:T(8,128)S(1)} %get-tuple-element.49.d_ref) | copy-start | bytes 3538948
  55.3 8.5 %collective-permute-start.4 = (f32[12,24,128]{2,1,0:T(8,128)S(1)}, f32[12,24,128]{2,1,0:T(8,128)S(1)}, u32[]{:S(2)}, u32[]{:S(2)}) collective-permute-start(f32[12,24,128]{2,1,0:T(8,128)S(1)} %get-tuple-element.50), channel_id=1, source_target_pairs={{0,1},{1,2},{2,3},{3,4},{4,5},{5,6},{6,7},{7,8},{8,9},{9,10},{10,1... | collective-permute-start | bytes 442376 | tf_op jit(solution)/shard_map/ppermute | solution.py:359
  57.2 8.3 %collective-permute-start.5 = (f32[12,24,128]{2,1,0:T(8,128)S(1)}, f32[12,24,128]{2,1,0:T(8,128)S(1)}, u32[]{:S(2)}, u32[]{:S(2)}) collective-permute-start(f32[12,24,128]{2,1,0:T(8,128)S(1)} %get-tuple-element.51), channel_id=1, source_target_pairs={{0,31},{1,0},{2,1},{3,2},{4,3},{5,4},{6,5},{7,6},{8,7},{9,8},{10,9... | collective-permute-start | bytes 442376 | tf_op jit(solution)/shard_map/ppermute | solution.py:359
  66.7 9.0 %copy-start.4 = (f32[12,96,128]{2,1,0:T(8,128)}, f32[12,96,128]{2,1,0:T(8,128)S(1)}, u32[]{:S(2)}) copy-start(f32[12,96,128]{2,1,0:T(8,128)S(1)} %get-tuple-element.52.side_ref) | copy-start | bytes 1769476
  66.7 42.4 %collective-permute-start.7 = (f32[12,64,128]{2,1,0:T(8,128)}, f32[12,64,128]{2,1,0:T(8,128)S(1)}, u32[]{:S(2)}, u32[]{:S(2)}) collective-permute-start(f32[12,64,128]{2,1,0:T(8,128)} %get-tuple-element.53), channel_id=1, source_target_pairs={{0,480},{32,0},{64,32},{96,64},{128,96},{160,128},{192,160},{224,1... | collective-permute-start | bytes 1179656 | tf_op jit(solution)/shard_map/ppermute | solution.py:359
  68.6 40.5 %collective-permute-start.6 = (f32[12,64,128]{2,1,0:T(8,128)}, f32[12,64,128]{2,1,0:T(8,128)}, u32[]{:S(2)}, u32[]{:S(2)}) collective-permute-start(f32[12,64,128]{2,1,0:T(8,128)} %get-tuple-element.53), channel_id=1, source_target_pairs={{0,32},{32,64},{64,96},{96,128},{128,160},{160,192},{192,224},{224... | collective-permute-start | bytes 1179656 | tf_op jit(solution)/shard_map/ppermute | solution.py:359
  109.1 1.3 copy-start.3
  110.4 1.1 copy-start.5
  111.4 0.9 copy-start.12
  112.3 0.9 copy-start.14
  113.2 0.9 copy-start.16
  114.1 0.8 copy-start.18
  115.0 0.8 copy-start.20
  115.8 0.8 copy-start.22
  123.2 0.8 copy-start.7
  124.0 0.7 copy-start.9
  150.8 1.0 copy-start.8
  151.8 1.0 copy-start.10

commit v2 on v1

v2 whole, which is shorter than its diff:
```python
import functools

import jax
import jax.numpy as jnp
from jax import lax
from jax.experimental import pallas as pl
from jax.experimental.pallas import tpu as pltpu
from jax.sharding import Mesh
from jax.sharding import PartitionSpec as P

TAPS = 33
ITERS = 2
FLUOR = 12
CHAN = 32
ROWS = 64
COLS = 128

HALF = TAPS // 2
A_HALO = 3 * HALF
P_HALO = 2 * HALF
G_HALO = HALF
A_ROWS = ROWS + 2 * A_HALO
P_ROWS = ROWS + 2 * P_HALO
G_ROWS = ROWS + 2 * G_HALO

GX = ("y", "x_hi", "core")
GY = ("x_lo", "z")
NEAR = ("y", "x_hi", "core", "x_lo")
FAR = "z"

tiny_floor = 1e-06
f32 = jnp.float32
bf16 = jnp.bfloat16


SPACES = {"s": pltpu.SMEM, "v": pltpu.VMEM, "a": pl.ANY}


def kernel(body, ins, outs, cost, scratch=()):
    return pl.pallas_call(
        body,
        in_specs=[pl.BlockSpec(memory_space=SPACES[kind]) for kind in ins],
        out_specs=[pl.BlockSpec(memory_space=pltpu.VMEM) for _ in outs],
        out_shape=[jax.ShapeDtypeStruct(shape, dtype) for shape, dtype in outs],
        scratch_shapes=list(scratch),
        compiler_params=pltpu.CompilerParams(vmem_limit_bytes=32 * 2**20),
        cost_estimate=pl.CostEstimate(flops=cost, bytes_accessed=cost // 100, transcendentals=0),
    )


def roll(x, by):
    by = by % 128
    return x if by == 0 else pltpu.roll(x, by, axis=x.ndim - 1)


def lane_of(shape):
    return lax.broadcasted_iota(jnp.int32, shape, len(shape) - 1)


def split(x):
    high = x.astype(bf16)
    return high, (x - high.astype(f32)).astype(bf16)


def dot(a, b):
    return jnp.dot(a, b, preferred_element_type=f32)


def dot_right(x, high, low):
    x_high, x_low = split(x)
    return dot(x_high, high) + dot(x_low, high) + dot(x_high, low)


def stacked(x, depth):
    high, low = split(x)
    parts = [high, low, high]
    spare = depth - 3 * x.shape[0]
    if spare:
        parts.append(jnp.zeros((spare, x.shape[1]), bf16))
    return jnp.concatenate(parts, axis=0)


def side_position(index, halo):
    left = index - COLS - halo
    right = index - halo
    position = jnp.where(index < COLS, index, jnp.where(index < COLS + halo, left, right))
    return jnp.where(index < COLS + 2 * halo, position, 1 << 20)


def tap_matrix(taps_ref, offset):
    out = jnp.zeros(offset.shape, f32)
    for t in range(TAPS):
        out = jnp.where(offset == t, taps_ref[t], out)
    return out


def inside(position, base, size):
    where = position + base
    return jnp.logical_and(where >= 0, where < size)


def exact_dot(a, b):
    return lax.dot_general(a, b, (((1,), (0,)), ((), ())), precision=lax.Precision.HIGHEST, preferred_element_type=f32)


def rows_cols(shape):
    return lax.broadcasted_iota(jnp.int32, shape, 0), lax.broadcasted_iota(jnp.int32, shape, 1)


def put_pair(x, high_ref, low_ref):
    high, low = split(x)
    high_ref[...] = high
    low_ref[...] = low


def put_left(x, part, ref):
    high, low = split(x)
    ref[...] = jnp.where(part < 2, high.astype(f32), low.astype(f32)).astype(bf16)


def matrices_body(sizes, at_ref, tx_ref, ty_ref, spectra_ref, gram_ref, myh, myl, pyh, pyl, byh, byl, mx, px, bx):
    spectra = spectra_ref[...]
    gram_ref[...] = lax.dot_general(
        spectra, spectra, (((1,), (1,)), ((), ())), precision=lax.Precision.HIGHEST, preferred_element_type=f32
    )
    size_x, size_y = sizes
    base_x = at_ref[0] * ROWS
    base_y = at_ref[1] * COLS
    r, c = rows_cols((256, 256))
    source = side_position(r, P_HALO)
    target = side_position(c, G_HALO)
    okay = jnp.logical_and(inside(source, base_y, size_y), inside(target, base_y, size_y))
    put_pair(jnp.where(okay, tap_matrix(ty_ref, target - source + HALF), 0.0), pyh, pyl)
    source = side_position(r, A_HALO)
    middle = c - P_HALO
    okay = jnp.logical_and(inside(source, base_y, size_y), inside(middle, base_y, size_y))
    first = jnp.where(okay, tap_matrix(ty_ref, source - middle + HALF), 0.0)
    middle = r - P_HALO
    second = jnp.where(inside(target, base_y, size_y), tap_matrix(ty_ref, target - middle + HALF), 0.0)
    put_pair(exact_dot(first, second), myh, myl)
    r, c = rows_cols((256, 128))
    source = side_position(r, G_HALO)
    okay = inside(source, base_y, size_y)
    put_pair(jnp.where(okay, tap_matrix(ty_ref, source - c + HALF), 0.0), byh, byl)
    r, c = rows_cols((128, 512))
    part = c // A_ROWS
    source = c - part * A_ROWS - A_HALO
    middle = r - P_HALO
    okay = jnp.logical_and(inside(source, base_x, size_x), inside(middle, base_x, size_x))
    okay = jnp.logical_and(okay, part < 3)
    first = jnp.where(okay, tap_matrix(tx_ref, source - middle + HALF), 0.0)
    r, c = rows_cols((G_ROWS, 128))
    target = r - G_HALO
    middle = c - P_HALO
    second = jnp.where(inside(target, base_x, size_x), tap_matrix(tx_ref, target - middle + HALF), 0.0)
    r, c = rows_cols((G_ROWS, 512))
    put_left(exact_dot(second, first), c // A_ROWS, mx)
    r, c = rows_cols((G_ROWS, 384))
    part = c // P_ROWS
    source = c - part * P_ROWS - P_HALO
    target = r - G_HALO
    okay = jnp.logical_and(inside(source, base_x, size_x), inside(target, base_x, size_x))
    put_left(jnp.where(okay, tap_matrix(tx_ref, target - source + HALF), 0.0), part, px)
    r, c = rows_cols((ROWS, 384))
    part = c // G_ROWS
    source = c - part * G_ROWS - G_HALO
    okay = jnp.logical_and(inside(source, base_x, size_x), part < 3)
    put_left(jnp.where(okay, tap_matrix(tx_ref, source - r + HALF), 0.0), part, bx)


def choose(odd, if_odd, if_even):
    return jnp.where(odd == 1, if_odd, if_even)


def project_body(at_ref, spectra_ref, a_any, m_any, p_ref, ya_ref, yb_ref, xa_ref, xb_ref, a_ref, m_ref, sems):
    step = 16
    copies = [
        pltpu.make_async_copy(m_any.at[:, pl.ds(k * step, step), :], m_ref.at[:, pl.ds(k * step, step), :], sems.at[k])
        for k in range(ROWS // step)
    ]
    for copy in copies:
        copy.start()
    copy_a = pltpu.make_async_copy(a_any, a_ref, sems.at[ROWS // step])
    copy_a.start()
    for k, copy in enumerate(copies):
        copy.wait()
        start = k * step
        acc = [jnp.zeros((step, COLS), f32) for _ in range(FLUOR)]
        for c in range(CHAN):
            seen = m_ref[c, start : start + step, :].astype(f32)
            for f in range(FLUOR):
                acc[f] = acc[f] + spectra_ref[f, c] * seen
        for f in range(FLUOR):
            p_ref[f, start : start + step, :] = acc[f]
    copy_a.wait()
    odd_x = at_ref[0] % 2
    odd_y = at_ref[1] % 2
    for ref, top in ((xa_ref, odd_x == 1), (xb_ref, odd_x == 0)):
        a_from = pl.multiple_of(jnp.where(top, 0, ROWS - A_HALO), 16)
        p_from = pl.multiple_of(jnp.where(top, 0, ROWS - P_HALO), 16)
        for f in range(FLUOR):
            ref[f, :A_HALO, :] = a_ref[f, pl.ds(a_from, A_HALO), :]
            ref[f, A_HALO:, :] = p_ref[f, pl.ds(p_from, P_HALO), :]
    lane = lane_of((32, 128))
    lane8 = lane_of((8, 128))
    for f in range(FLUOR):
        edges = []
        for a_from, p_from in ((0, 0), (COLS - A_HALO, COLS - P_HALO)):
            top = roll(a_ref[f, :32, :], -a_from)
            low = roll(a_ref[f, 32:, :], A_HALO - a_from)
            side = roll(p_ref[f, :32, :], 2 * A_HALO - p_from)
            main = jnp.where(lane < A_HALO, top, jnp.where(lane < 2 * A_HALO, low, side))
            rest = roll(p_ref[f, 32:40, :], -p_from)
            for k in range(1, 4):
                piece = roll(p_ref[f, 32 + 8 * k : 40 + 8 * k, :], 32 * k - p_from)
                rest = jnp.where(lane8 < 32 * k, rest, piece)
            edges.append((main, rest))
        (left, left_rest), (right, right_rest) = edges
        ya_ref[f, :32, :] = choose(odd_y, left, right)
        yb_ref[f, :32, :] = choose(odd_y, right, left)
        ya_ref[f, 32:, :] = choose(odd_y, left_rest, right_rest)
        yb_ref[f, 32:, :] = choose(odd_y, right_rest, left_rest)


def corner_body(at_ref, ya_ref, yb_ref, side_ref, ps_ref, xa_ref, xb_ref):
    odd_x = at_ref[0] % 2
    odd_y = at_ref[1] % 2
    lane = lane_of((32, 128))
    lane8 = lane_of((8, 128))
    for f in range(FLUOR):
        first = ya_ref[f, :32, :]
        second = yb_ref[f, :32, :]
        left = choose(odd_y, first, second)
        right = choose(odd_y, second, first)
        side_ref[f, :32, :] = jnp.where(lane < A_HALO, left, jnp.where(lane < 2 * A_HALO, roll(right, A_HALO), 0.0))
        side_ref[f, 32:, :] = jnp.where(lane < A_HALO, roll(left, -A_HALO), jnp.where(lane < 2 * A_HALO, right, 0.0))
        ps_ref[f, :32, :] = jnp.where(
            lane < P_HALO, roll(left, -2 * A_HALO), jnp.where(lane < 2 * P_HALO, roll(right, P_HALO - 2 * A_HALO), 0.0)
        )
        first = ya_ref[f, 32:, :]
        second = yb_ref[f, 32:, :]
        left = choose(odd_y, first, second)
        right = choose(odd_y, second, first)
        for k in range(4):
            ps_ref[f, 32 + 8 * k : 40 + 8 * k, :] = jnp.where(
                lane8 < P_HALO, roll(left, -32 * k), jnp.where(lane8 < 2 * P_HALO, roll(right, P_HALO - 32 * k), 0.0)
            )
    spare = 2 * A_HALO
    lane16 = lane_of((16, 128))
    for ref, top in ((xa_ref, odd_x == 1), (xb_ref, odd_x == 0)):
        a_from = pl.multiple_of(jnp.where(top, 0, ROWS - A_HALO), 16)
        p_from = pl.multiple_of(jnp.where(top, 0, ROWS - P_HALO), 16)
        for f in range(FLUOR):
            p_top = ps_ref[f, pl.ds(p_from, 32), :]
            a_side = side_ref[f, pl.ds(a_from, A_HALO), :]
            ref[f, :32, :] = jnp.where(lane < spare, a_side[:32], roll(p_top, spare))
            ref[f, 32:48, :] = jnp.where(lane16 < spare, a_side[32:], roll(p_top[:16], spare - P_HALO))
            ref[f, 48:, :] = jnp.where(lane8 < P_HALO, roll(p_top[16:24], -P_HALO), p_top[24:])


def gradient(f, abundance, myh, myl, mx, v_ref):
    u = dot_right(abundance, myh[...], myl[...])
    v_ref[f] = dot(mx[...], stacked(u, 512))


def mix(gram_ref, v_ref, d_ref, g_ref):
    step = 8
    for start in range(0, G_ROWS, step):
        part = [v_ref[f, start : start + step, :] for f in range(FLUOR)]
        for f in range(FLUOR):
            acc = -d_ref[f, start : start + step, :]
            for k in range(FLUOR):
                acc = acc + gram_ref[f, k] * part[k]
            g_ref[f, start : start + step, :] = acc


def sums(gram_ref, g_ref, byh, byl, bx, z_ref, sum_ref):
    for f in range(FLUOR):
        y = dot(bx[...], stacked(g_ref[f], 384))
        z_ref[f] = dot_right(y, byh[...], byl[...])
    grad = jnp.zeros((8, 128), f32)
    image = jnp.zeros((8, 128), f32)
    for start in range(0, ROWS, 8):
        part = [z_ref[f, start : start + 8, :] for f in range(FLUOR)]
        for f in range(FLUOR):
            acc = gram_ref[f, 0] * part[0]
            for k in range(1, FLUOR):
                acc = acc + gram_ref[f, k] * part[k]
            image = image + acc * part[f]
            g = g_ref[f, G_HALO + start : G_HALO + start + 8, :COLS]
            grad = grad + g * g
    grad = jnp.sum(grad, axis=0, keepdims=True)
    image = jnp.sum(image, axis=0, keepdims=True)
    lane = lane_of((1, 128))
    row = jnp.where(lane < 64, grad + roll(grad, 64), image + roll(image, 64))
    sum_ref[...] = jnp.broadcast_to(row, sum_ref.shape)


def step_length(total_ref):
    total = jnp.sum(total_ref[...], axis=0, keepdims=True)
    lane = lane_of((1, 128))
    grad = jnp.sum(jnp.where(lane < 64, total, 0.0), axis=1, keepdims=True)
    image = jnp.sum(jnp.where(lane < 64, 0.0, total), axis=1, keepdims=True)
    return grad / (image + tiny_floor)


def first_body(
    at_ref, gram_ref, a_ref, side_ref, p_ref, ps_ref, xa_ref, xb_ref, ca_ref, cb_ref, myh, myl, pyh, pyl, mx, px,
    ext_ref, d_ref, g_ref, ya_ref, yb_ref, v_ref, pe_ref,
):
    odd_x = at_ref[0] % 2
    odd_y = at_ref[1] % 2
    lane = lane_of((32, 128))
    lane16 = lane_of((16, 128))
    lane8 = lane_of((8, 128))
    spare = 2 * A_HALO
    sources = ((xa_ref, ca_ref, odd_x == 1), (xb_ref, cb_ref, odd_x == 0))
    for f in range(FLUOR):
        mid = slice(A_HALO, A_HALO + ROWS)
        ext_ref[f, mid, :COLS] = a_ref[f]
        ext_ref[f, mid, COLS:] = side_ref[f]
        mid = slice(P_HALO, P_HALO + ROWS)
        pe_ref[mid, :COLS] = p_ref[f]
        pe_ref[mid, COLS:] = ps_ref[f]
        for main, corner, above in sources:
            a_at = pl.multiple_of(jnp.where(above, 0, A_HALO + ROWS), 16)
            p_at = jnp.where(above, 0, P_HALO + ROWS)
            ext_ref[f, pl.ds(a_at, A_HALO), :COLS] = main[f, :A_HALO, :]
            ext_ref[f, pl.ds(a_at, A_HALO), COLS:] = corner[f, :A_HALO, :]
            pe_ref[pl.ds(pl.multiple_of(p_at, 16), P_HALO), :COLS] = main[f, A_HALO:, :]
            left = roll(corner[f, :32, :], -spare)
            right = roll(corner[f, 32:48, :], P_HALO - spare)
            pe_ref[pl.ds(pl.multiple_of(p_at, 16), 16), COLS:] = jnp.where(
                lane16 < P_HALO, left[:16], jnp.where(lane16 < 2 * P_HALO, right, 0.0)
            )
            last = corner[f, 48:, :]
            pe_ref[pl.ds(pl.multiple_of(p_at + 16, 16), 8), COLS:] = jnp.where(
                lane8 < P_HALO, left[16:24], jnp.where(lane8 < 2 * P_HALO, roll(last, P_HALO), 0.0)
            )
            pe_ref[pl.ds(pl.multiple_of(p_at + 24, 8), 8), COLS:] = jnp.where(
                lane8 < P_HALO, left[24:], jnp.where(lane8 < 2 * P_HALO, last, 0.0)
            )
        d_ref[f] = dot(px[...], stacked(dot_right(pe_ref[...], pyh[...], pyl[...]), 384))
        gradient(f, ext_ref[f], myh, myl, mx, v_ref)
    mix(gram_ref, v_ref, d_ref, g_ref)
    lane = lane_of((24, 128))
    for f in range(FLUOR):
        edges = []
        for start in (G_HALO, COLS - G_HALO - 32):
            out = roll(g_ref[f, :24, :COLS], -start)
            for k in range(1, 4):
                piece = roll(g_ref[f, 24 * k : 24 * k + 24, :COLS], 32 * k - start)
                out = jnp.where(lane < 32 * k, out, piece)
            edges.append(out)
        ya_ref[f] = choose(odd_y, edges[0], edges[1])
        yb_ref[f] = choose(odd_y, edges[1], edges[0])


def probe_body(gram_ref, g_ref, byh, byl, bx, sum_ref, z_ref):
    sums(gram_ref, g_ref, byh, byl, bx, z_ref, sum_ref)


def relay_body(near_ref, out_ref):
    out_ref[...] = jnp.broadcast_to(jnp.sum(near_ref[...], axis=0, keepdims=True), out_ref.shape)


def outer_body(at_ref, g_ref, ya_ref, yb_ref, side_ref, send_ref):
    odd_y = at_ref[1] % 2
    lane = lane_of((24, 128))
    for f in range(FLUOR):
        left = choose(odd_y, ya_ref[f], yb_ref[f])
        right = choose(odd_y, yb_ref[f], ya_ref[f])
        for k in range(4):
            own = roll(g_ref[f, 24 * k : 24 * k + 24, COLS:], 32)
            side_ref[f, 24 * k : 24 * k + 24, :] = jnp.where(
                lane < 32,
                roll(left, -32 * k),
                jnp.where(lane < 64, own, jnp.where(lane < 96, roll(right, 64 - 32 * k), 0.0)),
            )
        send_ref[f, :32, :] = g_ref[f, 2 * G_HALO : 2 * G_HALO + 32, :COLS]
        send_ref[f, 32:, :] = side_ref[f, 2 * G_HALO : 2 * G_HALO + 32, :]


def second_body(
    at_ref, gram_ref, total_ref, ext_ref, d_ref, g_ref, side_ref, xa_ref, xb_ref, myh, myl, mx, byh, byl, bx,
    a_out, g_out, sum_ref, v_ref, n_ref, z_ref, x_ref,
):
    odd_x = at_ref[0] % 2
    t = step_length(total_ref)
    for f in range(FLUOR):
        mid = slice(32, 32 + G_ROWS)
        x_ref[mid, :COLS] = jnp.maximum(ext_ref[f, mid, :COLS] - t * g_ref[f, :, :COLS], 0.0)
        x_ref[mid, COLS:] = jnp.maximum(ext_ref[f, mid, COLS:] - t * side_ref[f], 0.0)
        for ref, above in ((xa_ref, odd_x == 1), (xb_ref, odd_x == 0)):
            rows = pl.ds(pl.multiple_of(jnp.where(above, 0, 32 + G_ROWS), 16), 32)
            x_ref[rows, :COLS] = jnp.maximum(ext_ref[f, rows, :COLS] - t * ref[f, :32, :], 0.0)
            x_ref[rows, COLS:] = jnp.maximum(ext_ref[f, rows, COLS:] - t * ref[f, 32:, :], 0.0)
        a_out[f] = x_ref[A_HALO : A_HALO + ROWS, :COLS]
        gradient(f, x_ref[...], myh, myl, mx, v_ref)
    mix(gram_ref, v_ref, d_ref, n_ref)
    sums(gram_ref, n_ref, byh, byl, bx, z_ref, sum_ref)
    for f in range(FLUOR):
        g_out[f] = n_ref[f, G_HALO : G_HALO + ROWS, :COLS]


def last_body(total_ref, a_ref, g_ref, out_ref):
    t = step_length(total_ref)
    for f in range(FLUOR):
        out_ref[f] = jnp.maximum(a_ref[f] - t * g_ref[f], 0.0)


def length(axes):
    count = 1
    for axis in axes:
        count *= lax.axis_size(axis)
    return count


def trade(first, second, axes):
    count = length(axes)
    pairs_first = [(i, i ^ 1) for i in range(count)]
    pairs_second = [(i, (i + (1 if i % 2 else -1)) % count) for i in range(count)]
    got_second = lax.ppermute(second, axes, pairs_second)
    return lax.ppermute(first, axes, pairs_first), got_second


def spread(rows, axes):
    got = lax.all_to_all(rows.reshape(rows.shape[0], 1, 128), axes, 0, 0, tiled=True)
    return got.reshape(rows.shape[0], 128)


def local(sizes, abundance_start, measured, spectra, taps_x, taps_y):
    a0 = abundance_start[0]
    at = jnp.stack([lax.axis_index(GX), lax.axis_index(GY)]).astype(jnp.int32)
    wide = (256, 256)
    half = (256, 128)
    tile = (FLUOR, ROWS, COLS)
    near_count, far_count = length(NEAR), length((FAR,))

    p, ya, yb, xa, xb = kernel(
        project_body,
        "ssaa",
        [(tile, f32)] + [((FLUOR, 40, 128), f32)] * 2 + [((FLUOR, A_HALO + P_HALO, 128), f32)] * 2,
        10**8,
        [pltpu.VMEM(tile, f32), pltpu.VMEM((CHAN, ROWS, COLS), bf16), pltpu.SemaphoreType.DMA((5,))],
    )(at, spectra.T, a0, measured[0])
    xa, xb = trade(xa, xb, GX)
    ya, yb = trade(ya, yb, GY)
    gram, myh, myl, pyh, pyl, byh, byl, mx, px, bx = kernel(
        functools.partial(matrices_body, sizes),
        "sssv",
        [((FLUOR, FLUOR), f32)] + [(wide, bf16)] * 4 + [(half, bf16)] * 2
        + [((G_ROWS, 512), bf16), ((G_ROWS, 384), bf16), ((ROWS, 384), bf16)],
        10**9,
    )(at, taps_x, taps_y, spectra.T)
    side, ps, ca, cb = kernel(
        corner_body, "svv", [(tile, f32)] * 2 + [((FLUOR, 56, 128), f32)] * 2, 10**8
    )(at, ya, yb)
    ca, cb = trade(ca, cb, GX)
    ext, d, g, ya, yb = kernel(
        first_body,
        "ss" + "v" * 14,
        [((FLUOR, A_ROWS, 256), f32)] + [((FLUOR, G_ROWS, 256), f32)] * 2 + [((FLUOR, 24, 128), f32)] * 2,
        10**9,
        [pltpu.VMEM((FLUOR, G_ROWS, 256), f32), pltpu.VMEM((P_ROWS, 256), f32)],
    )(at, gram, a0, side, p, ps, xa, xb, ca, cb, myh, myl, pyh, pyl, mx, px)
    ya, yb = trade(ya, yb, GY)
    (partial,) = kernel(probe_body, "svvvv", [((near_count, 128), f32)], 10**9, [pltpu.VMEM(tile, f32)])(
        gram, g, byh, byl, bx
    )
    g_side, send = kernel(
        outer_body, "svvv", [((FLUOR, G_ROWS, 128), f32), ((FLUOR, 64, 128), f32)], 10**8
    )(at, g, ya, yb)
    xa, xb = trade(send, send, GX)
    relay = kernel(relay_body, "v", [((far_count, 128), f32)], 10**6)
    (near,) = relay(spread(partial, NEAR))
    total = spread(near, FAR)
    a1, g1, partial = kernel(
        second_body,
        "ss" + "v" * 13,
        [(tile, f32)] * 2 + [((near_count, 128), f32)],
        10**9,
        [
            pltpu.VMEM((FLUOR, G_ROWS, 256), f32),
            pltpu.VMEM((FLUOR, G_ROWS, 256), f32),
            pltpu.VMEM(tile, f32),
            pltpu.VMEM((A_ROWS, 256), f32),
        ],
    )(at, gram, total, ext, d, g, g_side, xa, xb, myh, myl, mx, byh, byl, bx)
    (near,) = relay(spread(partial, NEAR))
    total = spread(near, FAR)
    (out,) = kernel(last_body, "vvv", [(tile, f32)], 10**7)(total, a1, g1)
    return out[None]


def solution(mesh):
    count_x, count_y = mesh.shape["gx"], mesh.shape["gy"]
    parts = Mesh(
        mesh.devices.reshape(count_x // 4, 2, 2, 2, count_y // 2), ("y", "x_hi", "core", "x_lo", "z")
    )
    sizes = (count_x * ROWS, count_y * COLS)
    tiles = P(None, None, GX, GY)
    return jax.shard_map(
        functools.partial(local, sizes),
        mesh=parts,
        in_specs=(tiles, tiles, P(), P(), P()),
        out_specs=tiles,
        check_vma=False,
    )
```

time: 155 us -> 141 us (0.910)
  local copies, waits for them, and re-layouts: 15.2 us -> 2.75 us
  waiting for transfers between devices: 20.1 us -> 11.8 us
  starting transfers between devices: 36.4 us -> 44.3 us
  Pallas kernels: 22.1 us -> 26.2 us
  blocking collectives: 58.7 us -> 54.9 us
    unnamed x53 -> x14, local copies, waits for them, and re-layouts: 15.2 us -> 2.75 us
    ppermute x8 -> x10, waiting for transfers between devices: 20.1 us -> 11.8 us  [the longest x5 10.9 us: trade(): got_second = lax.ppermute(second, axes, pairs_second)]
    ppermute x8 -> x10, starting transfers between devices: 36.4 us -> 44.3 us  [the longest x5 23.5 us: trade(): got_second = lax.ppermute(second, axes, pairs_second)]
    pallas_call x8 -> x10, Pallas kernels: 22.1 us -> 26.2 us  [the longest x1 7.17 us: local(): kernel(first_body, 'ss' + 'v' * 14, [((FLUOR, A_ROWS, 256), f32)] + [((FL...]
    all_to_all x4, blocking collectives: 58.7 us -> 54.9 us  [spread(): lax.all_to_all(rows.reshape(rows.shape[0], 1, 128), axes, 0, 0, tiled=True)]
  transfers between devices with their start and end apart: 8 -> 10, of which waited for: 4 -> 3; matrix products, arithmetic and copies ran while one was open for 1% -> 0% of each run, Pallas kernels for 4% -> 6%
where the time goes in v2:
time: 141 us; the launch traced here: 140 us
  blocking collectives  54.9 us (39%)
  starting transfers between devices  44.3 us (31%)
  Pallas kernels  26.2 us (19%)
  waiting for transfers between devices  11.8 us (8%)
  local copies, waits for them, and re-layouts  2.75 us (2%)
    all_to_all x4, blocking collectives, spread(): lax.all_to_all(rows.reshape(rows.shape[0], 1, 128), axes, 0, 0, tiled=True)  54.9 us
    ppermute x5, starting transfers between devices, trade(): got_second = lax.ppermute(second, axes, pairs_second)  23.5 us
    ppermute x5, starting transfers between devices, trade(): return (lax.ppermute(first, axes, pairs_first), got_second)  20.7 us
    ppermute x5, waiting for transfers between devices, trade(): got_second = lax.ppermute(second, axes, pairs_second)  10.9 us
    pallas_call x1, Pallas kernels, local(): kernel(first_body, 'ss' + 'v' * 14, [((FLUOR, A_ROWS, 256), f32)] + [((FL...  7.17 us
    pallas_call x1, Pallas kernels, local(): kernel(second_body, 'ss' + 'v' * 13, [(tile, f32)] * 2 + [((near_count, 1...  6.53 us
    pallas_call x1, Pallas kernels, local(): kernel(functools.partial(matrices_body, sizes), 'sssv', [((FLUOR, FLUOR),...  5.04 us
  transfers between devices with their start and end apart: 10, of which 3 were waited for; matrix products, arithmetic and copies ran while one was open for 0% of the time, Pallas kernels for 6%

profile of v2, /device:TPU:1, one launch (start us, length us, event | category | flops | bytes accessed | tf_op | source)
XLA Modules:
  0.0 140.2 jit_solution(10678466752893737699)
XLA Ops:
  0.0 0.0 copy-start.4
  0.0 0.0 copy-start.6
  0.0 0.0 copy-start.5
  0.0 0.1 pad_add_fusion.at_ref
  0.1 0.0 copy-start
  0.1 1.0 copy-done
  1.1 0.0 copy-start.2
  1.1 1.0 copy-done.2
  2.1 0.0 copy-start.3
  2.1 0.7 copy-done.3
  2.8 2.7 %shard_map.56 = (f32[12,64,128]{2,1,0:T(8,128)S(1)}, f32[12,40,128]{2,1,0:T(8,128)S(1)}, f32[12,40,128]{2,1,0:T(8,128)S(1)}, f32[12,80,128]{2,1,0:T(8,128)S(1)}, f32[12,80,128]{2,1,0:T(8,128)S(1)}) custom-call(s32[2]{0:T(128)S(1)} %pad_add_fusion.at_ref, f32[12,32]{1,0:T(8,128)S(1)} %bitcast.33, f32[12,64,128]{2,1,0:T(8,128)S(1)} %bitcast.22, ...), custom_call_target="tpu_custom_call" | custom-call | flops 100000000 | bytes 1000000 | tf_op jit(solution)/shard_map/pallas_call | solution.py:440
  5.5 4.4 %collective-permute-start = (f32[12,40,128]{2,1,0:T(8,128)S(1)}, f32[12,40,128]{2,1,0:T(8,128)S(1)}, u32[]{:S(2)}, u32[]{:S(2)}) collective-permute-start(f32[12,40,128]{2,1,0:T(8,128)S(1)} %get-tuple-element.35), channel_id=1, source_target_pairs={{0,1},{1,0},{2,3},{3,2},{4,5},{5,4},{6,7},{7,6},{8,9},{9,8},{10,11... | collective-permute-start | bytes 737288 | tf_op jit(solution)/shard_map/ppermute | solution.py:424
  9.9 11.1 %collective-permute-start.1 = (f32[12,40,128]{2,1,0:T(8,128)S(1)}, f32[12,40,128]{2,1,0:T(8,128)S(1)}, u32[]{:S(2)}, u32[]{:S(2)}) collective-permute-start(f32[12,40,128]{2,1,0:T(8,128)S(1)} %get-tuple-element.36), channel_id=1, source_target_pairs={{0,31},{1,2},{2,1},{3,4},{4,3},{5,6},{6,5},{7,8},{8,7},{9,10},{10,... | collective-permute-start | bytes 737288 | tf_op jit(solution)/shard_map/ppermute | solution.py:423
  21.0 3.1 %collective-permute-start.2 = (f32[12,80,128]{2,1,0:T(8,128)S(1)}, f32[12,80,128]{2,1,0:T(8,128)S(1)}, u32[]{:S(2)}, u32[]{:S(2)}) collective-permute-start(f32[12,80,128]{2,1,0:T(8,128)S(1)} %get-tuple-element.40), channel_id=1, source_target_pairs={{0,32},{32,0},{64,96},{96,64},{128,160},{160,128},{192,224},{224,1... | collective-permute-start | bytes 1474568 | tf_op jit(solution)/shard_map/ppermute | solution.py:424
  24.2 4.3 %collective-permute-start.3 = (f32[12,80,128]{2,1,0:T(8,128)S(1)}, f32[12,80,128]{2,1,0:T(8,128)S(1)}, u32[]{:S(2)}, u32[]{:S(2)}) collective-permute-start(f32[12,80,128]{2,1,0:T(8,128)S(1)} %get-tuple-element.41), channel_id=1, source_target_pairs={{0,480},{32,64},{64,32},{96,128},{128,96},{160,192},{192,160},{224... | collective-permute-start | bytes 1474568 | tf_op jit(solution)/shard_map/ppermute | solution.py:423
  28.5 0.0 collective-permute-done.ya_ref
  28.5 0.0 collective-permute-done.1.yb_ref
  28.5 1.1 shard_map.57
  29.5 4.9 %collective-permute-start.4 = (f32[12,56,128]{2,1,0:T(8,128)S(1)}, f32[12,56,128]{2,1,0:T(8,128)S(1)}, u32[]{:S(2)}, u32[]{:S(2)}) collective-permute-start(f32[12,56,128]{2,1,0:T(8,128)S(1)} %get-tuple-element.42), channel_id=1, source_target_pairs={{0,32},{32,0},{64,96},{96,64},{128,160},{160,128},{192,224},{224,1... | collective-permute-start | bytes 1032200 | tf_op jit(solution)/shard_map/ppermute | solution.py:424
  34.4 0.0 copy-start.1
  34.4 2.2 %collective-permute-start.5 = (f32[12,56,128]{2,1,0:T(8,128)S(1)}, f32[12,56,128]{2,1,0:T(8,128)S(1)}, u32[]{:S(2)}, u32[]{:S(2)}) collective-permute-start(f32[12,56,128]{2,1,0:T(8,128)S(1)} %get-tuple-element.43), channel_id=1, source_target_pairs={{0,480},{32,64},{64,32},{96,128},{128,96},{160,192},{192,160},{224... | collective-permute-start | bytes 1032200 | tf_op jit(solution)/shard_map/ppermute | solution.py:423
  36.7 0.0 copy-done.4
  36.7 0.0 copy-done.6
  36.7 0.0 copy-done.5
  36.7 5.0 %shard_map.55 = (f32[12,12]{1,0:T(8,128)S(1)}, bf16[256,256]{1,0:T(8,128)(2,1)S(1)}, bf16[256,256]{1,0:T(8,128)(2,1)S(1)}, bf16[256,256]{1,0:T(8,128)(2,1)S(1)},...) custom-call(s32[2]{0:T(128)S(1)} %pad_add_fusion.at_ref, ...), custom_call_target="tpu_custom_call" | custom-call | flops 1000000000 | bytes 10000000 | tf_op jit(solution)/shard_map/pallas_call | solution.py:449
  41.7 0.0 collective-permute-done.2.xa_ref
  41.7 0.0 collective-permute-done.3.xb_ref
  41.8 0.0 collective-permute-done.4.ca_ref
  41.8 6.9 %collective-permute-done.5.cb_ref = f32[12,56,128]{2,1,0:T(8,128)S(1)} collective-permute-done((f32[12,56,128]{2,1,0:T(8,128)S(1)}, f32[12,56,128]{2,1,0:T(8,128)S(1)}, u32[]{:S(2)}, u32[]{:S(2)}) %collective-permute-start.5) | collective-permute-done | bytes 344096 | tf_op jit(solution)/shard_map/ppermute | solution.py:423
  48.7 0.0 copy-done.1
  48.7 7.2 %shard_map.58 = (f32[12,160,256]{2,1,0:T(8,128)S(1)}, f32[12,96,256]{2,1,0:T(8,128)S(1)}, f32[12,96,256]{2,1,0:T(8,128)S(1)}, f32[12,24,128]{2,1,0:T(8,128)S(1)}, f32[12,24,128]{2,1,0:T(8,128)S(1)}) custom-call(s32[2]{0:T(128)S(1)} %pad_add_fusion.at_ref, f32[12,12]{1,0:T(8,128)S(1)} %get-tuple-element.34.gram_ref, f32[12,64,128]{2,1,0:T(8,128)S(1)} %bitcast.23, ...), custom_call_target="tpu_custom_call" | custom-call | flops 1000000000 | bytes 10000000 | tf_op jit(solution)/shard_map/pallas_call | solution.py:460
  55.8 1.9 %collective-permute-start.6 = (f32[12,24,128]{2,1,0:T(8,128)S(1)}, f32[12,24,128]{2,1,0:T(8,128)S(1)}, u32[]{:S(2)}, u32[]{:S(2)}) collective-permute-start(f32[12,24,128]{2,1,0:T(8,128)S(1)} %get-tuple-element.56), channel_id=1, source_target_pairs={{0,1},{1,0},{2,3},{3,2},{4,5},{5,4},{6,7},{7,6},{8,9},{9,8},{10,11... | collective-permute-start | bytes 442376 | tf_op jit(solution)/shard_map/ppermute | solution.py:424
  57.8 3.1 %collective-permute-start.7 = (f32[12,24,128]{2,1,0:T(8,128)S(1)}, f32[12,24,128]{2,1,0:T(8,128)S(1)}, u32[]{:S(2)}, u32[]{:S(2)}) collective-permute-start(f32[12,24,128]{2,1,0:T(8,128)S(1)} %get-tuple-element.57), channel_id=1, source_target_pairs={{0,31},{1,2},{2,1},{3,4},{4,3},{5,6},{6,5},{7,8},{8,7},{9,10},{10,... | collective-permute-start | bytes 442376 | tf_op jit(solution)/shard_map/ppermute | solution.py:423
  60.9 0.8 collective-permute-done.6.ya_ref
  61.7 4.0 %collective-permute-done.7.yb_ref = f32[12,24,128]{2,1,0:T(8,128)S(1)} collective-permute-done((f32[12,24,128]{2,1,0:T(8,128)S(1)}, f32[12,24,128]{2,1,0:T(8,128)S(1)}, u32[]{:S(2)}, u32[]{:S(2)}) %collective-permute-start.7) | collective-permute-done | bytes 147488 | tf_op jit(solution)/shard_map/ppermute | solution.py:423
  65.8 1.0 shard_map.61
  66.8 2.8 %collective-permute-start.9 = (f32[12,64,128]{2,1,0:T(8,128)S(1)}, f32[12,64,128]{2,1,0:T(8,128)S(1)}, u32[]{:S(2)}, u32[]{:S(2)}) collective-permute-start(f32[12,64,128]{2,1,0:T(8,128)S(1)} %get-tuple-element.59), channel_id=1, source_target_pairs={{0,480},{32,64},{64,32},{96,128},{128,96},{160,192},{192,160},{224... | collective-permute-start | bytes 1179656 | tf_op jit(solution)/shard_map/ppermute | solution.py:423
  69.5 6.4 %collective-permute-start.8 = (f32[12,64,128]{2,1,0:T(8,128)S(1)}, f32[12,64,128]{2,1,0:T(8,128)S(1)}, u32[]{:S(2)}, u32[]{:S(2)}) collective-permute-start(f32[12,64,128]{2,1,0:T(8,128)S(1)} %get-tuple-element.59), channel_id=1, source_target_pairs={{0,32},{32,0},{64,96},{96,64},{128,160},{160,128},{192,224},{224,1... | collective-permute-start | bytes 1179656 | tf_op jit(solution)/shard_map/ppermute | solution.py:424
  76.0 1.9 %shard_map.59 = f32[32,128]{1,0:T(8,128)S(1)} custom-call(f32[12,12]{1,0:T(8,128)S(1)} %get-tuple-element.34.gram_ref, f32[12,96,256]{2,1,0:T(8,128)S(1)} %get-tuple-element.50.g_ref, bf16[256,128]{1,0:T(8,128)(2,1)S(1)} %get-tuple-element.51.byh, bf16[256,128]{1,0:T(8,128)(2,1)S(1)} %get-tuple-element.52.byl, bf16[64,384]{1,0:T(8,128)(2,1)S(1)} %get-tuple-element.53.bx), custom_call_target="tpu_custom_call" | custom-call | flops 1000000000 | bytes 10000000 | tf_op jit(solution)/shard_map/pallas_call | solution.py:468
  77.9 11.6 %all_to_all.20 = f32[32,1,128]{2,1,0:T(1,128)S(1)} all-to-all(f32[32,1,128]{2,1,0:T(1,128)S(1)} %bitcast.32), channel_id=1, replica_groups=mesh['y'=4,'x_hi'=2,'core'=2,'x_lo'=2,'z'=16] {'y','x_hi','core','x_lo'}, dimensions={0} | all-to-all | bytes 32768 | tf_op jit(solution)/shard_map/all_to_all | solution.py:428
  89.5 17.4 %all_to_all.21 = f32[16,1,128]{2,1,0:T(1,128)S(1)} all-to-all(f32[16,1,128]{2,1,0:T(1,128)S(1)} %bitcast.29), channel_id=1, replica_groups=mesh['y'=4,'x_hi'=2,'core'=2,'x_lo'=2,'z'=16] {'z'}, dimensions={0} | all-to-all | bytes 16384 | tf_op jit(solution)/shard_map/all_to_all | solution.py:428
  106.8 0.0 collective-permute-done.9.xb_ref
  106.8 0.0 collective-permute-done.8.xa_ref
  106.8 6.5 %shard_map.62 = (f32[12,64,128]{2,1,0:T(8,128)S(1)}, f32[12,64,128]{2,1,0:T(8,128)S(1)}, f32[32,128]{1,0:T(8,128)S(1)}) custom-call(s32[2]{0:T(128)S(1)} %pad_add_fusion.at_ref, f32[12,12]{1,0:T(8,128)S(1)} %get-tuple-element.34.gram_ref, f32[16,128]{1,0:T(8,128)S(1)} %bitcast.27, f32[12,160,256]{2,1,0:T(8,128)S(1)} %get-tuple-element.54.ext_ref, ...), custom_call_target="tpu_custom_call" | custom-call | flops 1000000000 | bytes 10000000 | tf_op jit(solution)/shard_map/pallas_call | solution.py:478
  113.4 12.1 %all_to_all.22 = f32[32,1,128]{2,1,0:T(1,128)S(1)} all-to-all(f32[32,1,128]{2,1,0:T(1,128)S(1)} %bitcast.31), channel_id=1, replica_groups=mesh['y'=4,'x_hi'=2,'core'=2,'x_lo'=2,'z'=16] {'y','x_hi','core','x_lo'}, dimensions={0} | all-to-all | bytes 32768 | tf_op jit(solution)/shard_map/all_to_all | solution.py:428
  125.5 13.8 %all_to_all.23 = f32[16,1,128]{2,1,0:T(1,128)S(1)} all-to-all(f32[16,1,128]{2,1,0:T(1,128)S(1)} %bitcast.30), channel_id=1, replica_groups=mesh['y'=4,'x_hi'=2,'core'=2,'x_lo'=2,'z'=16] {'z'}, dimensions={0} | all-to-all | bytes 16384 | tf_op jit(solution)/shard_map/all_to_all | solution.py:428
  139.3 0.9 shard_map.64
  (2 shorter events, 0.0 us)
Async XLA Ops:
  0.0 36.7 %copy-start.4 = (f32[32,12]{0,1:T(8,128)S(1)}, f32[32,12]{0,1:T(8,128)}, u32[]{:S(2)}) copy-start(f32[32,12]{0,1:T(8,128)} %param.7) | copy-start | bytes 4612
  0.0 36.7 %copy-start.6 = (f32[33]{0:T(128)S(1)}, f32[33]{0:T(128)}, u32[]{:S(2)}) copy-start(f32[33]{0:T(128)} %ty_ref.1) | copy-start | bytes 400
  0.0 36.7 %copy-start.5 = (f32[33]{0:T(128)S(1)}, f32[33]{0:T(128)}, u32[]{:S(2)}) copy-start(f32[33]{0:T(128)} %tx_ref.1) | copy-start | bytes 400
  0.1 1.0 copy-start
  1.1 1.0 copy-start.2
  2.1 0.7 copy-start.3
  5.5 22.9 %collective-permute-start = (f32[12,40,128]{2,1,0:T(8,128)S(1)}, f32[12,40,128]{2,1,0:T(8,128)S(1)}, u32[]{:S(2)}, u32[]{:S(2)}) collective-permute-start(f32[12,40,128]{2,1,0:T(8,128)S(1)} %get-tuple-element.35), channel_id=1, source_target_pairs={{0,1},{1,0},{2,3},{3,2},{4,5},{5,4},{6,7},{7,6},{8,9},{9,8},{10,11... | collective-permute-start | bytes 737288 | tf_op jit(solution)/shard_map/ppermute | solution.py:424
  9.9 18.6 %collective-permute-start.1 = (f32[12,40,128]{2,1,0:T(8,128)S(1)}, f32[12,40,128]{2,1,0:T(8,128)S(1)}, u32[]{:S(2)}, u32[]{:S(2)}) collective-permute-start(f32[12,40,128]{2,1,0:T(8,128)S(1)} %get-tuple-element.36), channel_id=1, source_target_pairs={{0,31},{1,2},{2,1},{3,4},{4,3},{5,6},{6,5},{7,8},{8,7},{9,10},{10,... | collective-permute-start | bytes 737288 | tf_op jit(solution)/shard_map/ppermute | solution.py:423
  21.0 20.7 %collective-permute-start.2 = (f32[12,80,128]{2,1,0:T(8,128)S(1)}, f32[12,80,128]{2,1,0:T(8,128)S(1)}, u32[]{:S(2)}, u32[]{:S(2)}) collective-permute-start(f32[12,80,128]{2,1,0:T(8,128)S(1)} %get-tuple-element.40), channel_id=1, source_target_pairs={{0,32},{32,0},{64,96},{96,64},{128,160},{160,128},{192,224},{224,1... | collective-permute-start | bytes 1474568 | tf_op jit(solution)/shard_map/ppermute | solution.py:424
  24.2 17.6 %collective-permute-start.3 = (f32[12,80,128]{2,1,0:T(8,128)S(1)}, f32[12,80,128]{2,1,0:T(8,128)S(1)}, u32[]{:S(2)}, u32[]{:S(2)}) collective-permute-start(f32[12,80,128]{2,1,0:T(8,128)S(1)} %get-tuple-element.41), channel_id=1, source_target_pairs={{0,480},{32,64},{64,32},{96,128},{128,96},{160,192},{192,160},{224... | collective-permute-start | bytes 1474568 | tf_op jit(solution)/shard_map/ppermute | solution.py:423
  29.5 12.2 %collective-permute-start.4 = (f32[12,56,128]{2,1,0:T(8,128)S(1)}, f32[12,56,128]{2,1,0:T(8,128)S(1)}, u32[]{:S(2)}, u32[]{:S(2)}) collective-permute-start(f32[12,56,128]{2,1,0:T(8,128)S(1)} %get-tuple-element.42), channel_id=1, source_target_pairs={{0,32},{32,0},{64,96},{96,64},{128,160},{160,128},{192,224},{224,1... | collective-permute-start | bytes 1032200 | tf_op jit(solution)/shard_map/ppermute | solution.py:424
  34.4 14.3 %copy-start.1 = (f32[1,12,64,128]{3,2,1,0:T(8,128)S(1)}, f32[1,12,64,128]{3,2,1,0:T(8,128)}, u32[]{:S(2)}) copy-start(f32[1,12,64,128]{3,2,1,0:T(8,128)} %param.5) | copy-start | bytes 1179652
  34.4 14.2 %collective-permute-start.5 = (f32[12,56,128]{2,1,0:T(8,128)S(1)}, f32[12,56,128]{2,1,0:T(8,128)S(1)}, u32[]{:S(2)}, u32[]{:S(2)}) collective-permute-start(f32[12,56,128]{2,1,0:T(8,128)S(1)} %get-tuple-element.43), channel_id=1, source_target_pairs={{0,480},{32,64},{64,32},{96,128},{128,96},{160,192},{192,160},{224... | collective-permute-start | bytes 1032200 | tf_op jit(solution)/shard_map/ppermute | solution.py:423
  55.8 5.9 %collective-permute-start.6 = (f32[12,24,128]{2,1,0:T(8,128)S(1)}, f32[12,24,128]{2,1,0:T(8,128)S(1)}, u32[]{:S(2)}, u32[]{:S(2)}) collective-permute-start(f32[12,24,128]{2,1,0:T(8,128)S(1)} %get-tuple-element.56), channel_id=1, source_target_pairs={{0,1},{1,0},{2,3},{3,2},{4,5},{5,4},{6,7},{7,6},{8,9},{9,8},{10,11... | collective-permute-start | bytes 442376 | tf_op jit(solution)/shard_map/ppermute | solution.py:424
  57.8 8.0 %collective-permute-start.7 = (f32[12,24,128]{2,1,0:T(8,128)S(1)}, f32[12,24,128]{2,1,0:T(8,128)S(1)}, u32[]{:S(2)}, u32[]{:S(2)}) collective-permute-start(f32[12,24,128]{2,1,0:T(8,128)S(1)} %get-tuple-element.57), channel_id=1, source_target_pairs={{0,31},{1,2},{2,1},{3,4},{4,3},{5,6},{6,5},{7,8},{8,7},{9,10},{10,... | collective-permute-start | bytes 442376 | tf_op jit(solution)/shard_map/ppermute | solution.py:423
  66.8 40.1 %collective-permute-start.9 = (f32[12,64,128]{2,1,0:T(8,128)S(1)}, f32[12,64,128]{2,1,0:T(8,128)S(1)}, u32[]{:S(2)}, u32[]{:S(2)}) collective-permute-start(f32[12,64,128]{2,1,0:T(8,128)S(1)} %get-tuple-element.59), channel_id=1, source_target_pairs={{0,480},{32,64},{64,32},{96,128},{128,96},{160,192},{192,160},{224... | collective-permute-start | bytes 1179656 | tf_op jit(solution)/shard_map/ppermute | solution.py:423
  69.5 37.3 %collective-permute-start.8 = (f32[12,64,128]{2,1,0:T(8,128)S(1)}, f32[12,64,128]{2,1,0:T(8,128)S(1)}, u32[]{:S(2)}, u32[]{:S(2)}) collective-permute-start(f32[12,64,128]{2,1,0:T(8,128)S(1)} %get-tuple-element.59), channel_id=1, source_target_pairs={{0,32},{32,0},{64,96},{96,64},{128,160},{160,128},{192,224},{224,1... | collective-permute-start | bytes 1179656 | tf_op jit(solution)/shard_map/ppermute | solution.py:424

commit v3 on v2

v3 whole, which is shorter than its diff:
```python
import functools

import jax
import jax.numpy as jnp
from jax import lax
from jax.experimental import pallas as pl
from jax.experimental.pallas import tpu as pltpu
from jax.sharding import Mesh
from jax.sharding import PartitionSpec as P

TAPS = 33
ITERS = 2
FLUOR = 12
CHAN = 32
ROWS = 64
COLS = 128

HALF = TAPS // 2
A_HALO = 3 * HALF
P_HALO = 2 * HALF
G_HALO = HALF
A_ROWS = ROWS + 2 * A_HALO
P_ROWS = ROWS + 2 * P_HALO
G_ROWS = ROWS + 2 * G_HALO

GX = ("y", "x_hi", "core")
GY = ("x_lo", "z")
NEAR = ("y", "x_hi", "core", "x_lo")
FAR = "z"

tiny_floor = 1e-06
f32 = jnp.float32
bf16 = jnp.bfloat16


SPACES = {"s": pltpu.SMEM, "v": pltpu.VMEM, "h": pltpu.HBM}


def kernel(body, ins, outs, cost, scratch=(), limit=32 * 2**20):
    return pl.pallas_call(
        body,
        in_specs=[pl.BlockSpec(memory_space=SPACES[kind]) for kind in ins],
        out_specs=[pl.BlockSpec(memory_space=pltpu.VMEM) for _ in outs],
        out_shape=[jax.ShapeDtypeStruct(shape, dtype) for shape, dtype in outs],
        scratch_shapes=list(scratch),
        compiler_params=pltpu.CompilerParams(vmem_limit_bytes=limit),
        cost_estimate=pl.CostEstimate(flops=cost, bytes_accessed=cost // 100, transcendentals=0),
    )


def index(axes):
    place = 0
    for axis in axes:
        place = place * lax.axis_size(axis) + lax.axis_index(axis)
    return place


def roll(x, by):
    by = by % 128
    return x if by == 0 else pltpu.roll(x, by, axis=x.ndim - 1)


def lane_of(shape):
    return lax.broadcasted_iota(jnp.int32, shape, len(shape) - 1)


def split(x):
    high = x.astype(bf16)
    return high, (x - high.astype(f32)).astype(bf16)


def dot(a, b):
    return jnp.dot(a, b, preferred_element_type=f32)


def dot_right(x, w):
    high, low = split(x)
    return dot(jnp.concatenate([high, low, high], axis=1), w)


def stacked(x, depth):
    high, low = split(x)
    parts = [high, low, high]
    spare = depth - 3 * x.shape[0]
    if spare:
        parts.append(jnp.zeros((spare, x.shape[1]), bf16))
    return jnp.concatenate(parts, axis=0)


def side_position(index, halo):
    left = index - COLS - halo
    right = index - halo
    position = jnp.where(index < COLS, index, jnp.where(index < COLS + halo, left, right))
    return jnp.where(index < COLS + 2 * halo, position, 1 << 20)


def tap_matrix(taps_ref, offset):
    out = jnp.zeros(offset.shape, f32)
    for t in range(TAPS):
        out = jnp.where(offset == t, taps_ref[t], out)
    return out


def inside(position, base, size):
    where = position + base
    return jnp.logical_and(where >= 0, where < size)


def exact_dot(a, b):
    return lax.dot_general(a, b, (((1,), (0,)), ((), ())), precision=lax.Precision.HIGHEST, preferred_element_type=f32)


def rows_cols(shape):
    return lax.broadcasted_iota(jnp.int32, shape, 0), lax.broadcasted_iota(jnp.int32, shape, 1)


def put_right(x, ref):
    high, low = split(x)
    rows = x.shape[0]
    ref[:rows, :] = high
    ref[rows : 2 * rows, :] = high
    ref[2 * rows :, :] = low


def put_left(x, part, ref):
    high, low = split(x)
    ref[...] = jnp.where(part < 2, high.astype(f32), low.astype(f32)).astype(bf16)


def matrices_body(sizes, tx_ref, ty_ref, spectra_ref, after_ref, gram_ref, my, py, by, mx, px, bx):
    spectra = spectra_ref[...]
    gram_ref[...] = lax.dot_general(
        spectra, spectra, (((1,), (1,)), ((), ())), precision=lax.Precision.HIGHEST, preferred_element_type=f32
    )
    size_x, size_y = sizes
    base_x = index(GX) * ROWS
    base_y = index(GY) * COLS
    r, c = rows_cols((256, 256))
    source = side_position(r, P_HALO)
    target = side_position(c, G_HALO)
    okay = jnp.logical_and(inside(source, base_y, size_y), inside(target, base_y, size_y))
    put_right(jnp.where(okay, tap_matrix(ty_ref, target - source + HALF), 0.0), py)
    source = side_position(r, A_HALO)
    middle = c - P_HALO
    okay = jnp.logical_and(inside(source, base_y, size_y), inside(middle, base_y, size_y))
    first = jnp.where(okay, tap_matrix(ty_ref, source - middle + HALF), 0.0)
    middle = r - P_HALO
    second = jnp.where(inside(target, base_y, size_y), tap_matrix(ty_ref, target - middle + HALF), 0.0)
    put_right(exact_dot(first, second), my)
    r, c = rows_cols((256, 128))
    source = side_position(r, G_HALO)
    okay = inside(source, base_y, size_y)
    put_right(jnp.where(okay, tap_matrix(ty_ref, source - c + HALF), 0.0), by)
    r, c = rows_cols((128, 512))
    part = c // A_ROWS
    source = c - part * A_ROWS - A_HALO
    middle = r - P_HALO
    okay = jnp.logical_and(inside(source, base_x, size_x), inside(middle, base_x, size_x))
    okay = jnp.logical_and(okay, part < 3)
    first = jnp.where(okay, tap_matrix(tx_ref, source - middle + HALF), 0.0)
    r, c = rows_cols((G_ROWS, 128))
    target = r - G_HALO
    middle = c - P_HALO
    second = jnp.where(inside(target, base_x, size_x), tap_matrix(tx_ref, target - middle + HALF), 0.0)
    r, c = rows_cols((G_ROWS, 512))
    put_left(exact_dot(second, first), c // A_ROWS, mx)
    r, c = rows_cols((G_ROWS, 384))
    part = c // P_ROWS
    source = c - part * P_ROWS - P_HALO
    target = r - G_HALO
    okay = jnp.logical_and(inside(source, base_x, size_x), inside(target, base_x, size_x))
    put_left(jnp.where(okay, tap_matrix(tx_ref, target - source + HALF), 0.0), part, px)
    r, c = rows_cols((ROWS, 384))
    part = c // G_ROWS
    source = c - part * G_ROWS - G_HALO
    okay = jnp.logical_and(inside(source, base_x, size_x), part < 3)
    put_left(jnp.where(okay, tap_matrix(tx_ref, source - r + HALF), 0.0), part, bx)


def choose(odd, if_odd, if_even):
    return jnp.where(odd == 1, if_odd, if_even)


def edge_rows(odd_x, pairing, depth):
    top = odd_x == 1 if pairing == 0 else odd_x == 0
    return pl.multiple_of(jnp.where(top, 0, ROWS - depth), 16)


def pack_x(odd_x, pairing, a_ref, p_ref, out_ref):
    a_rows = pl.ds(edge_rows(odd_x, pairing, A_HALO), A_HALO)
    p_rows = pl.ds(edge_rows(odd_x, pairing, P_HALO), P_HALO)
    for f in range(FLUOR):
        out_ref[f, :A_HALO, :] = a_ref[f, a_rows, :]
        out_ref[f, A_HALO:, :] = p_ref[f, p_rows, :]


def project_body(s_hbm, a_hbm, m_hbm, p_ref, xb_ref, xa_ref, ya_ref, yb_ref, spectra_ref, a_ref, m_ref, sems):
    step = 16
    copy_s = pltpu.make_async_copy(s_hbm, spectra_ref, sems.at[5])
    copy_s.start()
    copies = [
        pltpu.make_async_copy(m_hbm.at[:, pl.ds(k * step, step), :], m_ref.at[:, pl.ds(k * step, step), :], sems.at[k])
        for k in range(ROWS // step)
    ]
    for copy in copies:
        copy.start()
    copy_a = pltpu.make_async_copy(a_hbm, a_ref, sems.at[ROWS // step])
    copy_a.start()
    copy_s.wait()
    for k, copy in enumerate(copies):
        copy.wait()
        start = k * step
        acc = [jnp.zeros((step, COLS), f32) for _ in range(FLUOR)]
        for c in range(CHAN):
            seen = m_ref[c, start : start + step, :].astype(f32)
            for f in range(FLUOR):
                acc[f] = acc[f] + spectra_ref[f, c] * seen
        for f in range(FLUOR):
            p_ref[f, start : start + step, :] = acc[f]
    copy_a.wait()
    odd_x = index(GX) % 2
    pack_x(odd_x, 1, a_ref, p_ref, xb_ref)
    pack_x(odd_x, 0, a_ref, p_ref, xa_ref)
    odd_y = index(GY) % 2
    lane = lane_of((32, 128))
    lane8 = lane_of((8, 128))
    for f in range(FLUOR):
        edges = []
        for a_from, p_from in ((0, 0), (COLS - A_HALO, COLS - P_HALO)):
            top = roll(a_ref[f, :32, :], -a_from)
            low = roll(a_ref[f, 32:, :], A_HALO - a_from)
            side = roll(p_ref[f, :32, :], 2 * A_HALO - p_from)
            main = jnp.where(lane < A_HALO, top, jnp.where(lane < 2 * A_HALO, low, side))
            rest = roll(p_ref[f, 32:40, :], -p_from)
            for k in range(1, 4):
                piece = roll(p_ref[f, 32 + 8 * k : 40 + 8 * k, :], 32 * k - p_from)
                rest = jnp.where(lane8 < 32 * k, rest, piece)
            edges.append((main, rest))
        (left, left_rest), (right, right_rest) = edges
        ya_ref[f, :32, :] = choose(odd_y, left, right)
        yb_ref[f, :32, :] = choose(odd_y, right, left)
        ya_ref[f, 32:, :] = choose(odd_y, left_rest, right_rest)
        yb_ref[f, 32:, :] = choose(odd_y, right_rest, left_rest)


def pack_corner(odd_x, pairing, side_ref, ps_ref, out_ref):
    lane = lane_of((32, 128))
    lane8 = lane_of((8, 128))
    lane16 = lane_of((16, 128))
    spare = 2 * A_HALO
    a_rows = pl.ds(edge_rows(odd_x, pairing, A_HALO), A_HALO)
    p_rows = pl.ds(edge_rows(odd_x, pairing, P_HALO), P_HALO)
    for f in range(FLUOR):
        p_top = ps_ref[f, p_rows, :]
        a_side = side_ref[f, a_rows, :]
        out_ref[f, :32, :] = jnp.where(lane < spare, a_side[:32], roll(p_top, spare))
        out_ref[f, 32:48, :] = jnp.where(lane16 < spare, a_side[32:], roll(p_top[:16], spare - P_HALO))
        out_ref[f, 48:, :] = jnp.where(lane8 < P_HALO, roll(p_top[16:24], -P_HALO), p_top[24:])


def corner_body(ya_ref, yb_ref, side_ref, ps_ref, cb_ref, ca_ref):
    odd_x = index(GX) % 2
    odd_y = index(GY) % 2
    lane = lane_of((32, 128))
    lane8 = lane_of((8, 128))
    for f in range(FLUOR):
        first = ya_ref[f, :32, :]
        second = yb_ref[f, :32, :]
        left = choose(odd_y, first, second)
        right = choose(odd_y, second, first)
        side_ref[f, :32, :] = jnp.where(lane < A_HALO, left, jnp.where(lane < 2 * A_HALO, roll(right, A_HALO), 0.0))
        side_ref[f, 32:, :] = jnp.where(lane < A_HALO, roll(left, -A_HALO), jnp.where(lane < 2 * A_HALO, right, 0.0))
        ps_ref[f, :32, :] = jnp.where(
            lane < P_HALO, roll(left, -2 * A_HALO), jnp.where(lane < 2 * P_HALO, roll(right, P_HALO - 2 * A_HALO), 0.0)
        )
        first = ya_ref[f, 32:, :]
        second = yb_ref[f, 32:, :]
        left = choose(odd_y, first, second)
        right = choose(odd_y, second, first)
        for k in range(4):
            ps_ref[f, 32 + 8 * k : 40 + 8 * k, :] = jnp.where(
                lane8 < P_HALO, roll(left, -32 * k), jnp.where(lane8 < 2 * P_HALO, roll(right, P_HALO - 32 * k), 0.0)
            )
    pack_corner(odd_x, 0, side_ref, ps_ref, ca_ref)
    pack_corner(odd_x, 1, side_ref, ps_ref, cb_ref)


GROUP = 4


def along_y(x, w, put):
    for f in range(0, FLUOR, GROUP):
        part = x(slice(f, f + GROUP))
        out = dot_right(part.reshape(-1, part.shape[2]), w)
        out = out.reshape(GROUP, part.shape[1], out.shape[1])
        for k in range(GROUP):
            put(f + k, out[k])


X_GROUP = 4


def along_x(m, stack, out_ref):
    for f in range(0, FLUOR, X_GROUP):
        out = dot(m, jnp.concatenate([stack(f + k) for k in range(X_GROUP)], axis=1))
        for k in range(X_GROUP):
            out_ref[f + k] = out[:, 256 * k : 256 * k + 256]


def wide(main, side):
    return jnp.concatenate([main, side], axis=2)


def mix(gram_ref, v_ref, d_ref, g_ref):
    step = 8
    for start in range(0, G_ROWS, step):
        part = [v_ref[f, start : start + step, :] for f in range(FLUOR)]
        for f in range(FLUOR):
            acc = -d_ref[f, start : start + step, :]
            for k in range(FLUOR):
                acc = acc + gram_ref[f, k] * part[k]
            g_ref[f, start : start + step, :] = acc


def sums(gram_ref, g_ref, by, bx, y_ref, z_ref, sum_ref):
    along_x(bx[...], lambda f: stacked(g_ref[f], 384), y_ref)

    def put(f, z):
        z_ref[f] = z

    along_y(lambda part: y_ref[part], by[...], put)
    grad = jnp.zeros((8, 128), f32)
    image = jnp.zeros((8, 128), f32)
    for start in range(0, ROWS, 8):
        part = [z_ref[f, start : start + 8, :] for f in range(FLUOR)]
        for f in range(FLUOR):
            acc = gram_ref[f, 0] * part[0]
            for k in range(1, FLUOR):
                acc = acc + gram_ref[f, k] * part[k]
            image = image + acc * part[f]
            g = g_ref[f, G_HALO + start : G_HALO + start + 8, :COLS]
            grad = grad + g * g
    grad = jnp.sum(grad, axis=0, keepdims=True)
    image = jnp.sum(image, axis=0, keepdims=True)
    lane = lane_of((1, 128))
    row = jnp.where(lane < 64, grad + roll(grad, 64), image + roll(image, 64))
    sum_ref[...] = jnp.broadcast_to(row, sum_ref.shape)


def step_length(total_ref):
    total = jnp.sum(total_ref[...], axis=0, keepdims=True)
    lane = lane_of((1, 128))
    grad = jnp.sum(jnp.where(lane < 64, total, 0.0), axis=1, keepdims=True)
    image = jnp.sum(jnp.where(lane < 64, 0.0, total), axis=1, keepdims=True)
    return grad / (image + tiny_floor)


def put_stack(ref, f, start, depth, x):
    high, low = split(x)
    for at, part in ((0, high), (depth, low), (2 * depth, high)):
        ref[f, pl.ds(pl.multiple_of(start + at, 16), x.shape[0]), :] = part


def along_half(x, w_ref, start, put):
    w = jnp.concatenate([w_ref[256 * k + start : 256 * k + start + 128, :] for k in range(3)], axis=0)
    along_y(x, w, put)


def store(ref):
    def put(f, x):
        ref[f] = x

    return put


def own_body(
    a_ref, side_ref, p_ref, ps_ref, xb_ref, xa_ref, my, py, u_ref, w_ref, ua_ref, ub_ref, wa_ref, wb_ref
):
    along_y(lambda part: wide(p_ref[part], ps_ref[part]), py[...], store(w_ref))
    along_y(lambda part: wide(a_ref[part], side_ref[part]), my[...], store(u_ref))
    along_half(lambda part: xa_ref[part, :A_HALO, :], my, 0, store(ua_ref))
    along_half(lambda part: xb_ref[part, :A_HALO, :], my, 0, store(ub_ref))
    along_half(lambda part: xa_ref[part, A_HALO:, :], py, 0, store(wa_ref))
    along_half(lambda part: xb_ref[part, A_HALO:, :], py, 0, store(wb_ref))


def first_body(
    gram_ref, u_ref, w_ref, ua_ref, ub_ref, wa_ref, wb_ref, cb_ref, ca_ref, my, py, mx, px,
    d_ref, g_ref, ya_ref, yb_ref, v_ref, su_ref, sw_ref, side_ref,
):
    odd_x = index(GX) % 2
    odd_y = index(GY) % 2
    lane = lane_of((32, 128))
    lane16 = lane_of((16, 128))
    lane8 = lane_of((8, 128))
    spare = 2 * A_HALO
    su_ref[:, 3 * A_ROWS :, :] = jnp.zeros((FLUOR, 512 - 3 * A_ROWS, 256), bf16)
    for u_part, w_part, corner, above in (
        (ua_ref, wa_ref, ca_ref, odd_x == 1),
        (ub_ref, wb_ref, cb_ref, odd_x == 0),
    ):
        for f in range(FLUOR):
            left = roll(corner[f, :32, :], -spare)
            right = roll(corner[f, 32:48, :], P_HALO - spare)
            last = corner[f, 48:, :]
            side_ref[f, :16, :] = jnp.where(lane16 < P_HALO, left[:16], jnp.where(lane16 < 2 * P_HALO, right, 0.0))
            side_ref[f, 16:24, :] = jnp.where(
                lane8 < P_HALO, left[16:24], jnp.where(lane8 < 2 * P_HALO, roll(last, P_HALO), 0.0)
            )
            side_ref[f, 24:, :] = jnp.where(lane8 < P_HALO, left[24:], jnp.where(lane8 < 2 * P_HALO, last, 0.0))
        a_at = jnp.where(above, 0, A_HALO + ROWS)
        p_at = jnp.where(above, 0, P_HALO + ROWS)
        along_half(
            lambda part: side_ref[part],
            py,
            128,
            lambda f, x: put_stack(sw_ref, f, p_at, P_ROWS, x + w_part[f]),
        )
        along_half(
            lambda part: corner[part, :A_HALO, :],
            my,
            128,
            lambda f, x: put_stack(su_ref, f, a_at, A_ROWS, x + u_part[f]),
        )
    for f in range(FLUOR):
        put_stack(sw_ref, f, P_HALO, P_ROWS, w_ref[f])
        put_stack(su_ref, f, A_HALO, A_ROWS, u_ref[f])
    along_x(px[...], lambda f: sw_ref[f], d_ref)
    along_x(mx[...], lambda f: su_ref[f], v_ref)
    mix(gram_ref, v_ref, d_ref, g_ref)
    lane = lane_of((24, 128))
    for f in range(FLUOR):
        edges = []
        for start in (G_HALO, COLS - G_HALO - 32):
            out = roll(g_ref[f, :24, :COLS], -start)
            for k in range(1, 4):
                piece = roll(g_ref[f, 24 * k : 24 * k + 24, :COLS], 32 * k - start)
                out = jnp.where(lane < 32 * k, out, piece)
            edges.append(out)
        ya_ref[f] = choose(odd_y, edges[0], edges[1])
        yb_ref[f] = choose(odd_y, edges[1], edges[0])


def probe_body(gram_ref, g_ref, by, bx, sum_ref, y_ref, z_ref):
    sums(gram_ref, g_ref, by, bx, y_ref, z_ref, sum_ref)


def relay(near_ref, out_ref):
    out_ref[...] = jnp.broadcast_to(jnp.sum(near_ref[...], axis=0, keepdims=True), out_ref.shape)


def outer_body(near_ref, g_ref, ya_ref, yb_ref, far_ref, side_ref, send_ref):
    relay(near_ref, far_ref)
    odd_y = index(GY) % 2
    lane = lane_of((24, 128))
    for f in range(FLUOR):
        left = choose(odd_y, ya_ref[f], yb_ref[f])
        right = choose(odd_y, yb_ref[f], ya_ref[f])
        for k in range(4):
            own = roll(g_ref[f, 24 * k : 24 * k + 24, COLS:], 32)
            side_ref[f, 24 * k : 24 * k + 24, :] = jnp.where(
                lane < 32,
                roll(left, -32 * k),
                jnp.where(lane < 64, own, jnp.where(lane < 96, roll(right, 64 - 32 * k), 0.0)),
            )
        send_ref[f, :32, :] = g_ref[f, 2 * G_HALO : 2 * G_HALO + 32, :COLS]
        send_ref[f, 32:, :] = side_ref[f, 2 * G_HALO : 2 * G_HALO + 32, :]


def second_body(
    gram_ref, total_ref, a_ref, side_ref, za_ref, zb_ref, ca_ref, cb_ref, d_ref, g_ref, gs_ref, xa_ref, xb_ref,
    my, mx, by, bx,
    a_out, g_out, sum_ref, v_ref, n_ref, y_ref, z_ref, x_ref, u_ref,
):
    odd_x = index(GX) % 2
    t = step_length(total_ref)
    for f in range(FLUOR):
        tile = jnp.maximum(a_ref[f] - t * g_ref[f, G_HALO : G_HALO + ROWS, :COLS], 0.0)
        a_out[f] = tile
        x_ref[f, A_HALO : A_HALO + ROWS, :COLS] = tile
        x_ref[f, A_HALO : A_HALO + ROWS, COLS:] = jnp.maximum(
            side_ref[f] - t * gs_ref[f, G_HALO : G_HALO + ROWS, :], 0.0
        )
        for above, main, corner, far, near in (
            (True, choose(odd_x, za_ref[f, :A_HALO, :], zb_ref[f, :A_HALO, :]),
             choose(odd_x, ca_ref[f, :A_HALO, :], cb_ref[f, :A_HALO, :]), choose(odd_x, xa_ref[f], xb_ref[f]),
             slice(0, G_HALO)),
            (False, choose(odd_x, zb_ref[f, :A_HALO, :], za_ref[f, :A_HALO, :]),
             choose(odd_x, cb_ref[f, :A_HALO, :], ca_ref[f, :A_HALO, :]), choose(odd_x, xb_ref[f], xa_ref[f]),
             slice(G_ROWS - G_HALO, G_ROWS)),
        ):
            parts = [far[:32], g_ref[f, near, :COLS]], [far[32:], gs_ref[f, near, :]]
            if not above:
                parts = [part[::-1] for part in parts]
            rows = slice(0, A_HALO) if above else slice(A_HALO + ROWS, A_ROWS)
            x_ref[f, rows, :COLS] = jnp.maximum(main - t * jnp.concatenate(parts[0], axis=0), 0.0)
            x_ref[f, rows, COLS:] = jnp.maximum(corner - t * jnp.concatenate(parts[1], axis=0), 0.0)

    def put(f, u):
        u_ref[f] = u

    along_y(lambda part: x_ref[part], my[...], put)
    along_x(mx[...], lambda f: stacked(u_ref[f], 512), v_ref)
    mix(gram_ref, v_ref, d_ref, n_ref)
    sums(gram_ref, n_ref, by, bx, y_ref, z_ref, sum_ref)
    for f in range(FLUOR):
        g_out[f] = n_ref[f, G_HALO : G_HALO + ROWS, :COLS]


def last_body(total_ref, a_ref, g_ref, out_ref):
    t = step_length(total_ref)
    for f in range(FLUOR):
        out_ref[f] = jnp.maximum(a_ref[f] - t * g_ref[f], 0.0)


TILE = (FLUOR, ROWS, COLS)
G_SHAPE = (FLUOR, G_ROWS, 256)
PROBE_SCRATCH = (pltpu.VMEM((FLUOR, ROWS, 256), f32), pltpu.VMEM(TILE, f32))
OWN_COST = 10**10
NEAR_COUNT = 32
FAR_COUNT = 16

first_call = kernel(
    first_body,
    "s" + "v" * 12,
    [(G_SHAPE, f32)] * 2 + [((FLUOR, 24, 128), f32)] * 2,
    10**9,
    [
        pltpu.VMEM(G_SHAPE, f32),
        pltpu.VMEM((FLUOR, 512, 256), bf16),
        pltpu.VMEM((FLUOR, 3 * P_ROWS, 256), bf16),
        pltpu.VMEM((FLUOR, P_HALO, 128), f32),
    ],
)
probe_call = kernel(probe_body, "svvv", [((NEAR_COUNT, 128), f32)], 10**9, PROBE_SCRATCH)
second_call = kernel(
    second_body,
    "s" + "v" * 16,
    [(TILE, f32)] * 2 + [((NEAR_COUNT, 128), f32)],
    10**9,
    [
        pltpu.VMEM(G_SHAPE, f32),
        pltpu.VMEM(G_SHAPE, f32),
        *PROBE_SCRATCH,
        pltpu.VMEM((FLUOR, A_ROWS, 256), f32),
        pltpu.VMEM((FLUOR, A_ROWS, 256), f32),
    ],
)


def length(axes):
    count = 1
    for axis in axes:
        count *= lax.axis_size(axis)
    return count


def trade(first, second, axes):
    return trade_first(first, axes), trade_second(second, axes)


def trade_first(edge, axes):
    return lax.ppermute(edge, axes, [(i, i ^ 1) for i in range(length(axes))])


def trade_second(edge, axes):
    count = length(axes)
    return lax.ppermute(edge, axes, [(i, (i + (1 if i % 2 else -1)) % count) for i in range(count)])


def spread(rows, axes):
    got = lax.all_to_all(rows.reshape(rows.shape[0], 1, 128), axes, 0, 0, tiled=True)
    return got.reshape(rows.shape[0], 128)


def local(sizes, abundance_start, measured, spectra, taps_x, taps_y):
    assert (length(NEAR), length((FAR,))) == (NEAR_COUNT, FAR_COUNT)

    edge = (FLUOR, A_HALO + P_HALO, 128)
    a0 = abundance_start[0]
    p, xb, xa, ya, yb = kernel(
        project_body,
        "hhh",
        [(TILE, f32)] + [(edge, f32)] * 2 + [((FLUOR, 40, 128), f32)] * 2,
        10**7,
        [
            pltpu.SMEM((FLUOR, CHAN), f32),
            pltpu.VMEM(TILE, f32),
            pltpu.VMEM((CHAN, ROWS, COLS), bf16),
            pltpu.SemaphoreType.DMA((6,)),
        ],
        60_000_000,
    )(spectra.T, a0, measured[0])
    za, zb = trade(xa, xb, GX)
    ya, yb = trade(ya, yb, GY)
    corner = (FLUOR, 56, 128)
    side, ps, cb, ca = kernel(corner_body, "vv", [(TILE, f32)] * 2 + [(corner, f32)] * 2, 10**7)(ya, yb)
    ca, cb = trade(ca, cb, GX)
    gram, my, py, by, mx, px, bx = kernel(
        functools.partial(matrices_body, sizes),
        "ssvv",
        [((FLUOR, FLUOR), f32)] + [((768, 256), bf16)] * 2 + [((768, 128), bf16)]
        + [((G_ROWS, 512), bf16), ((G_ROWS, 384), bf16), ((ROWS, 384), bf16)],
        10**9,
    )(taps_x, taps_y, spectra.T, ps)
    halves = kernel(
        own_body,
        "v" * 8,
        [((FLUOR, rows, 256), f32) for rows in (ROWS, ROWS, A_HALO, A_HALO, P_HALO, P_HALO)],
        OWN_COST,
    )(a0, side, p, ps, zb, za, my, py)
    d, g, ya, yb = first_call(gram, *halves, cb, ca, my, py, mx, px)
    ya, yb = trade(ya, yb, GY)
    (partial,) = probe_call(gram, g, by, bx)
    near = spread(partial, NEAR)
    far, g_side, send = kernel(
        outer_body,
        "vvvv",
        [((FAR_COUNT, 128), f32), ((FLUOR, G_ROWS, 128), f32), ((FLUOR, 64, 128), f32)],
        10**8,
    )(near, g, ya, yb)
    xa, xb = trade(send, send, GX)
    total = spread(far, FAR)
    a1, g1, partial = second_call(
        gram, total, a0, side, za, zb, ca, cb, d, g, g_side, xa, xb, my, mx, by, bx
    )
    (far,) = kernel(relay, "v", [((FAR_COUNT, 128), f32)], 10**6)(spread(partial, NEAR))
    total = spread(far, FAR)
    (out,) = kernel(last_body, "vvv", [(TILE, f32)], 10**7)(total, a1, g1)
    return out[None]


def solution(mesh):
    count_x, count_y = mesh.shape["gx"], mesh.shape["gy"]
    parts = Mesh(
        mesh.devices.reshape(count_x // 4, 2, 2, 2, count_y // 2), ("y", "x_hi", "core", "x_lo", "z")
    )
    sizes = (count_x * ROWS, count_y * COLS)
    tiles = P(None, None, GX, GY)
    return jax.shard_map(
        functools.partial(local, sizes),
        mesh=parts,
        in_specs=(tiles, tiles, P(), P(), P()),
        out_specs=tiles,
        check_vma=False,
    )
```

time: 141 us -> 130 us (0.922)
  Pallas kernels: 26.2 us -> 21.3 us
  waiting for transfers between devices: 11.8 us -> 7.17 us
  local copies, waits for them, and re-layouts: 2.75 us -> 0.02 us
  blocking collectives: 54.9 us -> 57.4 us
    pallas_call x10, Pallas kernels: 26.2 us -> 21.3 us  [the longest x1 5.04 us: local(): kernel(functools.partial(matrices_body, sizes), 'ssvv', [((FLUOR, FLUOR),...]
    ppermute x10, waiting for transfers between devices: 11.8 us -> 7.17 us  [the longest x5 7.15 us: trade_second(): lax.ppermute(edge, axes, [(i, (i + (1 if i % 2 else -1)) % count) for i i...]
    unnamed x14 -> x10, local copies, waits for them, and re-layouts: 2.75 us -> 0.02 us
    all_to_all x4, blocking collectives: 54.9 us -> 57.4 us  [spread(): lax.all_to_all(rows.reshape(rows.shape[0], 1, 128), axes, 0, 0, tiled=True)]
  transfers between devices with their start and end apart: 10 -> 10, of which waited for: 3 -> 2; matrix products, arithmetic and copies ran while one was open for 0% -> 0% of each run, Pallas kernels for 6% -> 7%
where the time goes in v3:
time: 130 us; the launch traced here: 129 us
  blocking collectives  57.4 us (44%)
  starting transfers between devices  43 us (33%)
  Pallas kernels  21.3 us (16%)
  waiting for transfers between devices  7.17 us (6%)
    all_to_all x4, blocking collectives, spread(): lax.all_to_all(rows.reshape(rows.shape[0], 1, 128), axes, 0, 0, tiled=True)  57.4 us
    ppermute x5, starting transfers between devices, trade_second(): lax.ppermute(edge, axes, [(i, (i + (1 if i % 2 else -1)) % count) for i i...  28.5 us
    ppermute x5, starting transfers between devices, trade_first(): return lax.ppermute(edge, axes, [(i, i ^ 1) for i in range(length(axes))])  14.5 us
    ppermute x5, waiting for transfers between devices, trade_second(): lax.ppermute(edge, axes, [(i, (i + (1 if i % 2 else -1)) % count) for i i...  7.15 us
    pallas_call x1, Pallas kernels, local(): kernel(functools.partial(matrices_body, sizes), 'ssvv', [((FLUOR, FLUOR),...  5.04 us
    pallas_call x1, Pallas kernels, local(): second_call(gram, total, a0, side, za, zb, ca, cb, d, g, g_side, xa, xb,...  4.28 us
    pallas_call x1, Pallas kernels, local(): kernel(project_body, 'hhh', [(TILE, f32)] + [(edge, f32)] * 2 + [((FLUOR,...  3.6 us
    pallas_call x1, Pallas kernels, local(): d, g, ya, yb = first_call(gram, *halves, cb, ca, my, py, mx, px)  3.43 us
  transfers between devices with their start and end apart: 10, of which 2 were waited for; matrix products, arithmetic and copies ran while one was open for 0% of the time, Pallas kernels for 7%

profile of v3, /device:TPU:1, one launch (start us, length us, event | category | flops | bytes accessed | tf_op | source)
XLA Modules:
  0.0 129.0 jit_solution(10392242906202690262)
XLA Ops:
  0.0 0.0 copy-start.1
  0.0 0.0 copy-start.4
  0.0 0.0 copy-start.3
  0.0 3.6 %shard_map.55 = (f32[12,64,128]{2,1,0:T(8,128)}, f32[12,80,128]{2,1,0:T(8,128)}, f32[12,80,128]{2,1,0:T(8,128)}, f32[12,40,128]{2,1,0:T(8,128)}, f32[12,40,128]{2,1,0:T(8,128)}) custom-call(f32[12,32]{1,0:T(8,128)} %bitcast.30, f32[12,64,128]{2,1,0:T(8,128)} %bitcast.20, bf16[32,64,128]{2,1,0:T(8,128)(2,1)} %bitcast.33), custom_call_target="tpu_custom_call" | custom-call | flops 10000000 | bytes 100000 | tf_op jit(solution)/shard_map/pallas_call | solution.py:581
  3.6 6.0 %collective-permute-start.2 = (f32[12,80,128]{2,1,0:T(8,128)}, f32[12,80,128]{2,1,0:T(8,128)S(1)}, u32[]{:S(2)}, u32[]{:S(2)}) collective-permute-start(f32[12,80,128]{2,1,0:T(8,128)} %get-tuple-element.43), channel_id=1, source_target_pairs={{0,480},{32,64},{64,32},{96,128},{128,96},{160,192},{192,160},{224... | collective-permute-start | bytes 1474568 | tf_op jit(solution)/shard_map/ppermute | solution.py:568
  9.7 4.7 %collective-permute-start.3 = (f32[12,80,128]{2,1,0:T(8,128)}, f32[12,80,128]{2,1,0:T(8,128)S(1)}, u32[]{:S(2)}, u32[]{:S(2)}) collective-permute-start(f32[12,80,128]{2,1,0:T(8,128)} %get-tuple-element.44), channel_id=1, source_target_pairs={{0,32},{32,0},{64,96},{96,64},{128,160},{160,128},{192,224},{224,1... | collective-permute-start | bytes 1474568 | tf_op jit(solution)/shard_map/ppermute | solution.py:563
  14.3 3.1 %collective-permute-start = (f32[12,40,128]{2,1,0:T(8,128)}, f32[12,40,128]{2,1,0:T(8,128)S(1)}, u32[]{:S(2)}, u32[]{:S(2)}) collective-permute-start(f32[12,40,128]{2,1,0:T(8,128)} %get-tuple-element.37), channel_id=1, source_target_pairs={{0,1},{1,0},{2,3},{3,2},{4,5},{5,4},{6,7},{7,6},{8,9},{9,8},{10,11... | collective-permute-start | bytes 737288 | tf_op jit(solution)/shard_map/ppermute | solution.py:563
  17.4 10.2 %collective-permute-start.1 = (f32[12,40,128]{2,1,0:T(8,128)}, f32[12,40,128]{2,1,0:T(8,128)S(1)}, u32[]{:S(2)}, u32[]{:S(2)}) collective-permute-start(f32[12,40,128]{2,1,0:T(8,128)} %get-tuple-element.38), channel_id=1, source_target_pairs={{0,31},{1,2},{2,1},{3,4},{4,3},{5,6},{6,5},{7,8},{8,7},{9,10},{10,... | collective-permute-start | bytes 737288 | tf_op jit(solution)/shard_map/ppermute | solution.py:568
  27.7 0.0 collective-permute-done.ya_ref
  27.7 6.3 %collective-permute-done.1.yb_ref = f32[12,40,128]{2,1,0:T(8,128)S(1)} collective-permute-done((f32[12,40,128]{2,1,0:T(8,128)}, f32[12,40,128]{2,1,0:T(8,128)S(1)}, u32[]{:S(2)}, u32[]{:S(2)}) %collective-permute-start.1) | collective-permute-done | bytes 245792 | tf_op jit(solution)/shard_map/ppermute | solution.py:568
  34.0 0.5 shard_map.56
  34.5 3.1 %collective-permute-start.4 = (f32[12,56,128]{2,1,0:T(8,128)S(1)}, f32[12,56,128]{2,1,0:T(8,128)S(1)}, u32[]{:S(2)}, u32[]{:S(2)}) collective-permute-start(f32[12,56,128]{2,1,0:T(8,128)S(1)} %get-tuple-element.53), channel_id=1, source_target_pairs={{0,480},{32,64},{64,32},{96,128},{128,96},{160,192},{192,160},{224... | collective-permute-start | bytes 1032200 | tf_op jit(solution)/shard_map/ppermute | solution.py:568
  37.6 2.5 %collective-permute-start.5 = (f32[12,56,128]{2,1,0:T(8,128)S(1)}, f32[12,56,128]{2,1,0:T(8,128)S(1)}, u32[]{:S(2)}, u32[]{:S(2)}) collective-permute-start(f32[12,56,128]{2,1,0:T(8,128)S(1)} %get-tuple-element.54), channel_id=1, source_target_pairs={{0,32},{32,0},{64,96},{96,64},{128,160},{160,128},{192,224},{224,1... | collective-permute-start | bytes 1032200 | tf_op jit(solution)/shard_map/ppermute | solution.py:563
  40.1 0.0 copy-done.1
  40.1 0.0 copy-done.4
  40.1 0.0 copy-done.3
  40.1 0.0 copy-start
  40.1 0.0 copy-start.2
  40.1 5.0 %shard_map.57 = (f32[12,12]{1,0:T(8,128)S(1)}, bf16[768,256]{1,0:T(8,128)(2,1)S(1)}, bf16[768,256]{1,0:T(8,128)(2,1)S(1)}, bf16[768,128]{1,0:T(8,128)(2,1)S(1)},...) custom-call(f32[33]{0:T(128)S(1)} %copy-done.3, f32[33]{0:T(128)S(1)} %copy-done.4, ...), custom_call_target="tpu_custom_call" | custom-call | flops 1000000000 | bytes 10000000 | tf_op jit(solution)/shard_map/pallas_call | solution.py:599
  45.2 0.0 collective-permute-done.2.xb_ref.zb_ref
  45.2 0.0 collective-permute-done.3.xa_ref.za_ref
  45.2 0.0 copy-done
  45.2 0.0 copy-done.2
  45.2 1.3 %shard_map.58 = (f32[12,64,256]{2,1,0:T(8,128)S(1)}, f32[12,64,256]{2,1,0:T(8,128)S(1)}, f32[12,48,256]{2,1,0:T(8,128)S(1)}, f32[12,48,256]{2,1,0:T(8,128)S(1)},...) custom-call(f32[12,64,128]{2,1,0:T(8,128)S(1)} %bitcast.21, f32[12,64,128]{2,1,0:T(8,128)S(1)} %get-tuple-element.41.side_ref, ...), custom_call_target="tpu_custom_call" | custom-call | flops 10000000000 | bytes 100000000 | tf_op jit(solution)/shard_map/pallas_call | solution.py:606
  46.5 0.8 collective-permute-done.4.cb_ref
  47.4 0.0 collective-permute-done.5.ca_ref
  47.4 3.4 %shard_map.59 = (f32[12,96,256]{2,1,0:T(8,128)S(1)}, f32[12,96,256]{2,1,0:T(8,128)S(1)}, f32[12,24,128]{2,1,0:T(8,128)S(1)}, f32[12,24,128]{2,1,0:T(8,128)S(1)}) custom-call(f32[12,12]{1,0:T(8,128)S(1)} %get-tuple-element.40.gram_ref, f32[12,64,256]{2,1,0:T(8,128)S(1)} %get-tuple-element.47.u_ref, f32[12,64,256]{2,1,0:T(8,128)S(1)} %get-tuple-element.48.w_ref, ...), custom_call_target="tpu_custom_call" | custom-call | flops 1000000000 | bytes 10000000 | tf_op jit(solution)/shard_map/pallas_call | solution.py:612
  50.8 1.9 %collective-permute-start.6 = (f32[12,24,128]{2,1,0:T(8,128)S(1)}, f32[12,24,128]{2,1,0:T(8,128)S(1)}, u32[]{:S(2)}, u32[]{:S(2)}) collective-permute-start(f32[12,24,128]{2,1,0:T(8,128)S(1)} %get-tuple-element.60), channel_id=1, source_target_pairs={{0,1},{1,0},{2,3},{3,2},{4,5},{5,4},{6,7},{7,6},{8,9},{9,8},{10,11... | collective-permute-start | bytes 442376 | tf_op jit(solution)/shard_map/ppermute | solution.py:563
  52.8 5.8 %collective-permute-start.7 = (f32[12,24,128]{2,1,0:T(8,128)S(1)}, f32[12,24,128]{2,1,0:T(8,128)S(1)}, u32[]{:S(2)}, u32[]{:S(2)}) collective-permute-start(f32[12,24,128]{2,1,0:T(8,128)S(1)} %get-tuple-element.61), channel_id=1, source_target_pairs={{0,31},{1,2},{2,1},{3,4},{4,3},{5,6},{6,5},{7,8},{8,7},{9,10},{10,... | collective-permute-start | bytes 442376 | tf_op jit(solution)/shard_map/ppermute | solution.py:568
  58.5 1.7 %shard_map.60 = f32[32,128]{1,0:T(8,128)S(1)} custom-call(f32[12,12]{1,0:T(8,128)S(1)} %get-tuple-element.40.gram_ref, f32[12,96,256]{2,1,0:T(8,128)S(1)} %get-tuple-element.57.g_ref, bf16[768,128]{1,0:T(8,128)(2,1)S(1)} %get-tuple-element.58.by, bf16[64,384]{1,0:T(8,128)(2,1)S(1)} %get-tuple-element.59.bx), custom_call_target="tpu_custom_call" | custom-call | flops 1000000000 | bytes 10000000 | tf_op jit(solution)/shard_map/pallas_call | solution.py:614
  60.3 12.9 %all_to_all.20 = f32[32,1,128]{2,1,0:T(1,128)S(1)} all-to-all(f32[32,1,128]{2,1,0:T(1,128)S(1)} %bitcast.29), channel_id=1, replica_groups=mesh['y'=4,'x_hi'=2,'core'=2,'x_lo'=2,'z'=16] {'y','x_hi','core','x_lo'}, dimensions={0} | all-to-all | bytes 32768 | tf_op jit(solution)/shard_map/all_to_all | solution.py:572
  73.1 0.0 collective-permute-done.6.ya_ref
  73.1 0.0 collective-permute-done.7.yb_ref
  73.2 0.5 shard_map.61
  73.6 3.4 %collective-permute-start.9 = (f32[12,64,128]{2,1,0:T(8,128)S(1)}, f32[12,64,128]{2,1,0:T(8,128)S(1)}, u32[]{:S(2)}, u32[]{:S(2)}) collective-permute-start(f32[12,64,128]{2,1,0:T(8,128)S(1)} %get-tuple-element.65), channel_id=1, source_target_pairs={{0,480},{32,64},{64,32},{96,128},{128,96},{160,192},{192,160},{224... | collective-permute-start | bytes 1179656 | tf_op jit(solution)/shard_map/ppermute | solution.py:568
  77.0 2.3 %collective-permute-start.8 = (f32[12,64,128]{2,1,0:T(8,128)S(1)}, f32[12,64,128]{2,1,0:T(8,128)S(1)}, u32[]{:S(2)}, u32[]{:S(2)}) collective-permute-start(f32[12,64,128]{2,1,0:T(8,128)S(1)} %get-tuple-element.65), channel_id=1, source_target_pairs={{0,32},{32,0},{64,96},{96,64},{128,160},{160,128},{192,224},{224,1... | collective-permute-start | bytes 1179656 | tf_op jit(solution)/shard_map/ppermute | solution.py:563
  79.3 16.6 %all_to_all.21 = f32[16,1,128]{2,1,0:T(1,128)S(1)} all-to-all(f32[16,1,128]{2,1,0:T(1,128)S(1)} %bitcast.32), channel_id=1, replica_groups=mesh['y'=4,'x_hi'=2,'core'=2,'x_lo'=2,'z'=16] {'z'}, dimensions={0} | all-to-all | bytes 16384 | tf_op jit(solution)/shard_map/all_to_all | solution.py:572
  95.9 0.0 collective-permute-done.9.xb_ref
  95.9 0.0 collective-permute-done.8.xa_ref
  95.9 4.3 %shard_map.62 = (f32[12,64,128]{2,1,0:T(8,128)S(1)}, f32[12,64,128]{2,1,0:T(8,128)S(1)}, f32[32,128]{1,0:T(8,128)S(1)}) custom-call(f32[12,12]{1,0:T(8,128)S(1)} %get-tuple-element.40.gram_ref, f32[16,128]{1,0:T(8,128)S(1)} %bitcast.25, f32[12,64,128]{2,1,0:T(8,128)S(1)} %bitcast.22, f32[12,64,128]{2,1,0:T(8,128)S(1)} %get-tuple-element.41.side_ref, ...), custom_call_target="tpu_custom_call" | custom-call | flops 1000000000 | bytes 10000000 | tf_op jit(solution)/shard_map/pallas_call | solution.py:624
  100.2 14.1 %all_to_all.22 = f32[32,1,128]{2,1,0:T(1,128)S(1)} all-to-all(f32[32,1,128]{2,1,0:T(1,128)S(1)} %bitcast.28), channel_id=1, replica_groups=mesh['y'=4,'x_hi'=2,'core'=2,'x_lo'=2,'z'=16] {'y','x_hi','core','x_lo'}, dimensions={0} | all-to-all | bytes 32768 | tf_op jit(solution)/shard_map/all_to_all | solution.py:572
  114.3 13.8 %all_to_all.23 = f32[16,1,128]{2,1,0:T(1,128)S(1)} all-to-all(f32[16,1,128]{2,1,0:T(1,128)S(1)} %bitcast.27), channel_id=1, replica_groups=mesh['y'=4,'x_hi'=2,'core'=2,'x_lo'=2,'z'=16] {'z'}, dimensions={0} | all-to-all | bytes 16384 | tf_op jit(solution)/shard_map/all_to_all | solution.py:572
  128.1 0.9 shard_map.64
  (1 shorter events, 0.0 us)
Async XLA Ops:
  0.0 40.1 %copy-start.1 = (f32[32,12]{0,1:T(8,128)S(1)}, f32[32,12]{0,1:T(8,128)}, u32[]{:S(2)}) copy-start(f32[32,12]{0,1:T(8,128)} %param.7) | copy-start | bytes 4612
  0.0 40.1 %copy-start.4 = (f32[33]{0:T(128)S(1)}, f32[33]{0:T(128)}, u32[]{:S(2)}) copy-start(f32[33]{0:T(128)} %ty_ref.1) | copy-start | bytes 400
  0.0 40.1 %copy-start.3 = (f32[33]{0:T(128)S(1)}, f32[33]{0:T(128)}, u32[]{:S(2)}) copy-start(f32[33]{0:T(128)} %tx_ref.1) | copy-start | bytes 400
  3.6 41.6 %collective-permute-start.2 = (f32[12,80,128]{2,1,0:T(8,128)}, f32[12,80,128]{2,1,0:T(8,128)S(1)}, u32[]{:S(2)}, u32[]{:S(2)}) collective-permute-start(f32[12,80,128]{2,1,0:T(8,128)} %get-tuple-element.43), channel_id=1, source_target_pairs={{0,480},{32,64},{64,32},{96,128},{128,96},{160,192},{192,160},{224... | collective-permute-start | bytes 1474568 | tf_op jit(solution)/shard_map/ppermute | solution.py:568
  9.7 35.5 %collective-permute-start.3 = (f32[12,80,128]{2,1,0:T(8,128)}, f32[12,80,128]{2,1,0:T(8,128)S(1)}, u32[]{:S(2)}, u32[]{:S(2)}) collective-permute-start(f32[12,80,128]{2,1,0:T(8,128)} %get-tuple-element.44), channel_id=1, source_target_pairs={{0,32},{32,0},{64,96},{96,64},{128,160},{160,128},{192,224},{224,1... | collective-permute-start | bytes 1474568 | tf_op jit(solution)/shard_map/ppermute | solution.py:563
  14.3 13.3 %collective-permute-start = (f32[12,40,128]{2,1,0:T(8,128)}, f32[12,40,128]{2,1,0:T(8,128)S(1)}, u32[]{:S(2)}, u32[]{:S(2)}) collective-permute-start(f32[12,40,128]{2,1,0:T(8,128)} %get-tuple-element.37), channel_id=1, source_target_pairs={{0,1},{1,0},{2,3},{3,2},{4,5},{5,4},{6,7},{7,6},{8,9},{9,8},{10,11... | collective-permute-start | bytes 737288 | tf_op jit(solution)/shard_map/ppermute | solution.py:563
  17.4 16.6 %collective-permute-start.1 = (f32[12,40,128]{2,1,0:T(8,128)}, f32[12,40,128]{2,1,0:T(8,128)S(1)}, u32[]{:S(2)}, u32[]{:S(2)}) collective-permute-start(f32[12,40,128]{2,1,0:T(8,128)} %get-tuple-element.38), channel_id=1, source_target_pairs={{0,31},{1,2},{2,1},{3,4},{4,3},{5,6},{6,5},{7,8},{8,7},{9,10},{10,... | collective-permute-start | bytes 737288 | tf_op jit(solution)/shard_map/ppermute | solution.py:568
  34.5 12.9 %collective-permute-start.4 = (f32[12,56,128]{2,1,0:T(8,128)S(1)}, f32[12,56,128]{2,1,0:T(8,128)S(1)}, u32[]{:S(2)}, u32[]{:S(2)}) collective-permute-start(f32[12,56,128]{2,1,0:T(8,128)S(1)} %get-tuple-element.53), channel_id=1, source_target_pairs={{0,480},{32,64},{64,32},{96,128},{128,96},{160,192},{192,160},{224... | collective-permute-start | bytes 1032200 | tf_op jit(solution)/shard_map/ppermute | solution.py:568
  37.6 9.8 %collective-permute-start.5 = (f32[12,56,128]{2,1,0:T(8,128)S(1)}, f32[12,56,128]{2,1,0:T(8,128)S(1)}, u32[]{:S(2)}, u32[]{:S(2)}) collective-permute-start(f32[12,56,128]{2,1,0:T(8,128)S(1)} %get-tuple-element.54), channel_id=1, source_target_pairs={{0,32},{32,0},{64,96},{96,64},{128,160},{160,128},{192,224},{224,1... | collective-permute-start | bytes 1032200 | tf_op jit(solution)/shard_map/ppermute | solution.py:563
  40.1 5.1 %copy-start = (f32[1,12,64,128]{3,2,1,0:T(8,128)S(1)}, f32[1,12,64,128]{3,2,1,0:T(8,128)}, u32[]{:S(2)}) copy-start(f32[1,12,64,128]{3,2,1,0:T(8,128)} %param.5) | copy-start | bytes 1179652
  40.1 5.1 %copy-start.2 = (f32[12,64,128]{2,1,0:T(8,128)S(1)}, f32[12,64,128]{2,1,0:T(8,128)}, u32[]{:S(2)}) copy-start(f32[12,64,128]{2,1,0:T(8,128)} %get-tuple-element.42.p_ref) | copy-start | bytes 1179652
  50.8 22.3 %collective-permute-start.6 = (f32[12,24,128]{2,1,0:T(8,128)S(1)}, f32[12,24,128]{2,1,0:T(8,128)S(1)}, u32[]{:S(2)}, u32[]{:S(2)}) collective-permute-start(f32[12,24,128]{2,1,0:T(8,128)S(1)} %get-tuple-element.60), channel_id=1, source_target_pairs={{0,1},{1,0},{2,3},{3,2},{4,5},{5,4},{6,7},{7,6},{8,9},{9,8},{10,11... | collective-permute-start | bytes 442376 | tf_op jit(solution)/shard_map/ppermute | solution.py:563
  52.8 20.4 %collective-permute-start.7 = (f32[12,24,128]{2,1,0:T(8,128)S(1)}, f32[12,24,128]{2,1,0:T(8,128)S(1)}, u32[]{:S(2)}, u32[]{:S(2)}) collective-permute-start(f32[12,24,128]{2,1,0:T(8,128)S(1)} %get-tuple-element.61), channel_id=1, source_target_pairs={{0,31},{1,2},{2,1},{3,4},{4,3},{5,6},{6,5},{7,8},{8,7},{9,10},{10,... | collective-permute-start | bytes 442376 | tf_op jit(solution)/shard_map/ppermute | solution.py:568
  73.6 22.3 %collective-permute-start.9 = (f32[12,64,128]{2,1,0:T(8,128)S(1)}, f32[12,64,128]{2,1,0:T(8,128)S(1)}, u32[]{:S(2)}, u32[]{:S(2)}) collective-permute-start(f32[12,64,128]{2,1,0:T(8,128)S(1)} %get-tuple-element.65), channel_id=1, source_target_pairs={{0,480},{32,64},{64,32},{96,128},{128,96},{160,192},{192,160},{224... | collective-permute-start | bytes 1179656 | tf_op jit(solution)/shard_map/ppermute | solution.py:568
  77.0 18.9 %collective-permute-start.8 = (f32[12,64,128]{2,1,0:T(8,128)S(1)}, f32[12,64,128]{2,1,0:T(8,128)S(1)}, u32[]{:S(2)}, u32[]{:S(2)}) collective-permute-start(f32[12,64,128]{2,1,0:T(8,128)S(1)} %get-tuple-element.65), channel_id=1, source_target_pairs={{0,32},{32,0},{64,96},{96,64},{128,160},{160,128},{192,224},{224,1... | collective-permute-start | bytes 1179656 | tf_op jit(solution)/shard_map/ppermute | solution.py:563

commit v4 on v3

--- a/solution.py
+++ b/solution.py
@@ -36,11 +36,11 @@
 SPACES = {"s": pltpu.SMEM, "v": pltpu.VMEM, "h": pltpu.HBM}
 
 
-def kernel(body, ins, outs, cost, scratch=(), limit=32 * 2**20):
+def kernel(body, ins, outs, cost, scratch=(), limit=32 * 2**20, space=pltpu.VMEM):
     return pl.pallas_call(
         body,
         in_specs=[pl.BlockSpec(memory_space=SPACES[kind]) for kind in ins],
-        out_specs=[pl.BlockSpec(memory_space=pltpu.VMEM) for _ in outs],
+        out_specs=[pl.BlockSpec(memory_space=space) for _ in outs],
         out_shape=[jax.ShapeDtypeStruct(shape, dtype) for shape, dtype in outs],
         scratch_shapes=list(scratch),
         compiler_params=pltpu.CompilerParams(vmem_limit_bytes=limit),
@@ -127,7 +127,7 @@
     ref[...] = jnp.where(part < 2, high.astype(f32), low.astype(f32)).astype(bf16)
 
 
-def matrices_body(sizes, tx_ref, ty_ref, spectra_ref, after_ref, gram_ref, my, py, by, mx, px, bx):
+def matrices_body(sizes, tx_ref, ty_ref, spectra_ref, gram_ref, my, py, by, mx, px, bx):
     spectra = spectra_ref[...]
     gram_ref[...] = lax.dot_general(
         spectra, spectra, (((1,), (1,)), ((), ())), precision=lax.Precision.HIGHEST, preferred_element_type=f32
@@ -186,16 +186,11 @@
     return pl.multiple_of(jnp.where(top, 0, ROWS - depth), 16)
 
 
-def pack_x(odd_x, pairing, a_ref, p_ref, out_ref):
-    a_rows = pl.ds(edge_rows(odd_x, pairing, A_HALO), A_HALO)
-    p_rows = pl.ds(edge_rows(odd_x, pairing, P_HALO), P_HALO)
-    for f in range(FLUOR):
-        out_ref[f, :A_HALO, :] = a_ref[f, a_rows, :]
-        out_ref[f, A_HALO:, :] = p_ref[f, p_rows, :]
-
-
-def project_body(s_hbm, a_hbm, m_hbm, p_ref, xb_ref, xa_ref, ya_ref, yb_ref, spectra_ref, a_ref, m_ref, sems):
-    step = 16
+def project_body(
+    s_hbm, a_hbm, m_hbm, p_hbm, xb_hbm, xa_hbm, ya_hbm, yb_hbm,
+    spectra_ref, a_ref, m_ref, p_ref, ya_ref, yb_ref, sems, out_sems,
+):
+    step = 32
     copy_s = pltpu.make_async_copy(s_hbm, spectra_ref, sems.at[5])
     copy_s.start()
     copies = [
@@ -206,6 +201,8 @@
         copy.start()
     copy_a = pltpu.make_async_copy(a_hbm, a_ref, sems.at[ROWS // step])
     copy_a.start()
+    odd_x = index(GX) % 2
+    edges = []
     copy_s.wait()
     for k, copy in enumerate(copies):
         copy.wait()
@@ -217,15 +214,27 @@
                 acc[f] = acc[f] + spectra_ref[f, c] * seen
         for f in range(FLUOR):
             p_ref[f, start : start + step, :] = acc[f]
-    copy_a.wait()
-    odd_x = index(GX) % 2
-    pack_x(odd_x, 1, a_ref, p_ref, xb_ref)
-    pack_x(odd_x, 0, a_ref, p_ref, xa_ref)
+        if k == 0:
+            copy_a.wait()
+            for pairing, x_hbm in ((1, xb_hbm), (0, xa_hbm)):
+                rows = pl.ds(edge_rows(odd_x, pairing, A_HALO), A_HALO)
+                edges.append(
+                    pltpu.make_async_copy(a_ref.at[:, rows, :], x_hbm.at[:, pl.ds(0, A_HALO), :], out_sems.at[pairing])
+                )
+                edges[-1].start()
+    for k, x_hbm in ((1, xb_hbm), (0, xa_hbm)):
+        rows = pl.ds(edge_rows(odd_x, k, P_HALO), P_HALO)
+        edges.append(
+            pltpu.make_async_copy(p_ref.at[:, rows, :], x_hbm.at[:, pl.ds(A_HALO, P_HALO), :], out_sems.at[2 + k])
+        )
+        edges[-1].start()
+    edges.append(pltpu.make_async_copy(p_ref, p_hbm, out_sems.at[4]))
+    edges[-1].start()
     odd_y = index(GY) % 2
     lane = lane_of((32, 128))
     lane8 = lane_of((8, 128))
     for f in range(FLUOR):
-        edges = []
+        sides = []
         for a_from, p_from in ((0, 0), (COLS - A_HALO, COLS - P_HALO)):
             top = roll(a_ref[f, :32, :], -a_from)
             low = roll(a_ref[f, 32:, :], A_HALO - a_from)
@@ -235,12 +244,17 @@
             for k in range(1, 4):
                 piece = roll(p_ref[f, 32 + 8 * k : 40 + 8 * k, :], 32 * k - p_from)
                 rest = jnp.where(lane8 < 32 * k, rest, piece)
-            edges.append((main, rest))
-        (left, left_rest), (right, right_rest) = edges
+            sides.append((main, rest))
+        (left, left_rest), (right, right_rest) = sides
         ya_ref[f, :32, :] = choose(odd_y, left, right)
         yb_ref[f, :32, :] = choose(odd_y, right, left)
         ya_ref[f, 32:, :] = choose(odd_y, left_rest, right_rest)
         yb_ref[f, 32:, :] = choose(odd_y, right_rest, left_rest)
+    for k, (ref, y_hbm) in enumerate(((ya_ref, ya_hbm), (yb_ref, yb_hbm))):
+        edges.append(pltpu.make_async_copy(ref, y_hbm, out_sems.at[5 + k]))
+        edges[-1].start()
+    for copy in edges:
+        copy.wait()
 
 
 def pack_corner(odd_x, pairing, side_ref, ps_ref, out_ref):
@@ -313,13 +327,32 @@
 
 def mix(gram_ref, v_ref, d_ref, g_ref):
     step = 8
+
+    def mixed(part, f):
+        acc = gram_ref[f, 0] * part[0]
+        for k in range(1, FLUOR):
+            acc = acc + gram_ref[f, k] * part[k]
+        return acc
+
     for start in range(0, G_ROWS, step):
-        part = [v_ref[f, start : start + step, :] for f in range(FLUOR)]
+        part = [v_ref[f, start : start + step, :COLS] for f in range(FLUOR)]
         for f in range(FLUOR):
-            acc = -d_ref[f, start : start + step, :]
-            for k in range(FLUOR):
-                acc = acc + gram_ref[f, k] * part[k]
-            g_ref[f, start : start + step, :] = acc
+            g_ref[f, start : start + step, :COLS] = mixed(part, f) - d_ref[f, start : start + step, :COLS]
+    lane = lane_of((step, 128))
+    group = G_ROWS // 4
+    for start in range(0, group, step):
+        rows = [slice(k * group + start, k * group + start + step) for k in range(4)]
+        part = []
+        for f in range(FLUOR):
+            packed = v_ref[f, rows[0], COLS:]
+            for k in range(1, 4):
+                packed = packed + roll(v_ref[f, rows[k], COLS:], 32 * k)
+            part.append(packed)
+        for f in range(FLUOR):
+            out = mixed(part, f)
+            for k in range(4):
+                side = jnp.where(lane < 2 * G_HALO, roll(out, -32 * k), 0.0)
+                g_ref[f, rows[k], COLS:] = side - d_ref[f, rows[k], COLS:]
 
 
 def sums(gram_ref, g_ref, by, bx, y_ref, z_ref, sum_ref):
@@ -587,9 +620,14 @@
             pltpu.SMEM((FLUOR, CHAN), f32),
             pltpu.VMEM(TILE, f32),
             pltpu.VMEM((CHAN, ROWS, COLS), bf16),
+            pltpu.VMEM(TILE, f32),
+            pltpu.VMEM((FLUOR, 40, 128), f32),
+            pltpu.VMEM((FLUOR, 40, 128), f32),
             pltpu.SemaphoreType.DMA((6,)),
+            pltpu.SemaphoreType.DMA((7,)),
         ],
         60_000_000,
+        pltpu.HBM,
     )(spectra.T, a0, measured[0])
     za, zb = trade(xa, xb, GX)
     ya, yb = trade(ya, yb, GY)
@@ -598,11 +636,11 @@
     ca, cb = trade(ca, cb, GX)
     gram, my, py, by, mx, px, bx = kernel(
         functools.partial(matrices_body, sizes),
-        "ssvv",
+        "ssv",
         [((FLUOR, FLUOR), f32)] + [((768, 256), bf16)] * 2 + [((768, 128), bf16)]
         + [((G_ROWS, 512), bf16), ((G_ROWS, 384), bf16), ((ROWS, 384), bf16)],
         10**9,
-    )(taps_x, taps_y, spectra.T, ps)
+    )(taps_x, taps_y, spectra.T)
     halves = kernel(
         own_body,
         "v" * 8,

time: 130 us -> 128 us (0.985)
  local copies, waits for them, and re-layouts: 0.02 us -> 2.01 us
  waiting for transfers between devices: 7.17 us -> 5.86 us
    unnamed x10, local copies, waits for them, and re-layouts: 0.02 us -> 2.01 us
    ppermute x5, waiting for transfers between devices: 7.15 us -> 5.85 us  [trade_second(): lax.ppermute(edge, axes, [(i, (i + (1 if i % 2 else -1)) % count) for i i...]
  transfers between devices with their start and end apart: 10 -> 10, of which waited for: 2 -> 1; matrix products, arithmetic and copies ran while one was open for 0% -> 0% of each run, Pallas kernels for 7% -> 7%
where the time goes in v4:
time: 128 us; the launch traced here: 127 us
  blocking collectives  56.9 us (44%)
  starting transfers between devices  42.2 us (33%)
  Pallas kernels  20.2 us (16%)
  waiting for transfers between devices  5.86 us (5%)
  local copies, waits for them, and re-layouts  2.01 us (2%)
    all_to_all x4, blocking collectives, spread(): lax.all_to_all(rows.reshape(rows.shape[0], 1, 128), axes, 0, 0, tiled=True)  56.9 us
    ppermute x5, starting transfers between devices, trade_second(): lax.ppermute(edge, axes, [(i, (i + (1 if i % 2 else -1)) % count) for i i...  27.7 us
    ppermute x5, starting transfers between devices, trade_first(): return lax.ppermute(edge, axes, [(i, i ^ 1) for i in range(length(axes))])  14.6 us
    ppermute x5, waiting for transfers between devices, trade_second(): lax.ppermute(edge, axes, [(i, (i + (1 if i % 2 else -1)) % count) for i i...  5.85 us
    pallas_call x1, Pallas kernels, local(): kernel(functools.partial(matrices_body, sizes), 'ssv', [((FLUOR, FLUOR),...  5.03 us
    pallas_call x1, Pallas kernels, local(): second_call(gram, total, a0, side, za, zb, ca, cb, d, g, g_side, xa, xb,...  3.92 us
    pallas_call x1, Pallas kernels, local(): d, g, ya, yb = first_call(gram, *halves, cb, ca, my, py, mx, px)  3.16 us
    pallas_call x1, Pallas kernels, local(): kernel(project_body, 'hhh', [(TILE, f32)] + [(edge, f32)] * 2 + [((FLUOR,...  3.14 us
  transfers between devices with their start and end apart: 10, of which 1 were waited for; matrix products, arithmetic and copies ran while one was open for 0% of the time, Pallas kernels for 7%

profile of v4, /device:TPU:1, one launch (start us, length us, event | category | flops | bytes accessed | tf_op | source)
XLA Modules:
  0.0 127.4 jit_solution(3910311244556995998)
XLA Ops:
  0.0 3.1 %shard_map.56 = (f32[12,64,128]{2,1,0:T(8,128)}, f32[12,80,128]{2,1,0:T(8,128)}, f32[12,80,128]{2,1,0:T(8,128)}, f32[12,40,128]{2,1,0:T(8,128)}, f32[12,40,128]{2,1,0:T(8,128)}) custom-call(f32[12,32]{1,0:T(8,128)} %bitcast.30, f32[12,64,128]{2,1,0:T(8,128)} %bitcast.20, bf16[32,64,128]{2,1,0:T(8,128)(2,1)} %bitcast.33), custom_call_target="tpu_custom_call" | custom-call | flops 10000000 | bytes 100000 | tf_op jit(solution)/shard_map/pallas_call | solution.py:614
  3.1 6.0 %collective-permute-start.2 = (f32[12,80,128]{2,1,0:T(8,128)}, f32[12,80,128]{2,1,0:T(8,128)S(1)}, u32[]{:S(2)}, u32[]{:S(2)}) collective-permute-start(f32[12,80,128]{2,1,0:T(8,128)} %get-tuple-element.43), channel_id=1, source_target_pairs={{0,480},{32,64},{64,32},{96,128},{128,96},{160,192},{192,160},{224... | collective-permute-start | bytes 1474568 | tf_op jit(solution)/shard_map/ppermute | solution.py:601
  9.2 4.7 %collective-permute-start.3 = (f32[12,80,128]{2,1,0:T(8,128)}, f32[12,80,128]{2,1,0:T(8,128)S(1)}, u32[]{:S(2)}, u32[]{:S(2)}) collective-permute-start(f32[12,80,128]{2,1,0:T(8,128)} %get-tuple-element.44), channel_id=1, source_target_pairs={{0,32},{32,0},{64,96},{96,64},{128,160},{160,128},{192,224},{224,1... | collective-permute-start | bytes 1474568 | tf_op jit(solution)/shard_map/ppermute | solution.py:596
  13.9 3.1 %collective-permute-start = (f32[12,40,128]{2,1,0:T(8,128)}, f32[12,40,128]{2,1,0:T(8,128)S(1)}, u32[]{:S(2)}, u32[]{:S(2)}) collective-permute-start(f32[12,40,128]{2,1,0:T(8,128)} %get-tuple-element.38), channel_id=1, source_target_pairs={{0,1},{1,0},{2,3},{3,2},{4,5},{5,4},{6,7},{7,6},{8,9},{9,8},{10,11... | collective-permute-start | bytes 737288 | tf_op jit(solution)/shard_map/ppermute | solution.py:596
  16.9 0.0 copy-start
  17.0 10.4 %collective-permute-start.1 = (f32[12,40,128]{2,1,0:T(8,128)}, f32[12,40,128]{2,1,0:T(8,128)S(1)}, u32[]{:S(2)}, u32[]{:S(2)}) collective-permute-start(f32[12,40,128]{2,1,0:T(8,128)} %get-tuple-element.39), channel_id=1, source_target_pairs={{0,31},{1,2},{2,1},{3,4},{4,3},{5,6},{6,5},{7,8},{8,7},{9,10},{10,... | collective-permute-start | bytes 737288 | tf_op jit(solution)/shard_map/ppermute | solution.py:601
  27.3 0.0 copy-start.1
  27.4 0.7 copy-done.1
  28.0 0.0 copy-start.3
  28.0 0.7 copy-done.3
  28.7 0.0 copy-start.4
  28.7 0.7 copy-done.4
  29.4 0.0 copy-start.2
  29.4 5.0 %shard_map.55 = (f32[12,12]{1,0:T(8,128)S(1)}, bf16[768,256]{1,0:T(8,128)(2,1)S(1)}, bf16[768,256]{1,0:T(8,128)(2,1)S(1)}, bf16[768,128]{1,0:T(8,128)(2,1)S(1)},...) custom-call(f32[33]{0:T(128)S(1)} %copy-done.3, f32[33]{0:T(128)S(1)} %copy-done.4, ...), custom_call_target="tpu_custom_call" | custom-call | flops 1000000000 | bytes 10000000 | tf_op jit(solution)/shard_map/pallas_call | solution.py:637
  34.4 0.0 collective-permute-done.ya_ref
  34.4 0.0 collective-permute-done.1.yb_ref
  34.4 0.5 shard_map.57
  34.9 3.3 %collective-permute-start.4 = (f32[12,56,128]{2,1,0:T(8,128)S(1)}, f32[12,56,128]{2,1,0:T(8,128)S(1)}, u32[]{:S(2)}, u32[]{:S(2)}) collective-permute-start(f32[12,56,128]{2,1,0:T(8,128)S(1)} %get-tuple-element.53), channel_id=1, source_target_pairs={{0,480},{32,64},{64,32},{96,128},{128,96},{160,192},{192,160},{224... | collective-permute-start | bytes 1032200 | tf_op jit(solution)/shard_map/ppermute | solution.py:601
  38.3 2.6 %collective-permute-start.5 = (f32[12,56,128]{2,1,0:T(8,128)S(1)}, f32[12,56,128]{2,1,0:T(8,128)S(1)}, u32[]{:S(2)}, u32[]{:S(2)}) collective-permute-start(f32[12,56,128]{2,1,0:T(8,128)S(1)} %get-tuple-element.54), channel_id=1, source_target_pairs={{0,32},{32,0},{64,96},{96,64},{128,160},{160,128},{192,224},{224,1... | collective-permute-start | bytes 1032200 | tf_op jit(solution)/shard_map/ppermute | solution.py:596
  40.9 0.0 collective-permute-done.2.xb_ref.zb_ref
  40.9 0.0 collective-permute-done.3.xa_ref.za_ref
  40.9 0.0 copy-done
  40.9 0.0 copy-done.2
  40.9 1.3 %shard_map.58 = (f32[12,64,256]{2,1,0:T(8,128)S(1)}, f32[12,64,256]{2,1,0:T(8,128)S(1)}, f32[12,48,256]{2,1,0:T(8,128)S(1)}, f32[12,48,256]{2,1,0:T(8,128)S(1)},...) custom-call(f32[12,64,128]{2,1,0:T(8,128)S(1)} %bitcast.21, f32[12,64,128]{2,1,0:T(8,128)S(1)} %get-tuple-element.40.side_ref, ...), custom_call_target="tpu_custom_call" | custom-call | flops 10000000000 | bytes 100000000 | tf_op jit(solution)/shard_map/pallas_call | solution.py:644
  42.3 5.8 %collective-permute-done.4.cb_ref = f32[12,56,128]{2,1,0:T(8,128)S(1)} collective-permute-done((f32[12,56,128]{2,1,0:T(8,128)S(1)}, f32[12,56,128]{2,1,0:T(8,128)S(1)}, u32[]{:S(2)}, u32[]{:S(2)}) %collective-permute-start.4) | collective-permute-done | bytes 344096 | tf_op jit(solution)/shard_map/ppermute | solution.py:601
  48.1 0.0 collective-permute-done.5.ca_ref
  48.1 3.2 %shard_map.59 = (f32[12,96,256]{2,1,0:T(8,128)S(1)}, f32[12,96,256]{2,1,0:T(8,128)S(1)}, f32[12,24,128]{2,1,0:T(8,128)S(1)}, f32[12,24,128]{2,1,0:T(8,128)S(1)}) custom-call(f32[12,12]{1,0:T(8,128)S(1)} %get-tuple-element.37.gram_ref, f32[12,64,256]{2,1,0:T(8,128)S(1)} %get-tuple-element.47.u_ref, f32[12,64,256]{2,1,0:T(8,128)S(1)} %get-tuple-element.48.w_ref, ...), custom_call_target="tpu_custom_call" | custom-call | flops 1000000000 | bytes 10000000 | tf_op jit(solution)/shard_map/pallas_call | solution.py:650
  51.3 1.9 %collective-permute-start.6 = (f32[12,24,128]{2,1,0:T(8,128)S(1)}, f32[12,24,128]{2,1,0:T(8,128)S(1)}, u32[]{:S(2)}, u32[]{:S(2)}) collective-permute-start(f32[12,24,128]{2,1,0:T(8,128)S(1)} %get-tuple-element.60), channel_id=1, source_target_pairs={{0,1},{1,0},{2,3},{3,2},{4,5},{5,4},{6,7},{7,6},{8,9},{9,8},{10,11... | collective-permute-start | bytes 442376 | tf_op jit(solution)/shard_map/ppermute | solution.py:596
  53.2 4.5 %collective-permute-start.7 = (f32[12,24,128]{2,1,0:T(8,128)S(1)}, f32[12,24,128]{2,1,0:T(8,128)S(1)}, u32[]{:S(2)}, u32[]{:S(2)}) collective-permute-start(f32[12,24,128]{2,1,0:T(8,128)S(1)} %get-tuple-element.61), channel_id=1, source_target_pairs={{0,31},{1,2},{2,1},{3,4},{4,3},{5,6},{6,5},{7,8},{8,7},{9,10},{10,... | collective-permute-start | bytes 442376 | tf_op jit(solution)/shard_map/ppermute | solution.py:601
  57.7 1.7 %shard_map.60 = f32[32,128]{1,0:T(8,128)S(1)} custom-call(f32[12,12]{1,0:T(8,128)S(1)} %get-tuple-element.37.gram_ref, f32[12,96,256]{2,1,0:T(8,128)S(1)} %get-tuple-element.57.g_ref, bf16[768,128]{1,0:T(8,128)(2,1)S(1)} %get-tuple-element.58.by, bf16[64,384]{1,0:T(8,128)(2,1)S(1)} %get-tuple-element.59.bx), custom_call_target="tpu_custom_call" | custom-call | flops 1000000000 | bytes 10000000 | tf_op jit(solution)/shard_map/pallas_call | solution.py:652
  59.5 12.2 %all_to_all.20 = f32[32,1,128]{2,1,0:T(1,128)S(1)} all-to-all(f32[32,1,128]{2,1,0:T(1,128)S(1)} %bitcast.29), channel_id=1, replica_groups=mesh['y'=4,'x_hi'=2,'core'=2,'x_lo'=2,'z'=16] {'y','x_hi','core','x_lo'}, dimensions={0} | all-to-all | bytes 32768 | tf_op jit(solution)/shard_map/all_to_all | solution.py:605
  71.7 0.0 collective-permute-done.6.ya_ref
  71.7 0.0 collective-permute-done.7.yb_ref
  71.7 0.5 shard_map.61
  72.2 3.4 %collective-permute-start.9 = (f32[12,64,128]{2,1,0:T(8,128)S(1)}, f32[12,64,128]{2,1,0:T(8,128)S(1)}, u32[]{:S(2)}, u32[]{:S(2)}) collective-permute-start(f32[12,64,128]{2,1,0:T(8,128)S(1)} %get-tuple-element.65), channel_id=1, source_target_pairs={{0,480},{32,64},{64,32},{96,128},{128,96},{160,192},{192,160},{224... | collective-permute-start | bytes 1179656 | tf_op jit(solution)/shard_map/ppermute | solution.py:601
  75.6 2.3 %collective-permute-start.8 = (f32[12,64,128]{2,1,0:T(8,128)S(1)}, f32[12,64,128]{2,1,0:T(8,128)S(1)}, u32[]{:S(2)}, u32[]{:S(2)}) collective-permute-start(f32[12,64,128]{2,1,0:T(8,128)S(1)} %get-tuple-element.65), channel_id=1, source_target_pairs={{0,32},{32,0},{64,96},{96,64},{128,160},{160,128},{192,224},{224,1... | collective-permute-start | bytes 1179656 | tf_op jit(solution)/shard_map/ppermute | solution.py:596
  77.9 16.7 %all_to_all.21 = f32[16,1,128]{2,1,0:T(1,128)S(1)} all-to-all(f32[16,1,128]{2,1,0:T(1,128)S(1)} %bitcast.32), channel_id=1, replica_groups=mesh['y'=4,'x_hi'=2,'core'=2,'x_lo'=2,'z'=16] {'z'}, dimensions={0} | all-to-all | bytes 16384 | tf_op jit(solution)/shard_map/all_to_all | solution.py:605
  94.6 0.0 collective-permute-done.9.xb_ref
  94.6 0.0 collective-permute-done.8.xa_ref
  94.6 3.9 %shard_map.62 = (f32[12,64,128]{2,1,0:T(8,128)S(1)}, f32[12,64,128]{2,1,0:T(8,128)S(1)}, f32[32,128]{1,0:T(8,128)S(1)}) custom-call(f32[12,12]{1,0:T(8,128)S(1)} %get-tuple-element.37.gram_ref, f32[16,128]{1,0:T(8,128)S(1)} %bitcast.25, f32[12,64,128]{2,1,0:T(8,128)S(1)} %bitcast.22, f32[12,64,128]{2,1,0:T(8,128)S(1)} %get-tuple-element.40.side_ref, ...), custom_call_target="tpu_custom_call" | custom-call | flops 1000000000 | bytes 10000000 | tf_op jit(solution)/shard_map/pallas_call | solution.py:662
  98.6 14.1 %all_to_all.22 = f32[32,1,128]{2,1,0:T(1,128)S(1)} all-to-all(f32[32,1,128]{2,1,0:T(1,128)S(1)} %bitcast.28), channel_id=1, replica_groups=mesh['y'=4,'x_hi'=2,'core'=2,'x_lo'=2,'z'=16] {'y','x_hi','core','x_lo'}, dimensions={0} | all-to-all | bytes 32768 | tf_op jit(solution)/shard_map/all_to_all | solution.py:605
  112.7 13.8 %all_to_all.23 = f32[16,1,128]{2,1,0:T(1,128)S(1)} all-to-all(f32[16,1,128]{2,1,0:T(1,128)S(1)} %bitcast.27), channel_id=1, replica_groups=mesh['y'=4,'x_hi'=2,'core'=2,'x_lo'=2,'z'=16] {'z'}, dimensions={0} | all-to-all | bytes 16384 | tf_op jit(solution)/shard_map/all_to_all | solution.py:605
  126.5 0.9 shard_map.64
  (1 shorter events, 0.0 us)
Async XLA Ops:
  3.1 37.8 %collective-permute-start.2 = (f32[12,80,128]{2,1,0:T(8,128)}, f32[12,80,128]{2,1,0:T(8,128)S(1)}, u32[]{:S(2)}, u32[]{:S(2)}) collective-permute-start(f32[12,80,128]{2,1,0:T(8,128)} %get-tuple-element.43), channel_id=1, source_target_pairs={{0,480},{32,64},{64,32},{96,128},{128,96},{160,192},{192,160},{224... | collective-permute-start | bytes 1474568 | tf_op jit(solution)/shard_map/ppermute | solution.py:601
  9.2 31.7 %collective-permute-start.3 = (f32[12,80,128]{2,1,0:T(8,128)}, f32[12,80,128]{2,1,0:T(8,128)S(1)}, u32[]{:S(2)}, u32[]{:S(2)}) collective-permute-start(f32[12,80,128]{2,1,0:T(8,128)} %get-tuple-element.44), channel_id=1, source_target_pairs={{0,32},{32,0},{64,96},{96,64},{128,160},{160,128},{192,224},{224,1... | collective-permute-start | bytes 1474568 | tf_op jit(solution)/shard_map/ppermute | solution.py:596
  13.9 20.5 %collective-permute-start = (f32[12,40,128]{2,1,0:T(8,128)}, f32[12,40,128]{2,1,0:T(8,128)S(1)}, u32[]{:S(2)}, u32[]{:S(2)}) collective-permute-start(f32[12,40,128]{2,1,0:T(8,128)} %get-tuple-element.38), channel_id=1, source_target_pairs={{0,1},{1,0},{2,3},{3,2},{4,5},{5,4},{6,7},{7,6},{8,9},{9,8},{10,11... | collective-permute-start | bytes 737288 | tf_op jit(solution)/shard_map/ppermute | solution.py:596
  16.9 24.0 %copy-start = (f32[1,12,64,128]{3,2,1,0:T(8,128)S(1)}, f32[1,12,64,128]{3,2,1,0:T(8,128)}, u32[]{:S(2)}) copy-start(f32[1,12,64,128]{3,2,1,0:T(8,128)} %param.5) | copy-start | bytes 1179652
  17.0 17.4 %collective-permute-start.1 = (f32[12,40,128]{2,1,0:T(8,128)}, f32[12,40,128]{2,1,0:T(8,128)S(1)}, u32[]{:S(2)}, u32[]{:S(2)}) collective-permute-start(f32[12,40,128]{2,1,0:T(8,128)} %get-tuple-element.39), channel_id=1, source_target_pairs={{0,31},{1,2},{2,1},{3,4},{4,3},{5,6},{6,5},{7,8},{8,7},{9,10},{10,... | collective-permute-start | bytes 737288 | tf_op jit(solution)/shard_map/ppermute | solution.py:601
  27.3 0.7 copy-start.1
  28.0 0.7 copy-start.3
  28.7 0.7 copy-start.4
  29.4 11.6 %copy-start.2 = (f32[12,64,128]{2,1,0:T(8,128)S(1)}, f32[12,64,128]{2,1,0:T(8,128)}, u32[]{:S(2)}) copy-start(f32[12,64,128]{2,1,0:T(8,128)} %get-tuple-element.41.p_ref) | copy-start | bytes 1179652
  34.9 13.2 %collective-permute-start.4 = (f32[12,56,128]{2,1,0:T(8,128)S(1)}, f32[12,56,128]{2,1,0:T(8,128)S(1)}, u32[]{:S(2)}, u32[]{:S(2)}) collective-permute-start(f32[12,56,128]{2,1,0:T(8,128)S(1)} %get-tuple-element.53), channel_id=1, source_target_pairs={{0,480},{32,64},{64,32},{96,128},{128,96},{160,192},{192,160},{224... | collective-permute-start | bytes 1032200 | tf_op jit(solution)/shard_map/ppermute | solution.py:601
  38.3 9.8 %collective-permute-start.5 = (f32[12,56,128]{2,1,0:T(8,128)S(1)}, f32[12,56,128]{2,1,0:T(8,128)S(1)}, u32[]{:S(2)}, u32[]{:S(2)}) collective-permute-start(f32[12,56,128]{2,1,0:T(8,128)S(1)} %get-tuple-element.54), channel_id=1, source_target_pairs={{0,32},{32,0},{64,96},{96,64},{128,160},{160,128},{192,224},{224,1... | collective-permute-start | bytes 1032200 | tf_op jit(solution)/shard_map/ppermute | solution.py:596
  51.3 20.4 %collective-permute-start.6 = (f32[12,24,128]{2,1,0:T(8,128)S(1)}, f32[12,24,128]{2,1,0:T(8,128)S(1)}, u32[]{:S(2)}, u32[]{:S(2)}) collective-permute-start(f32[12,24,128]{2,1,0:T(8,128)S(1)} %get-tuple-element.60), channel_id=1, source_target_pairs={{0,1},{1,0},{2,3},{3,2},{4,5},{5,4},{6,7},{7,6},{8,9},{9,8},{10,11... | collective-permute-start | bytes 442376 | tf_op jit(solution)/shard_map/ppermute | solution.py:596
  53.2 18.5 %collective-permute-start.7 = (f32[12,24,128]{2,1,0:T(8,128)S(1)}, f32[12,24,128]{2,1,0:T(8,128)S(1)}, u32[]{:S(2)}, u32[]{:S(2)}) collective-permute-start(f32[12,24,128]{2,1,0:T(8,128)S(1)} %get-tuple-element.61), channel_id=1, source_target_pairs={{0,31},{1,2},{2,1},{3,4},{4,3},{5,6},{6,5},{7,8},{8,7},{9,10},{10,... | collective-permute-start | bytes 442376 | tf_op jit(solution)/shard_map/ppermute | solution.py:601
  72.2 22.4 %collective-permute-start.9 = (f32[12,64,128]{2,1,0:T(8,128)S(1)}, f32[12,64,128]{2,1,0:T(8,128)S(1)}, u32[]{:S(2)}, u32[]{:S(2)}) collective-permute-start(f32[12,64,128]{2,1,0:T(8,128)S(1)} %get-tuple-element.65), channel_id=1, source_target_pairs={{0,480},{32,64},{64,32},{96,128},{128,96},{160,192},{192,160},{224... | collective-permute-start | bytes 1179656 | tf_op jit(solution)/shard_map/ppermute | solution.py:601
  75.6 19.0 %collective-permute-start.8 = (f32[12,64,128]{2,1,0:T(8,128)S(1)}, f32[12,64,128]{2,1,0:T(8,128)S(1)}, u32[]{:S(2)}, u32[]{:S(2)}) collective-permute-start(f32[12,64,128]{2,1,0:T(8,128)S(1)} %get-tuple-element.65), channel_id=1, source_target_pairs={{0,32},{32,0},{64,96},{96,64},{128,160},{160,128},{192,224},{224,1... | collective-permute-start | bytes 1179656 | tf_op jit(solution)/shard_map/ppermute | solution.py:596

commit v5 on v4

--- a/solution.py
+++ b/solution.py
@@ -127,13 +127,7 @@
     ref[...] = jnp.where(part < 2, high.astype(f32), low.astype(f32)).astype(bf16)
 
 
-def matrices_body(sizes, tx_ref, ty_ref, spectra_ref, gram_ref, my, py, by, mx, px, bx):
-    spectra = spectra_ref[...]
-    gram_ref[...] = lax.dot_general(
-        spectra, spectra, (((1,), (1,)), ((), ())), precision=lax.Precision.HIGHEST, preferred_element_type=f32
-    )
-    size_x, size_y = sizes
-    base_x = index(GX) * ROWS
+def y_matrices_body(size_y, ty_ref, my, py, by):
     base_y = index(GY) * COLS
     r, c = rows_cols((256, 256))
     source = side_position(r, P_HALO)
@@ -151,6 +145,14 @@
     source = side_position(r, G_HALO)
     okay = inside(source, base_y, size_y)
     put_right(jnp.where(okay, tap_matrix(ty_ref, source - c + HALF), 0.0), by)
+
+
+def x_matrices_body(size_x, tx_ref, spectra_ref, after_ref, gram_ref, mx, px, bx):
+    spectra = spectra_ref[...]
+    gram_ref[...] = lax.dot_general(
+        spectra, spectra, (((1,), (1,)), ((), ())), precision=lax.Precision.HIGHEST, preferred_element_type=f32
+    )
+    base_x = index(GX) * ROWS
     r, c = rows_cols((128, 512))
     part = c // A_ROWS
     source = c - part * A_ROWS - A_HALO
@@ -406,15 +408,16 @@
     return put
 
 
-def own_body(
-    a_ref, side_ref, p_ref, ps_ref, xb_ref, xa_ref, my, py, u_ref, w_ref, ua_ref, ub_ref, wa_ref, wb_ref
-):
+def own_body(a_ref, side_ref, p_ref, ps_ref, xb_ref, my, py, u_ref, w_ref, ub_ref, wb_ref):
     along_y(lambda part: wide(p_ref[part], ps_ref[part]), py[...], store(w_ref))
     along_y(lambda part: wide(a_ref[part], side_ref[part]), my[...], store(u_ref))
+    along_half(lambda part: xb_ref[part, :A_HALO, :], my, 0, store(ub_ref))
+    along_half(lambda part: xb_ref[part, A_HALO:, :], py, 0, store(wb_ref))
+
+
+def first_rows_body(xa_ref, my, py, ua_ref, wa_ref):
     along_half(lambda part: xa_ref[part, :A_HALO, :], my, 0, store(ua_ref))
-    along_half(lambda part: xb_ref[part, :A_HALO, :], my, 0, store(ub_ref))
     along_half(lambda part: xa_ref[part, A_HALO:, :], py, 0, store(wa_ref))
-    along_half(lambda part: xb_ref[part, A_HALO:, :], py, 0, store(wb_ref))
 
 
 def first_body(
@@ -631,23 +634,29 @@
     )(spectra.T, a0, measured[0])
     za, zb = trade(xa, xb, GX)
     ya, yb = trade(ya, yb, GY)
+    my, py, by = kernel(
+        functools.partial(y_matrices_body, sizes[1]),
+        "s",
+        [((768, 256), bf16)] * 2 + [((768, 128), bf16)],
+        10**9,
+    )(taps_y)
     corner = (FLUOR, 56, 128)
     side, ps, cb, ca = kernel(corner_body, "vv", [(TILE, f32)] * 2 + [(corner, f32)] * 2, 10**7)(ya, yb)
     ca, cb = trade(ca, cb, GX)
-    gram, my, py, by, mx, px, bx = kernel(
-        functools.partial(matrices_body, sizes),
-        "ssv",
-        [((FLUOR, FLUOR), f32)] + [((768, 256), bf16)] * 2 + [((768, 128), bf16)]
-        + [((G_ROWS, 512), bf16), ((G_ROWS, 384), bf16), ((ROWS, 384), bf16)],
+    gram, mx, px, bx = kernel(
+        functools.partial(x_matrices_body, sizes[0]),
+        "svv",
+        [((FLUOR, FLUOR), f32), ((G_ROWS, 512), bf16), ((G_ROWS, 384), bf16), ((ROWS, 384), bf16)],
         10**9,
-    )(taps_x, taps_y, spectra.T)
-    halves = kernel(
+    )(taps_x, spectra.T, ps)
+    u, w, ub, wb = kernel(
         own_body,
-        "v" * 8,
-        [((FLUOR, rows, 256), f32) for rows in (ROWS, ROWS, A_HALO, A_HALO, P_HALO, P_HALO)],
+        "v" * 7,
+        [((FLUOR, rows, 256), f32) for rows in (ROWS, ROWS, A_HALO, P_HALO)],
         OWN_COST,
-    )(a0, side, p, ps, zb, za, my, py)
-    d, g, ya, yb = first_call(gram, *halves, cb, ca, my, py, mx, px)
+    )(a0, side, p, ps, zb, my, py)
+    ua, wa = kernel(first_rows_body, "vvv", [((FLUOR, rows, 256), f32) for rows in (A_HALO, P_HALO)], 10**7)(za, my, py)
+    d, g, ya, yb = first_call(gram, u, w, ua, ub, wa, wb, cb, ca, my, py, mx, px)
     ya, yb = trade(ya, yb, GY)
     (partial,) = probe_call(gram, g, by, bx)
     near = spread(partial, NEAR)

time: 128 us -> 126 us (0.984)
  waiting for transfers between devices: 5.86 us -> 3 us
  blocking collectives: 56.9 us -> 58.4 us
  local copies, waits for them, and re-layouts: 2.01 us -> 0.67 us
    ppermute x5, waiting for transfers between devices: 5.85 us -> 2.99 us  [trade_second(): lax.ppermute(edge, axes, [(i, (i + (1 if i % 2 else -1)) % count) for i i...]
    ppermute x5, starting transfers between devices: 14.6 us -> 16.2 us  [trade_first(): return lax.ppermute(edge, axes, [(i, i ^ 1) for i in range(length(axes))])]
    ppermute x5, starting transfers between devices: 27.7 us -> 26 us  [trade_second(): lax.ppermute(edge, axes, [(i, (i + (1 if i % 2 else -1)) % count) for i i...]
    all_to_all x4, blocking collectives: 56.9 us -> 58.4 us  [spread(): lax.all_to_all(rows.reshape(rows.shape[0], 1, 128), axes, 0, 0, tiled=True)]
    unnamed x10, local copies, waits for them, and re-layouts: 2.01 us -> 0.67 us
    pallas_call x3 -> x5, Pallas kernels: 9.51 us -> 10.1 us  [the longest x1 3.14 us: local(): first_call(gram, u, w, ua, ub, wa, wb, cb, ca, my, py, mx, px)]
where the time goes in v5:
time: 126 us; the launch traced here: 125 us
  blocking collectives  58.4 us (46%)
  starting transfers between devices  42.3 us (34%)
  Pallas kernels  20.8 us (17%)
  waiting for transfers between devices  3 us (2%)
    all_to_all x4, blocking collectives, spread(): lax.all_to_all(rows.reshape(rows.shape[0], 1, 128), axes, 0, 0, tiled=True)  58.4 us
    ppermute x5, starting transfers between devices, trade_second(): lax.ppermute(edge, axes, [(i, (i + (1 if i % 2 else -1)) % count) for i i...  26 us
    ppermute x5, starting transfers between devices, trade_first(): return lax.ppermute(edge, axes, [(i, i ^ 1) for i in range(length(axes))])  16.2 us
    pallas_call x1, Pallas kernels, local(): second_call(gram, total, a0, side, za, zb, ca, cb, d, g, g_side, xa, xb,...  3.92 us
    pallas_call x1, Pallas kernels, local(): first_call(gram, u, w, ua, ub, wa, wb, cb, ca, my, py, mx, px)  3.14 us
    pallas_call x1, Pallas kernels, local(): kernel(project_body, 'hhh', [(TILE, f32)] + [(edge, f32)] * 2 + [((FLUOR,...  3.14 us
    ppermute x5, waiting for transfers between devices, trade_second(): lax.ppermute(edge, axes, [(i, (i + (1 if i % 2 else -1)) % count) for i i...  2.99 us
    pallas_call x1, Pallas kernels, local(): kernel(functools.partial(y_matrices_body, sizes[1]), 's', [((768, 256), b...  2.76 us
  transfers between devices with their start and end apart: 10, of which 1 were waited for; matrix products, arithmetic and copies ran while one was open for 0% of the time, Pallas kernels for 7%

profile of v5, /device:TPU:1, one launch (start us, length us, event | category | flops | bytes accessed | tf_op | source)
XLA Modules:
  0.0 125.4 jit_solution(13376507123588486598)
XLA Ops:
  0.0 3.1 %shard_map.55 = (f32[12,64,128]{2,1,0:T(8,128)}, f32[12,80,128]{2,1,0:T(8,128)}, f32[12,80,128]{2,1,0:T(8,128)}, f32[12,40,128]{2,1,0:T(8,128)}, f32[12,40,128]{2,1,0:T(8,128)}) custom-call(f32[12,32]{1,0:T(8,128)} %bitcast.30, f32[12,64,128]{2,1,0:T(8,128)} %bitcast.20, bf16[32,64,128]{2,1,0:T(8,128)(2,1)} %bitcast.33), custom_call_target="tpu_custom_call" | custom-call | flops 10000000 | bytes 100000 | tf_op jit(solution)/shard_map/pallas_call | solution.py:617
  3.1 6.0 %collective-permute-start.2 = (f32[12,80,128]{2,1,0:T(8,128)}, f32[12,80,128]{2,1,0:T(8,128)S(1)}, u32[]{:S(2)}, u32[]{:S(2)}) collective-permute-start(f32[12,80,128]{2,1,0:T(8,128)} %get-tuple-element.43), channel_id=1, source_target_pairs={{0,480},{32,64},{64,32},{96,128},{128,96},{160,192},{192,160},{224... | collective-permute-start | bytes 1474568 | tf_op jit(solution)/shard_map/ppermute | solution.py:604
  9.2 3.5 %collective-permute-start = (f32[12,40,128]{2,1,0:T(8,128)}, f32[12,40,128]{2,1,0:T(8,128)S(1)}, u32[]{:S(2)}, u32[]{:S(2)}) collective-permute-start(f32[12,40,128]{2,1,0:T(8,128)} %get-tuple-element.37), channel_id=1, source_target_pairs={{0,1},{1,0},{2,3},{3,2},{4,5},{5,4},{6,7},{7,6},{8,9},{9,8},{10,11... | collective-permute-start | bytes 737288 | tf_op jit(solution)/shard_map/ppermute | solution.py:599
  12.7 10.2 %collective-permute-start.1 = (f32[12,40,128]{2,1,0:T(8,128)}, f32[12,40,128]{2,1,0:T(8,128)S(1)}, u32[]{:S(2)}, u32[]{:S(2)}) collective-permute-start(f32[12,40,128]{2,1,0:T(8,128)} %get-tuple-element.38), channel_id=1, source_target_pairs={{0,31},{1,2},{2,1},{3,4},{4,3},{5,6},{6,5},{7,8},{8,7},{9,10},{10,... | collective-permute-start | bytes 737288 | tf_op jit(solution)/shard_map/ppermute | solution.py:604
  23.0 0.0 copy-start.1
  23.0 4.8 %collective-permute-start.3 = (f32[12,80,128]{2,1,0:T(8,128)}, f32[12,80,128]{2,1,0:T(8,128)S(1)}, u32[]{:S(2)}, u32[]{:S(2)}) collective-permute-start(f32[12,80,128]{2,1,0:T(8,128)} %get-tuple-element.48), channel_id=1, source_target_pairs={{0,32},{32,0},{64,96},{96,64},{128,160},{160,128},{192,224},{224,1... | collective-permute-start | bytes 1474568 | tf_op jit(solution)/shard_map/ppermute | solution.py:599
  27.8 0.0 copy-start.3
  27.8 0.6 copy-done.3
  28.4 0.0 copy-start.4
  28.4 2.8 %shard_map.58 = (bf16[768,256]{1,0:T(8,128)(2,1)S(1)}, bf16[768,256]{1,0:T(8,128)(2,1)S(1)}, bf16[768,128]{1,0:T(8,128)(2,1)S(1)}) custom-call(f32[33]{0:T(128)S(1)} %copy-done.3), custom_call_target="tpu_custom_call" | custom-call | flops 1000000000 | bytes 10000000 | tf_op jit(solution)/shard_map/pallas_call | solution.py:637
  31.2 0.0 collective-permute-done.ya_ref
  31.2 0.0 collective-permute-done.1.yb_ref
  31.2 0.5 shard_map.56
  31.8 2.2 %collective-permute-start.4 = (f32[12,56,128]{2,1,0:T(8,128)S(1)}, f32[12,56,128]{2,1,0:T(8,128)S(1)}, u32[]{:S(2)}, u32[]{:S(2)}) collective-permute-start(f32[12,56,128]{2,1,0:T(8,128)S(1)} %get-tuple-element.53), channel_id=1, source_target_pairs={{0,480},{32,64},{64,32},{96,128},{128,96},{160,192},{192,160},{224... | collective-permute-start | bytes 1032200 | tf_op jit(solution)/shard_map/ppermute | solution.py:604
  34.0 3.7 %collective-permute-start.5 = (f32[12,56,128]{2,1,0:T(8,128)S(1)}, f32[12,56,128]{2,1,0:T(8,128)S(1)}, u32[]{:S(2)}, u32[]{:S(2)}) collective-permute-start(f32[12,56,128]{2,1,0:T(8,128)S(1)} %get-tuple-element.54), channel_id=1, source_target_pairs={{0,32},{32,0},{64,96},{96,64},{128,160},{160,128},{192,224},{224,1... | collective-permute-start | bytes 1032200 | tf_op jit(solution)/shard_map/ppermute | solution.py:599
  37.7 0.0 copy-done.1
  37.7 0.0 copy-done.4
  37.7 0.0 copy-start
  37.7 0.0 copy-start.2
  37.8 2.7 %shard_map.57 = (f32[12,12]{1,0:T(8,128)S(1)}, bf16[96,512]{1,0:T(8,128)(2,1)S(1)}, bf16[96,384]{1,0:T(8,128)(2,1)S(1)}, bf16[64,384]{1,0:T(8,128)(2,1)S(1)}) custom-call(f32[33]{0:T(128)S(1)} %copy-done.4, f32[12,32]{1,0:T(8,128)S(1)} %bitcast.31, f32[12,64,128]{2,1,0:T(8,128)S(1)} %get-tuple-element.39.after_ref.ps_ref), custom_call_target="tpu_custom_call" | custom-call | flops 1000000000 | bytes 10000000 | tf_op jit(solution)/shard_map/pallas_call | solution.py:646
  40.5 0.0 collective-permute-done.2.xb_ref.zb_ref
  40.5 0.0 copy-done
  40.5 0.0 copy-done.2
  40.5 1.1 shard_map.59
  41.6 0.0 collective-permute-done.3.xa_ref.za_ref
  41.6 0.4 shard_map.60
  42.0 3.0 %collective-permute-done.4.cb_ref = f32[12,56,128]{2,1,0:T(8,128)S(1)} collective-permute-done((f32[12,56,128]{2,1,0:T(8,128)S(1)}, f32[12,56,128]{2,1,0:T(8,128)S(1)}, u32[]{:S(2)}, u32[]{:S(2)}) %collective-permute-start.4) | collective-permute-done | bytes 344096 | tf_op jit(solution)/shard_map/ppermute | solution.py:604
  45.0 0.0 collective-permute-done.5.ca_ref
  45.0 3.1 %shard_map.61 = (f32[12,96,256]{2,1,0:T(8,128)S(1)}, f32[12,96,256]{2,1,0:T(8,128)S(1)}, f32[12,24,128]{2,1,0:T(8,128)S(1)}, f32[12,24,128]{2,1,0:T(8,128)S(1)}) custom-call(f32[12,12]{1,0:T(8,128)S(1)} %get-tuple-element.40.gram_ref, f32[12,64,256]{2,1,0:T(8,128)S(1)} %get-tuple-element.46.u_ref, f32[12,64,256]{2,1,0:T(8,128)S(1)} %get-tuple-element.47.w_ref, ...), custom_call_target="tpu_custom_call" | custom-call | flops 1000000000 | bytes 10000000 | tf_op jit(solution)/shard_map/pallas_call | solution.py:659
  48.2 1.9 %collective-permute-start.6 = (f32[12,24,128]{2,1,0:T(8,128)S(1)}, f32[12,24,128]{2,1,0:T(8,128)S(1)}, u32[]{:S(2)}, u32[]{:S(2)}) collective-permute-start(f32[12,24,128]{2,1,0:T(8,128)S(1)} %get-tuple-element.60), channel_id=1, source_target_pairs={{0,1},{1,0},{2,3},{3,2},{4,5},{5,4},{6,7},{7,6},{8,9},{9,8},{10,11... | collective-permute-start | bytes 442376 | tf_op jit(solution)/shard_map/ppermute | solution.py:599
  50.1 4.1 %collective-permute-start.7 = (f32[12,24,128]{2,1,0:T(8,128)S(1)}, f32[12,24,128]{2,1,0:T(8,128)S(1)}, u32[]{:S(2)}, u32[]{:S(2)}) collective-permute-start(f32[12,24,128]{2,1,0:T(8,128)S(1)} %get-tuple-element.61), channel_id=1, source_target_pairs={{0,31},{1,2},{2,1},{3,4},{4,3},{5,6},{6,5},{7,8},{8,7},{9,10},{10,... | collective-permute-start | bytes 442376 | tf_op jit(solution)/shard_map/ppermute | solution.py:604
  54.2 1.7 %shard_map.62 = f32[32,128]{1,0:T(8,128)S(1)} custom-call(f32[12,12]{1,0:T(8,128)S(1)} %get-tuple-element.40.gram_ref, f32[12,96,256]{2,1,0:T(8,128)S(1)} %get-tuple-element.57.g_ref, bf16[768,128]{1,0:T(8,128)(2,1)S(1)} %get-tuple-element.58.by, bf16[64,384]{1,0:T(8,128)(2,1)S(1)} %get-tuple-element.59.bx), custom_call_target="tpu_custom_call" | custom-call | flops 1000000000 | bytes 10000000 | tf_op jit(solution)/shard_map/pallas_call | solution.py:661
  55.9 14.0 %all_to_all.20 = f32[32,1,128]{2,1,0:T(1,128)S(1)} all-to-all(f32[32,1,128]{2,1,0:T(1,128)S(1)} %bitcast.29), channel_id=1, replica_groups=mesh['y'=4,'x_hi'=2,'core'=2,'x_lo'=2,'z'=16] {'y','x_hi','core','x_lo'}, dimensions={0} | all-to-all | bytes 32768 | tf_op jit(solution)/shard_map/all_to_all | solution.py:608
  70.0 0.0 collective-permute-done.6.ya_ref
  70.0 0.0 collective-permute-done.7.yb_ref
  70.0 0.5 shard_map.63
  70.4 3.4 %collective-permute-start.9 = (f32[12,64,128]{2,1,0:T(8,128)S(1)}, f32[12,64,128]{2,1,0:T(8,128)S(1)}, u32[]{:S(2)}, u32[]{:S(2)}) collective-permute-start(f32[12,64,128]{2,1,0:T(8,128)S(1)} %get-tuple-element.65), channel_id=1, source_target_pairs={{0,480},{32,64},{64,32},{96,128},{128,96},{160,192},{192,160},{224... | collective-permute-start | bytes 1179656 | tf_op jit(solution)/shard_map/ppermute | solution.py:604
  73.9 2.3 %collective-permute-start.8 = (f32[12,64,128]{2,1,0:T(8,128)S(1)}, f32[12,64,128]{2,1,0:T(8,128)S(1)}, u32[]{:S(2)}, u32[]{:S(2)}) collective-permute-start(f32[12,64,128]{2,1,0:T(8,128)S(1)} %get-tuple-element.65), channel_id=1, source_target_pairs={{0,32},{32,0},{64,96},{96,64},{128,160},{160,128},{192,224},{224,1... | collective-permute-start | bytes 1179656 | tf_op jit(solution)/shard_map/ppermute | solution.py:599
  76.2 16.5 %all_to_all.21 = f32[16,1,128]{2,1,0:T(1,128)S(1)} all-to-all(f32[16,1,128]{2,1,0:T(1,128)S(1)} %bitcast.32), channel_id=1, replica_groups=mesh['y'=4,'x_hi'=2,'core'=2,'x_lo'=2,'z'=16] {'z'}, dimensions={0} | all-to-all | bytes 16384 | tf_op jit(solution)/shard_map/all_to_all | solution.py:608
  92.6 0.0 collective-permute-done.9.xb_ref
  92.6 0.0 collective-permute-done.8.xa_ref
  92.6 3.9 %shard_map.64 = (f32[12,64,128]{2,1,0:T(8,128)S(1)}, f32[12,64,128]{2,1,0:T(8,128)S(1)}, f32[32,128]{1,0:T(8,128)S(1)}) custom-call(f32[12,12]{1,0:T(8,128)S(1)} %get-tuple-element.40.gram_ref, f32[16,128]{1,0:T(8,128)S(1)} %bitcast.25, f32[12,64,128]{2,1,0:T(8,128)S(1)} %bitcast.22, f32[12,64,128]{2,1,0:T(8,128)S(1)} %get-tuple-element.41.side_ref, ...), custom_call_target="tpu_custom_call" | custom-call | flops 1000000000 | bytes 10000000 | tf_op jit(solution)/shard_map/pallas_call | solution.py:671
  96.6 14.1 %all_to_all.22 = f32[32,1,128]{2,1,0:T(1,128)S(1)} all-to-all(f32[32,1,128]{2,1,0:T(1,128)S(1)} %bitcast.28), channel_id=1, replica_groups=mesh['y'=4,'x_hi'=2,'core'=2,'x_lo'=2,'z'=16] {'y','x_hi','core','x_lo'}, dimensions={0} | all-to-all | bytes 32768 | tf_op jit(solution)/shard_map/all_to_all | solution.py:608
  110.7 13.8 %all_to_all.23 = f32[16,1,128]{2,1,0:T(1,128)S(1)} all-to-all(f32[16,1,128]{2,1,0:T(1,128)S(1)} %bitcast.27), channel_id=1, replica_groups=mesh['y'=4,'x_hi'=2,'core'=2,'x_lo'=2,'z'=16] {'z'}, dimensions={0} | all-to-all | bytes 16384 | tf_op jit(solution)/shard_map/all_to_all | solution.py:608
  124.5 0.9 shard_map.66
  (1 shorter events, 0.0 us)
Async XLA Ops:
  3.1 37.4 %collective-permute-start.2 = (f32[12,80,128]{2,1,0:T(8,128)}, f32[12,80,128]{2,1,0:T(8,128)S(1)}, u32[]{:S(2)}, u32[]{:S(2)}) collective-permute-start(f32[12,80,128]{2,1,0:T(8,128)} %get-tuple-element.43), channel_id=1, source_target_pairs={{0,480},{32,64},{64,32},{96,128},{128,96},{160,192},{192,160},{224... | collective-permute-start | bytes 1474568 | tf_op jit(solution)/shard_map/ppermute | solution.py:604
  9.2 22.0 %collective-permute-start = (f32[12,40,128]{2,1,0:T(8,128)}, f32[12,40,128]{2,1,0:T(8,128)S(1)}, u32[]{:S(2)}, u32[]{:S(2)}) collective-permute-start(f32[12,40,128]{2,1,0:T(8,128)} %get-tuple-element.37), channel_id=1, source_target_pairs={{0,1},{1,0},{2,3},{3,2},{4,5},{5,4},{6,7},{7,6},{8,9},{9,8},{10,11... | collective-permute-start | bytes 737288 | tf_op jit(solution)/shard_map/ppermute | solution.py:599
  12.7 18.5 %collective-permute-start.1 = (f32[12,40,128]{2,1,0:T(8,128)}, f32[12,40,128]{2,1,0:T(8,128)S(1)}, u32[]{:S(2)}, u32[]{:S(2)}) collective-permute-start(f32[12,40,128]{2,1,0:T(8,128)} %get-tuple-element.38), channel_id=1, source_target_pairs={{0,31},{1,2},{2,1},{3,4},{4,3},{5,6},{6,5},{7,8},{8,7},{9,10},{10,... | collective-permute-start | bytes 737288 | tf_op jit(solution)/shard_map/ppermute | solution.py:604
  23.0 14.7 %copy-start.1 = (f32[32,12]{0,1:T(8,128)S(1)}, f32[32,12]{0,1:T(8,128)}, u32[]{:S(2)}) copy-start(f32[32,12]{0,1:T(8,128)} %param.7) | copy-start | bytes 4612
  23.0 18.6 %collective-permute-start.3 = (f32[12,80,128]{2,1,0:T(8,128)}, f32[12,80,128]{2,1,0:T(8,128)S(1)}, u32[]{:S(2)}, u32[]{:S(2)}) collective-permute-start(f32[12,80,128]{2,1,0:T(8,128)} %get-tuple-element.48), channel_id=1, source_target_pairs={{0,32},{32,0},{64,96},{96,64},{128,160},{160,128},{192,224},{224,1... | collective-permute-start | bytes 1474568 | tf_op jit(solution)/shard_map/ppermute | solution.py:599
  27.8 0.7 copy-start.3
  28.4 9.3 %copy-start.4 = (f32[33]{0:T(128)S(1)}, f32[33]{0:T(128)}, u32[]{:S(2)}) copy-start(f32[33]{0:T(128)} %tx_ref.1) | copy-start | bytes 400
  31.8 13.2 %collective-permute-start.4 = (f32[12,56,128]{2,1,0:T(8,128)S(1)}, f32[12,56,128]{2,1,0:T(8,128)S(1)}, u32[]{:S(2)}, u32[]{:S(2)}) collective-permute-start(f32[12,56,128]{2,1,0:T(8,128)S(1)} %get-tuple-element.53), channel_id=1, source_target_pairs={{0,480},{32,64},{64,32},{96,128},{128,96},{160,192},{192,160},{224... | collective-permute-start | bytes 1032200 | tf_op jit(solution)/shard_map/ppermute | solution.py:604
  34.0 11.0 %collective-permute-start.5 = (f32[12,56,128]{2,1,0:T(8,128)S(1)}, f32[12,56,128]{2,1,0:T(8,128)S(1)}, u32[]{:S(2)}, u32[]{:S(2)}) collective-permute-start(f32[12,56,128]{2,1,0:T(8,128)S(1)} %get-tuple-element.54), channel_id=1, source_target_pairs={{0,32},{32,0},{64,96},{96,64},{128,160},{160,128},{192,224},{224,1... | collective-permute-start | bytes 1032200 | tf_op jit(solution)/shard_map/ppermute | solution.py:599
  37.7 2.8 %copy-start = (f32[1,12,64,128]{3,2,1,0:T(8,128)S(1)}, f32[1,12,64,128]{3,2,1,0:T(8,128)}, u32[]{:S(2)}) copy-start(f32[1,12,64,128]{3,2,1,0:T(8,128)} %param.5) | copy-start | bytes 1179652
  37.7 2.8 %copy-start.2 = (f32[12,64,128]{2,1,0:T(8,128)S(1)}, f32[12,64,128]{2,1,0:T(8,128)}, u32[]{:S(2)}) copy-start(f32[12,64,128]{2,1,0:T(8,128)} %get-tuple-element.42.p_ref) | copy-start | bytes 1179652
  48.2 21.8 %collective-permute-start.6 = (f32[12,24,128]{2,1,0:T(8,128)S(1)}, f32[12,24,128]{2,1,0:T(8,128)S(1)}, u32[]{:S(2)}, u32[]{:S(2)}) collective-permute-start(f32[12,24,128]{2,1,0:T(8,128)S(1)} %get-tuple-element.60), channel_id=1, source_target_pairs={{0,1},{1,0},{2,3},{3,2},{4,5},{5,4},{6,7},{7,6},{8,9},{9,8},{10,11... | collective-permute-start | bytes 442376 | tf_op jit(solution)/shard_map/ppermute | solution.py:599
  50.1 19.9 %collective-permute-start.7 = (f32[12,24,128]{2,1,0:T(8,128)S(1)}, f32[12,24,128]{2,1,0:T(8,128)S(1)}, u32[]{:S(2)}, u32[]{:S(2)}) collective-permute-start(f32[12,24,128]{2,1,0:T(8,128)S(1)} %get-tuple-element.61), channel_id=1, source_target_pairs={{0,31},{1,2},{2,1},{3,4},{4,3},{5,6},{6,5},{7,8},{8,7},{9,10},{10,... | collective-permute-start | bytes 442376 | tf_op jit(solution)/shard_map/ppermute | solution.py:604
  70.4 22.2 %collective-permute-start.9 = (f32[12,64,128]{2,1,0:T(8,128)S(1)}, f32[12,64,128]{2,1,0:T(8,128)S(1)}, u32[]{:S(2)}, u32[]{:S(2)}) collective-permute-start(f32[12,64,128]{2,1,0:T(8,128)S(1)} %get-tuple-element.65), channel_id=1, source_target_pairs={{0,480},{32,64},{64,32},{96,128},{128,96},{160,192},{192,160},{224... | collective-permute-start | bytes 1179656 | tf_op jit(solution)/shard_map/ppermute | solution.py:604
  73.9 18.8 %collective-permute-start.8 = (f32[12,64,128]{2,1,0:T(8,128)S(1)}, f32[12,64,128]{2,1,0:T(8,128)S(1)}, u32[]{:S(2)}, u32[]{:S(2)}) collective-permute-start(f32[12,64,128]{2,1,0:T(8,128)S(1)} %get-tuple-element.65), channel_id=1, source_target_pairs={{0,32},{32,0},{64,96},{96,64},{128,160},{160,128},{192,224},{224,1... | collective-permute-start | bytes 1179656 | tf_op jit(solution)/shard_map/ppermute | solution.py:599

commit v6 on v5

--- a/solution.py
+++ b/solution.py
@@ -259,9 +259,12 @@
         copy.wait()
 
 
+REST = FLUOR * A_HALO
+
+
 def pack_corner(odd_x, pairing, side_ref, ps_ref, out_ref):
     lane = lane_of((32, 128))
-    lane8 = lane_of((8, 128))
+    lane4 = lane_of((4, 128))
     lane16 = lane_of((16, 128))
     spare = 2 * A_HALO
     a_rows = pl.ds(edge_rows(odd_x, pairing, A_HALO), A_HALO)
@@ -269,9 +272,13 @@
     for f in range(FLUOR):
         p_top = ps_ref[f, p_rows, :]
         a_side = side_ref[f, a_rows, :]
-        out_ref[f, :32, :] = jnp.where(lane < spare, a_side[:32], roll(p_top, spare))
-        out_ref[f, 32:48, :] = jnp.where(lane16 < spare, a_side[32:], roll(p_top[:16], spare - P_HALO))
-        out_ref[f, 48:, :] = jnp.where(lane8 < P_HALO, roll(p_top[16:24], -P_HALO), p_top[24:])
+        at = A_HALO * f
+        out_ref[at : at + 32, :] = jnp.where(lane < spare, a_side[:32], roll(p_top, spare))
+        out_ref[at + 32 : at + 48, :] = jnp.where(lane16 < spare, a_side[32:], roll(p_top[:16], spare - P_HALO))
+        rest = roll(p_top[16:20], -P_HALO)
+        for k in range(1, 4):
+            rest = jnp.where(lane4 < 32 * k, rest, roll(p_top[16 + 4 * k : 20 + 4 * k], 32 * k - P_HALO))
+        out_ref[REST + 4 * f : REST + 4 * f + 4, :] = rest
 
 
 def corner_body(ya_ref, yb_ref, side_ref, ps_ref, cb_ref, ca_ref):
@@ -436,14 +443,16 @@
         (ub_ref, wb_ref, cb_ref, odd_x == 0),
     ):
         for f in range(FLUOR):
-            left = roll(corner[f, :32, :], -spare)
-            right = roll(corner[f, 32:48, :], P_HALO - spare)
-            last = corner[f, 48:, :]
+            at = A_HALO * f
+            left = roll(corner[at : at + 32, :], -spare)
+            right = roll(corner[at + 32 : at + 48, :], P_HALO - spare)
+            rest = corner[REST + 4 * f : REST + 4 * f + 4, :]
+            last = jnp.concatenate([roll(rest, P_HALO - 32 * k) for k in range(4)], axis=0)
             side_ref[f, :16, :] = jnp.where(lane16 < P_HALO, left[:16], jnp.where(lane16 < 2 * P_HALO, right, 0.0))
             side_ref[f, 16:24, :] = jnp.where(
-                lane8 < P_HALO, left[16:24], jnp.where(lane8 < 2 * P_HALO, roll(last, P_HALO), 0.0)
+                lane8 < P_HALO, left[16:24], jnp.where(lane8 < 2 * P_HALO, last[:8], 0.0)
             )
-            side_ref[f, 24:, :] = jnp.where(lane8 < P_HALO, left[24:], jnp.where(lane8 < 2 * P_HALO, last, 0.0))
+            side_ref[f, 24:, :] = jnp.where(lane8 < P_HALO, left[24:], jnp.where(lane8 < 2 * P_HALO, last[8:], 0.0))
         a_at = jnp.where(above, 0, A_HALO + ROWS)
         p_at = jnp.where(above, 0, P_HALO + ROWS)
         along_half(
@@ -453,7 +462,7 @@
             lambda f, x: put_stack(sw_ref, f, p_at, P_ROWS, x + w_part[f]),
         )
         along_half(
-            lambda part: corner[part, :A_HALO, :],
+            lambda part: corner[A_HALO * part.start : A_HALO * part.stop, :].reshape(-1, A_HALO, 128),
             my,
             128,
             lambda f, x: put_stack(su_ref, f, a_at, A_ROWS, x + u_part[f]),
@@ -519,10 +528,10 @@
         )
         for above, main, corner, far, near in (
             (True, choose(odd_x, za_ref[f, :A_HALO, :], zb_ref[f, :A_HALO, :]),
-             choose(odd_x, ca_ref[f, :A_HALO, :], cb_ref[f, :A_HALO, :]), choose(odd_x, xa_ref[f], xb_ref[f]),
+             choose(odd_x, ca_ref[A_HALO * f : A_HALO * f + A_HALO, :], cb_ref[A_HALO * f : A_HALO * f + A_HALO, :]), choose(odd_x, xa_ref[f], xb_ref[f]),
              slice(0, G_HALO)),
             (False, choose(odd_x, zb_ref[f, :A_HALO, :], za_ref[f, :A_HALO, :]),
-             choose(odd_x, cb_ref[f, :A_HALO, :], ca_ref[f, :A_HALO, :]), choose(odd_x, xb_ref[f], xa_ref[f]),
+             choose(odd_x, cb_ref[A_HALO * f : A_HALO * f + A_HALO, :], ca_ref[A_HALO * f : A_HALO * f + A_HALO, :]), choose(odd_x, xb_ref[f], xa_ref[f]),
              slice(G_ROWS - G_HALO, G_ROWS)),
         ):
             parts = [far[:32], g_ref[f, near, :COLS]], [far[32:], gs_ref[f, near, :]]
@@ -543,10 +552,17 @@
         g_out[f] = n_ref[f, G_HALO : G_HALO + ROWS, :COLS]
 
 
-def last_body(total_ref, a_ref, g_ref, out_ref):
+def last_body(total_ref, a_ref, g_ref, out_hbm, out_ref, sems):
     t = step_length(total_ref)
-    for f in range(FLUOR):
-        out_ref[f] = jnp.maximum(a_ref[f] - t * g_ref[f], 0.0)
+    copies = []
+    for k in range(4):
+        fields = slice(3 * k, 3 * k + 3)
+        out_ref[fields] = jnp.maximum(a_ref[fields] - t * g_ref[fields], 0.0)
+        part = pl.ds(3 * k, 3)
+        copies.append(pltpu.make_async_copy(out_ref.at[part], out_hbm.at[part], sems.at[k]))
+        copies[-1].start()
+    for copy in copies:
+        copy.wait()
 
 
 TILE = (FLUOR, ROWS, COLS)
@@ -640,7 +656,7 @@
         [((768, 256), bf16)] * 2 + [((768, 128), bf16)],
         10**9,
     )(taps_y)
-    corner = (FLUOR, 56, 128)
+    corner = (REST + 4 * FLUOR, 128)
     side, ps, cb, ca = kernel(corner_body, "vv", [(TILE, f32)] * 2 + [(corner, f32)] * 2, 10**7)(ya, yb)
     ca, cb = trade(ca, cb, GX)
     gram, mx, px, bx = kernel(
@@ -673,7 +689,14 @@
     )
     (far,) = kernel(relay, "v", [((FAR_COUNT, 128), f32)], 10**6)(spread(partial, NEAR))
     total = spread(far, FAR)
-    (out,) = kernel(last_body, "vvv", [(TILE, f32)], 10**7)(total, a1, g1)
+    (out,) = kernel(
+        last_body,
+        "vvv",
+        [(TILE, f32)],
+        10**7,
+        [pltpu.VMEM(TILE, f32), pltpu.SemaphoreType.DMA((4,))],
+        space=pltpu.HBM,
+    )(total, a1, g1)
     return out[None]
 
 

time: 126 us -> 126 us (level)
  no operation moved by 1% of the time
where the time goes in v6:
time: 126 us; the launch traced here: 125 us
  blocking collectives  58.4 us (46%)
  starting transfers between devices  42.2 us (33%)
  Pallas kernels  20.9 us (17%)
  waiting for transfers between devices  2.48 us (2%)
    all_to_all x4, blocking collectives, spread(): lax.all_to_all(rows.reshape(rows.shape[0], 1, 128), axes, 0, 0, tiled=True)  58.4 us
    ppermute x5, starting transfers between devices, trade_second(): lax.ppermute(edge, axes, [(i, (i + (1 if i % 2 else -1)) % count) for i i...  26 us
    ppermute x5, starting transfers between devices, trade_first(): return lax.ppermute(edge, axes, [(i, i ^ 1) for i in range(length(axes))])  16.2 us
    pallas_call x1, Pallas kernels, local(): second_call(gram, total, a0, side, za, zb, ca, cb, d, g, g_side, xa, xb,...  3.93 us
    pallas_call x1, Pallas kernels, local(): first_call(gram, u, w, ua, ub, wa, wb, cb, ca, my, py, mx, px)  3.17 us
    pallas_call x1, Pallas kernels, local(): kernel(project_body, 'hhh', [(TILE, f32)] + [(edge, f32)] * 2 + [((FLUOR,...  3.14 us
    pallas_call x1, Pallas kernels, local(): kernel(functools.partial(y_matrices_body, sizes[1]), 's', [((768, 256), b...  2.76 us
    pallas_call x1, Pallas kernels, local(): kernel(functools.partial(x_matrices_body, sizes[0]), 'svv', [((FLUOR, FLU...  2.73 us
  transfers between devices with their start and end apart: 10, of which 1 were waited for; matrix products, arithmetic and copies ran while one was open for 0% of the time, Pallas kernels for 7%

profile of v6, /device:TPU:1, one launch (start us, length us, event | category | flops | bytes accessed | tf_op | source)
XLA Modules:
  0.0 125.1 jit_solution(1289361895255645477)
XLA Ops:
  0.0 3.1 %shard_map.55 = (f32[12,64,128]{2,1,0:T(8,128)}, f32[12,80,128]{2,1,0:T(8,128)}, f32[12,80,128]{2,1,0:T(8,128)}, f32[12,40,128]{2,1,0:T(8,128)}, f32[12,40,128]{2,1,0:T(8,128)}) custom-call(f32[12,32]{1,0:T(8,128)} %bitcast.30, f32[12,64,128]{2,1,0:T(8,128)} %bitcast.20, bf16[32,64,128]{2,1,0:T(8,128)(2,1)} %bitcast.33), custom_call_target="tpu_custom_call" | custom-call | flops 10000000 | bytes 100000 | tf_op jit(solution)/shard_map/pallas_call | solution.py:633
  3.1 6.0 %collective-permute-start.2 = (f32[12,80,128]{2,1,0:T(8,128)}, f32[12,80,128]{2,1,0:T(8,128)S(1)}, u32[]{:S(2)}, u32[]{:S(2)}) collective-permute-start(f32[12,80,128]{2,1,0:T(8,128)} %get-tuple-element.43), channel_id=1, source_target_pairs={{0,480},{32,64},{64,32},{96,128},{128,96},{160,192},{192,160},{224... | collective-permute-start | bytes 1474568 | tf_op jit(solution)/shard_map/ppermute | solution.py:620
  9.2 3.5 %collective-permute-start = (f32[12,40,128]{2,1,0:T(8,128)}, f32[12,40,128]{2,1,0:T(8,128)S(1)}, u32[]{:S(2)}, u32[]{:S(2)}) collective-permute-start(f32[12,40,128]{2,1,0:T(8,128)} %get-tuple-element.37), channel_id=1, source_target_pairs={{0,1},{1,0},{2,3},{3,2},{4,5},{5,4},{6,7},{7,6},{8,9},{9,8},{10,11... | collective-permute-start | bytes 737288 | tf_op jit(solution)/shard_map/ppermute | solution.py:615
  12.7 10.2 %collective-permute-start.1 = (f32[12,40,128]{2,1,0:T(8,128)}, f32[12,40,128]{2,1,0:T(8,128)S(1)}, u32[]{:S(2)}, u32[]{:S(2)}) collective-permute-start(f32[12,40,128]{2,1,0:T(8,128)} %get-tuple-element.38), channel_id=1, source_target_pairs={{0,31},{1,2},{2,1},{3,4},{4,3},{5,6},{6,5},{7,8},{8,7},{9,10},{10,... | collective-permute-start | bytes 737288 | tf_op jit(solution)/shard_map/ppermute | solution.py:620
  23.0 0.0 copy-start.1
  23.0 4.8 %collective-permute-start.3 = (f32[12,80,128]{2,1,0:T(8,128)}, f32[12,80,128]{2,1,0:T(8,128)S(1)}, u32[]{:S(2)}, u32[]{:S(2)}) collective-permute-start(f32[12,80,128]{2,1,0:T(8,128)} %get-tuple-element.48), channel_id=1, source_target_pairs={{0,32},{32,0},{64,96},{96,64},{128,160},{160,128},{192,224},{224,1... | collective-permute-start | bytes 1474568 | tf_op jit(solution)/shard_map/ppermute | solution.py:615
  27.8 0.0 copy-start.3
  27.8 0.6 copy-done.3
  28.4 0.0 copy-start.4
  28.4 2.8 %shard_map.58 = (bf16[768,256]{1,0:T(8,128)(2,1)S(1)}, bf16[768,256]{1,0:T(8,128)(2,1)S(1)}, bf16[768,128]{1,0:T(8,128)(2,1)S(1)}) custom-call(f32[33]{0:T(128)S(1)} %copy-done.3), custom_call_target="tpu_custom_call" | custom-call | flops 1000000000 | bytes 10000000 | tf_op jit(solution)/shard_map/pallas_call | solution.py:653
  31.2 0.0 collective-permute-done.ya_ref
  31.2 0.0 collective-permute-done.1.yb_ref
  31.2 0.6 shard_map.56
  31.8 2.2 %collective-permute-start.4 = (f32[624,128]{1,0:T(8,128)S(1)}, f32[624,128]{1,0:T(8,128)S(1)}, u32[]{:S(2)}, u32[]{:S(2)}) collective-permute-start(f32[624,128]{1,0:T(8,128)S(1)} %get-tuple-element.53), channel_id=1, source_target_pairs={{0,480},{32,64},{64,32},{96,128},{128,96},{160,192},{192,160},{224... | collective-permute-start | bytes 958472 | tf_op jit(solution)/shard_map/ppermute | solution.py:620
  34.0 3.7 %collective-permute-start.5 = (f32[624,128]{1,0:T(8,128)S(1)}, f32[624,128]{1,0:T(8,128)S(1)}, u32[]{:S(2)}, u32[]{:S(2)}) collective-permute-start(f32[624,128]{1,0:T(8,128)S(1)} %get-tuple-element.54), channel_id=1, source_target_pairs={{0,32},{32,0},{64,96},{96,64},{128,160},{160,128},{192,224},{224,1... | collective-permute-start | bytes 958472 | tf_op jit(solution)/shard_map/ppermute | solution.py:615
  37.8 0.0 copy-done.1
  37.8 0.0 copy-done.4
  37.8 0.0 copy-start
  37.8 0.0 copy-start.2
  37.8 2.7 %shard_map.57 = (f32[12,12]{1,0:T(8,128)S(1)}, bf16[96,512]{1,0:T(8,128)(2,1)S(1)}, bf16[96,384]{1,0:T(8,128)(2,1)S(1)}, bf16[64,384]{1,0:T(8,128)(2,1)S(1)}) custom-call(f32[33]{0:T(128)S(1)} %copy-done.4, f32[12,32]{1,0:T(8,128)S(1)} %bitcast.31, f32[12,64,128]{2,1,0:T(8,128)S(1)} %get-tuple-element.39.after_ref.ps_ref), custom_call_target="tpu_custom_call" | custom-call | flops 1000000000 | bytes 10000000 | tf_op jit(solution)/shard_map/pallas_call | solution.py:662
  40.5 0.0 collective-permute-done.2.xb_ref.zb_ref
  40.5 0.0 copy-done
  40.6 0.0 copy-done.2
  40.6 1.1 shard_map.59
  41.6 0.0 collective-permute-done.3.xa_ref.za_ref
  41.6 0.4 shard_map.60
  42.1 2.5 %collective-permute-done.4.cb_ref = f32[624,128]{1,0:T(8,128)S(1)} collective-permute-done((f32[624,128]{1,0:T(8,128)S(1)}, f32[624,128]{1,0:T(8,128)S(1)}, u32[]{:S(2)}, u32[]{:S(2)}) %collective-permute-start.4) | collective-permute-done | bytes 319520 | tf_op jit(solution)/shard_map/ppermute | solution.py:620
  44.5 0.0 collective-permute-done.5.ca_ref
  44.5 3.2 %shard_map.61 = (f32[12,96,256]{2,1,0:T(8,128)S(1)}, f32[12,96,256]{2,1,0:T(8,128)S(1)}, f32[12,24,128]{2,1,0:T(8,128)S(1)}, f32[12,24,128]{2,1,0:T(8,128)S(1)}) custom-call(f32[12,12]{1,0:T(8,128)S(1)} %get-tuple-element.40.gram_ref, f32[12,64,256]{2,1,0:T(8,128)S(1)} %get-tuple-element.46.u_ref, f32[12,64,256]{2,1,0:T(8,128)S(1)} %get-tuple-element.47.w_ref, ...), custom_call_target="tpu_custom_call" | custom-call | flops 1000000000 | bytes 10000000 | tf_op jit(solution)/shard_map/pallas_call | solution.py:675
  47.7 1.9 %collective-permute-start.6 = (f32[12,24,128]{2,1,0:T(8,128)S(1)}, f32[12,24,128]{2,1,0:T(8,128)S(1)}, u32[]{:S(2)}, u32[]{:S(2)}) collective-permute-start(f32[12,24,128]{2,1,0:T(8,128)S(1)} %get-tuple-element.60), channel_id=1, source_target_pairs={{0,1},{1,0},{2,3},{3,2},{4,5},{5,4},{6,7},{7,6},{8,9},{9,8},{10,11... | collective-permute-start | bytes 442376 | tf_op jit(solution)/shard_map/ppermute | solution.py:615
  49.6 4.1 %collective-permute-start.7 = (f32[12,24,128]{2,1,0:T(8,128)S(1)}, f32[12,24,128]{2,1,0:T(8,128)S(1)}, u32[]{:S(2)}, u32[]{:S(2)}) collective-permute-start(f32[12,24,128]{2,1,0:T(8,128)S(1)} %get-tuple-element.61), channel_id=1, source_target_pairs={{0,31},{1,2},{2,1},{3,4},{4,3},{5,6},{6,5},{7,8},{8,7},{9,10},{10,... | collective-permute-start | bytes 442376 | tf_op jit(solution)/shard_map/ppermute | solution.py:620
  53.7 1.7 %shard_map.62 = f32[32,128]{1,0:T(8,128)S(1)} custom-call(f32[12,12]{1,0:T(8,128)S(1)} %get-tuple-element.40.gram_ref, f32[12,96,256]{2,1,0:T(8,128)S(1)} %get-tuple-element.57.g_ref, bf16[768,128]{1,0:T(8,128)(2,1)S(1)} %get-tuple-element.58.by, bf16[64,384]{1,0:T(8,128)(2,1)S(1)} %get-tuple-element.59.bx), custom_call_target="tpu_custom_call" | custom-call | flops 1000000000 | bytes 10000000 | tf_op jit(solution)/shard_map/pallas_call | solution.py:677
  55.5 14.1 %all_to_all.20 = f32[32,1,128]{2,1,0:T(1,128)S(1)} all-to-all(f32[32,1,128]{2,1,0:T(1,128)S(1)} %bitcast.29), channel_id=1, replica_groups=mesh['y'=4,'x_hi'=2,'core'=2,'x_lo'=2,'z'=16] {'y','x_hi','core','x_lo'}, dimensions={0} | all-to-all | bytes 32768 | tf_op jit(solution)/shard_map/all_to_all | solution.py:624
  69.5 0.0 collective-permute-done.6.ya_ref
  69.5 0.0 collective-permute-done.7.yb_ref
  69.5 0.5 shard_map.63
  70.0 3.4 %collective-permute-start.9 = (f32[12,64,128]{2,1,0:T(8,128)S(1)}, f32[12,64,128]{2,1,0:T(8,128)S(1)}, u32[]{:S(2)}, u32[]{:S(2)}) collective-permute-start(f32[12,64,128]{2,1,0:T(8,128)S(1)} %get-tuple-element.65), channel_id=1, source_target_pairs={{0,480},{32,64},{64,32},{96,128},{128,96},{160,192},{192,160},{224... | collective-permute-start | bytes 1179656 | tf_op jit(solution)/shard_map/ppermute | solution.py:620
  73.4 2.3 %collective-permute-start.8 = (f32[12,64,128]{2,1,0:T(8,128)S(1)}, f32[12,64,128]{2,1,0:T(8,128)S(1)}, u32[]{:S(2)}, u32[]{:S(2)}) collective-permute-start(f32[12,64,128]{2,1,0:T(8,128)S(1)} %get-tuple-element.65), channel_id=1, source_target_pairs={{0,32},{32,0},{64,96},{96,64},{128,160},{160,128},{192,224},{224,1... | collective-permute-start | bytes 1179656 | tf_op jit(solution)/shard_map/ppermute | solution.py:615
  75.7 16.5 %all_to_all.21 = f32[16,1,128]{2,1,0:T(1,128)S(1)} all-to-all(f32[16,1,128]{2,1,0:T(1,128)S(1)} %bitcast.32), channel_id=1, replica_groups=mesh['y'=4,'x_hi'=2,'core'=2,'x_lo'=2,'z'=16] {'z'}, dimensions={0} | all-to-all | bytes 16384 | tf_op jit(solution)/shard_map/all_to_all | solution.py:624
  92.2 0.0 collective-permute-done.9.xb_ref
  92.2 0.0 collective-permute-done.8.xa_ref
  92.2 3.9 %shard_map.64 = (f32[12,64,128]{2,1,0:T(8,128)S(1)}, f32[12,64,128]{2,1,0:T(8,128)S(1)}, f32[32,128]{1,0:T(8,128)S(1)}) custom-call(f32[12,12]{1,0:T(8,128)S(1)} %get-tuple-element.40.gram_ref, f32[16,128]{1,0:T(8,128)S(1)} %bitcast.25, f32[12,64,128]{2,1,0:T(8,128)S(1)} %bitcast.22, f32[12,64,128]{2,1,0:T(8,128)S(1)} %get-tuple-element.41.side_ref, ...), custom_call_target="tpu_custom_call" | custom-call | flops 1000000000 | bytes 10000000 | tf_op jit(solution)/shard_map/pallas_call | solution.py:687
  96.1 14.1 %all_to_all.22 = f32[32,1,128]{2,1,0:T(1,128)S(1)} all-to-all(f32[32,1,128]{2,1,0:T(1,128)S(1)} %bitcast.28), channel_id=1, replica_groups=mesh['y'=4,'x_hi'=2,'core'=2,'x_lo'=2,'z'=16] {'y','x_hi','core','x_lo'}, dimensions={0} | all-to-all | bytes 32768 | tf_op jit(solution)/shard_map/all_to_all | solution.py:624
  110.2 13.8 %all_to_all.23 = f32[16,1,128]{2,1,0:T(1,128)S(1)} all-to-all(f32[16,1,128]{2,1,0:T(1,128)S(1)} %bitcast.27), channel_id=1, replica_groups=mesh['y'=4,'x_hi'=2,'core'=2,'x_lo'=2,'z'=16] {'z'}, dimensions={0} | all-to-all | bytes 16384 | tf_op jit(solution)/shard_map/all_to_all | solution.py:624
  124.0 0.9 shard_map.66
  (1 shorter events, 0.0 us)
Async XLA Ops:
  3.1 37.4 %collective-permute-start.2 = (f32[12,80,128]{2,1,0:T(8,128)}, f32[12,80,128]{2,1,0:T(8,128)S(1)}, u32[]{:S(2)}, u32[]{:S(2)}) collective-permute-start(f32[12,80,128]{2,1,0:T(8,128)} %get-tuple-element.43), channel_id=1, source_target_pairs={{0,480},{32,64},{64,32},{96,128},{128,96},{160,192},{192,160},{224... | collective-permute-start | bytes 1474568 | tf_op jit(solution)/shard_map/ppermute | solution.py:620
  9.2 22.0 %collective-permute-start = (f32[12,40,128]{2,1,0:T(8,128)}, f32[12,40,128]{2,1,0:T(8,128)S(1)}, u32[]{:S(2)}, u32[]{:S(2)}) collective-permute-start(f32[12,40,128]{2,1,0:T(8,128)} %get-tuple-element.37), channel_id=1, source_target_pairs={{0,1},{1,0},{2,3},{3,2},{4,5},{5,4},{6,7},{7,6},{8,9},{9,8},{10,11... | collective-permute-start | bytes 737288 | tf_op jit(solution)/shard_map/ppermute | solution.py:615
  12.7 18.5 %collective-permute-start.1 = (f32[12,40,128]{2,1,0:T(8,128)}, f32[12,40,128]{2,1,0:T(8,128)S(1)}, u32[]{:S(2)}, u32[]{:S(2)}) collective-permute-start(f32[12,40,128]{2,1,0:T(8,128)} %get-tuple-element.38), channel_id=1, source_target_pairs={{0,31},{1,2},{2,1},{3,4},{4,3},{5,6},{6,5},{7,8},{8,7},{9,10},{10,... | collective-permute-start | bytes 737288 | tf_op jit(solution)/shard_map/ppermute | solution.py:620
  23.0 14.8 %copy-start.1 = (f32[32,12]{0,1:T(8,128)S(1)}, f32[32,12]{0,1:T(8,128)}, u32[]{:S(2)}) copy-start(f32[32,12]{0,1:T(8,128)} %param.7) | copy-start | bytes 4612
  23.0 18.6 %collective-permute-start.3 = (f32[12,80,128]{2,1,0:T(8,128)}, f32[12,80,128]{2,1,0:T(8,128)S(1)}, u32[]{:S(2)}, u32[]{:S(2)}) collective-permute-start(f32[12,80,128]{2,1,0:T(8,128)} %get-tuple-element.48), channel_id=1, source_target_pairs={{0,32},{32,0},{64,96},{96,64},{128,160},{160,128},{192,224},{224,1... | collective-permute-start | bytes 1474568 | tf_op jit(solution)/shard_map/ppermute | solution.py:615
  27.8 0.7 copy-start.3
  28.4 9.3 %copy-start.4 = (f32[33]{0:T(128)S(1)}, f32[33]{0:T(128)}, u32[]{:S(2)}) copy-start(f32[33]{0:T(128)} %tx_ref.1) | copy-start | bytes 400
  31.8 12.7 %collective-permute-start.4 = (f32[624,128]{1,0:T(8,128)S(1)}, f32[624,128]{1,0:T(8,128)S(1)}, u32[]{:S(2)}, u32[]{:S(2)}) collective-permute-start(f32[624,128]{1,0:T(8,128)S(1)} %get-tuple-element.53), channel_id=1, source_target_pairs={{0,480},{32,64},{64,32},{96,128},{128,96},{160,192},{192,160},{224... | collective-permute-start | bytes 958472 | tf_op jit(solution)/shard_map/ppermute | solution.py:620
  34.0 10.5 %collective-permute-start.5 = (f32[624,128]{1,0:T(8,128)S(1)}, f32[624,128]{1,0:T(8,128)S(1)}, u32[]{:S(2)}, u32[]{:S(2)}) collective-permute-start(f32[624,128]{1,0:T(8,128)S(1)} %get-tuple-element.54), channel_id=1, source_target_pairs={{0,32},{32,0},{64,96},{96,64},{128,160},{160,128},{192,224},{224,1... | collective-permute-start | bytes 958472 | tf_op jit(solution)/shard_map/ppermute | solution.py:615
  37.8 2.8 %copy-start = (f32[1,12,64,128]{3,2,1,0:T(8,128)S(1)}, f32[1,12,64,128]{3,2,1,0:T(8,128)}, u32[]{:S(2)}) copy-start(f32[1,12,64,128]{3,2,1,0:T(8,128)} %param.5) | copy-start | bytes 1179652
  37.8 2.8 %copy-start.2 = (f32[12,64,128]{2,1,0:T(8,128)S(1)}, f32[12,64,128]{2,1,0:T(8,128)}, u32[]{:S(2)}) copy-start(f32[12,64,128]{2,1,0:T(8,128)} %get-tuple-element.42.p_ref) | copy-start | bytes 1179652
  47.7 21.8 %collective-permute-start.6 = (f32[12,24,128]{2,1,0:T(8,128)S(1)}, f32[12,24,128]{2,1,0:T(8,128)S(1)}, u32[]{:S(2)}, u32[]{:S(2)}) collective-permute-start(f32[12,24,128]{2,1,0:T(8,128)S(1)} %get-tuple-element.60), channel_id=1, source_target_pairs={{0,1},{1,0},{2,3},{3,2},{4,5},{5,4},{6,7},{7,6},{8,9},{9,8},{10,11... | collective-permute-start | bytes 442376 | tf_op jit(solution)/shard_map/ppermute | solution.py:615
  49.6 19.9 %collective-permute-start.7 = (f32[12,24,128]{2,1,0:T(8,128)S(1)}, f32[12,24,128]{2,1,0:T(8,128)S(1)}, u32[]{:S(2)}, u32[]{:S(2)}) collective-permute-start(f32[12,24,128]{2,1,0:T(8,128)S(1)} %get-tuple-element.61), channel_id=1, source_target_pairs={{0,31},{1,2},{2,1},{3,4},{4,3},{5,6},{6,5},{7,8},{8,7},{9,10},{10,... | collective-permute-start | bytes 442376 | tf_op jit(solution)/shard_map/ppermute | solution.py:620
  70.0 22.2 %collective-permute-start.9 = (f32[12,64,128]{2,1,0:T(8,128)S(1)}, f32[12,64,128]{2,1,0:T(8,128)S(1)}, u32[]{:S(2)}, u32[]{:S(2)}) collective-permute-start(f32[12,64,128]{2,1,0:T(8,128)S(1)} %get-tuple-element.65), channel_id=1, source_target_pairs={{0,480},{32,64},{64,32},{96,128},{128,96},{160,192},{192,160},{224... | collective-permute-start | bytes 1179656 | tf_op jit(solution)/shard_map/ppermute | solution.py:620
  73.4 18.8 %collective-permute-start.8 = (f32[12,64,128]{2,1,0:T(8,128)S(1)}, f32[12,64,128]{2,1,0:T(8,128)S(1)}, u32[]{:S(2)}, u32[]{:S(2)}) collective-permute-start(f32[12,64,128]{2,1,0:T(8,128)S(1)} %get-tuple-element.65), channel_id=1, source_target_pairs={{0,32},{32,0},{64,96},{96,64},{128,160},{160,128},{192,224},{224,1... | collective-permute-start | bytes 1179656 | tf_op jit(solution)/shard_map/ppermute | solution.py:615

commit v7 on v6

--- a/solution.py
+++ b/solution.py
@@ -513,7 +513,7 @@
 
 
 def second_body(
-    gram_ref, total_ref, a_ref, side_ref, za_ref, zb_ref, ca_ref, cb_ref, d_ref, g_ref, gs_ref, xa_ref, xb_ref,
+    gram_ref, total_ref, a_ref, side_ref, za_ref, zb_ref, ca_ref, cb_ref, d_ref, g_ref, gs_ref, xb_ref, xa_ref,
     my, mx, by, bx,
     a_out, g_out, sum_ref, v_ref, n_ref, y_ref, z_ref, x_ref, u_ref,
 ):
@@ -685,7 +685,7 @@
     xa, xb = trade(send, send, GX)
     total = spread(far, FAR)
     a1, g1, partial = second_call(
-        gram, total, a0, side, za, zb, ca, cb, d, g, g_side, xa, xb, my, mx, by, bx
+        gram, total, a0, side, za, zb, ca, cb, d, g, g_side, xb, xa, my, mx, by, bx
     )
     (far,) = kernel(relay, "v", [((FAR_COUNT, 128), f32)], 10**6)(spread(partial, NEAR))
     total = spread(far, FAR)

time: 126 us -> 124 us (0.984)
  transfers between devices with their start and end apart: 10 -> 10, of which waited for: 1 -> 1; matrix products, arithmetic and copies ran while one was open for 0% -> 0% of each run, Pallas kernels for 7% -> 8%
where the time goes in v7:
time: 124 us
  blocking collectives  57.3 us (46%)
  starting transfers between devices  41.9 us (34%)
  Pallas kernels  20.9 us (17%)
  waiting for transfers between devices  2.48 us (2%)
    all_to_all x4, blocking collectives, spread(): lax.all_to_all(rows.reshape(rows.shape[0], 1, 128), axes, 0, 0, tiled=True)  57.3 us
    ppermute x5, starting transfers between devices, trade_second(): lax.ppermute(edge, axes, [(i, (i + (1 if i % 2 else -1)) % count) for i i...  25.3 us
    ppermute x5, starting transfers between devices, trade_first(): return lax.ppermute(edge, axes, [(i, i ^ 1) for i in range(length(axes))])  16.6 us
    pallas_call x1, Pallas kernels, local(): second_call(gram, total, a0, side, za, zb, ca, cb, d, g, g_side, xb, xa,...  3.93 us
    pallas_call x1, Pallas kernels, local(): first_call(gram, u, w, ua, ub, wa, wb, cb, ca, my, py, mx, px)  3.17 us
    pallas_call x1, Pallas kernels, local(): kernel(project_body, 'hhh', [(TILE, f32)] + [(edge, f32)] * 2 + [((FLUOR,...  3.14 us
    pallas_call x1, Pallas kernels, local(): kernel(functools.partial(y_matrices_body, sizes[1]), 's', [((768, 256), b...  2.76 us
    pallas_call x1, Pallas kernels, local(): kernel(functools.partial(x_matrices_body, sizes[0]), 'svv', [((FLUOR, FLU...  2.73 us
  transfers between devices with their start and end apart: 10, of which 1 were waited for; matrix products, arithmetic and copies ran while one was open for 0% of the time, Pallas kernels for 8%

profile of v7, /device:TPU:1, one launch (start us, length us, event | category | flops | bytes accessed | tf_op | source)
XLA Modules:
  0.0 123.6 jit_solution(4460488201339897512)
XLA Ops:
  0.0 3.1 %shard_map.55 = (f32[12,64,128]{2,1,0:T(8,128)}, f32[12,80,128]{2,1,0:T(8,128)}, f32[12,80,128]{2,1,0:T(8,128)}, f32[12,40,128]{2,1,0:T(8,128)}, f32[12,40,128]{2,1,0:T(8,128)}) custom-call(f32[12,32]{1,0:T(8,128)} %bitcast.30, f32[12,64,128]{2,1,0:T(8,128)} %bitcast.20, bf16[32,64,128]{2,1,0:T(8,128)(2,1)} %bitcast.33), custom_call_target="tpu_custom_call" | custom-call | flops 10000000 | bytes 100000 | tf_op jit(solution)/shard_map/pallas_call | solution.py:633
  3.1 6.0 %collective-permute-start.2 = (f32[12,80,128]{2,1,0:T(8,128)}, f32[12,80,128]{2,1,0:T(8,128)S(1)}, u32[]{:S(2)}, u32[]{:S(2)}) collective-permute-start(f32[12,80,128]{2,1,0:T(8,128)} %get-tuple-element.43), channel_id=1, source_target_pairs={{0,480},{32,64},{64,32},{96,128},{128,96},{160,192},{192,160},{224... | collective-permute-start | bytes 1474568 | tf_op jit(solution)/shard_map/ppermute | solution.py:620
  9.2 3.5 %collective-permute-start = (f32[12,40,128]{2,1,0:T(8,128)}, f32[12,40,128]{2,1,0:T(8,128)S(1)}, u32[]{:S(2)}, u32[]{:S(2)}) collective-permute-start(f32[12,40,128]{2,1,0:T(8,128)} %get-tuple-element.37), channel_id=1, source_target_pairs={{0,1},{1,0},{2,3},{3,2},{4,5},{5,4},{6,7},{7,6},{8,9},{9,8},{10,11... | collective-permute-start | bytes 737288 | tf_op jit(solution)/shard_map/ppermute | solution.py:615
  12.7 10.2 %collective-permute-start.1 = (f32[12,40,128]{2,1,0:T(8,128)}, f32[12,40,128]{2,1,0:T(8,128)S(1)}, u32[]{:S(2)}, u32[]{:S(2)}) collective-permute-start(f32[12,40,128]{2,1,0:T(8,128)} %get-tuple-element.38), channel_id=1, source_target_pairs={{0,31},{1,2},{2,1},{3,4},{4,3},{5,6},{6,5},{7,8},{8,7},{9,10},{10,... | collective-permute-start | bytes 737288 | tf_op jit(solution)/shard_map/ppermute | solution.py:620
  23.0 0.0 copy-start.1
  23.0 4.8 %collective-permute-start.3 = (f32[12,80,128]{2,1,0:T(8,128)}, f32[12,80,128]{2,1,0:T(8,128)S(1)}, u32[]{:S(2)}, u32[]{:S(2)}) collective-permute-start(f32[12,80,128]{2,1,0:T(8,128)} %get-tuple-element.48), channel_id=1, source_target_pairs={{0,32},{32,0},{64,96},{96,64},{128,160},{160,128},{192,224},{224,1... | collective-permute-start | bytes 1474568 | tf_op jit(solution)/shard_map/ppermute | solution.py:615
  27.8 0.0 copy-start.3
  27.8 0.6 copy-done.3
  28.4 0.0 copy-start.4
  28.4 2.8 %shard_map.58 = (bf16[768,256]{1,0:T(8,128)(2,1)S(1)}, bf16[768,256]{1,0:T(8,128)(2,1)S(1)}, bf16[768,128]{1,0:T(8,128)(2,1)S(1)}) custom-call(f32[33]{0:T(128)S(1)} %copy-done.3), custom_call_target="tpu_custom_call" | custom-call | flops 1000000000 | bytes 10000000 | tf_op jit(solution)/shard_map/pallas_call | solution.py:653
  31.2 0.0 collective-permute-done.ya_ref
  31.2 0.0 collective-permute-done.1.yb_ref
  31.2 0.6 shard_map.56
  31.8 2.2 %collective-permute-start.4 = (f32[624,128]{1,0:T(8,128)S(1)}, f32[624,128]{1,0:T(8,128)S(1)}, u32[]{:S(2)}, u32[]{:S(2)}) collective-permute-start(f32[624,128]{1,0:T(8,128)S(1)} %get-tuple-element.53), channel_id=1, source_target_pairs={{0,480},{32,64},{64,32},{96,128},{128,96},{160,192},{192,160},{224... | collective-permute-start | bytes 958472 | tf_op jit(solution)/shard_map/ppermute | solution.py:620
  34.0 3.7 %collective-permute-start.5 = (f32[624,128]{1,0:T(8,128)S(1)}, f32[624,128]{1,0:T(8,128)S(1)}, u32[]{:S(2)}, u32[]{:S(2)}) collective-permute-start(f32[624,128]{1,0:T(8,128)S(1)} %get-tuple-element.54), channel_id=1, source_target_pairs={{0,32},{32,0},{64,96},{96,64},{128,160},{160,128},{192,224},{224,1... | collective-permute-start | bytes 958472 | tf_op jit(solution)/shard_map/ppermute | solution.py:615
  37.8 0.0 copy-done.1
  37.8 0.0 copy-done.4
  37.8 0.0 copy-start
  37.8 0.0 copy-start.2
  37.8 2.7 %shard_map.57 = (f32[12,12]{1,0:T(8,128)S(1)}, bf16[96,512]{1,0:T(8,128)(2,1)S(1)}, bf16[96,384]{1,0:T(8,128)(2,1)S(1)}, bf16[64,384]{1,0:T(8,128)(2,1)S(1)}) custom-call(f32[33]{0:T(128)S(1)} %copy-done.4, f32[12,32]{1,0:T(8,128)S(1)} %bitcast.31, f32[12,64,128]{2,1,0:T(8,128)S(1)} %get-tuple-element.39.after_ref.ps_ref), custom_call_target="tpu_custom_call" | custom-call | flops 1000000000 | bytes 10000000 | tf_op jit(solution)/shard_map/pallas_call | solution.py:662
  40.5 0.0 collective-permute-done.2.xb_ref.zb_ref
  40.5 0.0 copy-done
  40.6 0.0 copy-done.2
  40.6 1.1 shard_map.59
  41.6 0.0 collective-permute-done.3.xa_ref.za_ref
  41.6 0.4 shard_map.60
  42.1 2.5 %collective-permute-done.4.cb_ref = f32[624,128]{1,0:T(8,128)S(1)} collective-permute-done((f32[624,128]{1,0:T(8,128)S(1)}, f32[624,128]{1,0:T(8,128)S(1)}, u32[]{:S(2)}, u32[]{:S(2)}) %collective-permute-start.4) | collective-permute-done | bytes 319520 | tf_op jit(solution)/shard_map/ppermute | solution.py:620
  44.5 0.0 collective-permute-done.5.ca_ref
  44.5 3.2 %shard_map.61 = (f32[12,96,256]{2,1,0:T(8,128)S(1)}, f32[12,96,256]{2,1,0:T(8,128)S(1)}, f32[12,24,128]{2,1,0:T(8,128)S(1)}, f32[12,24,128]{2,1,0:T(8,128)S(1)}) custom-call(f32[12,12]{1,0:T(8,128)S(1)} %get-tuple-element.40.gram_ref, f32[12,64,256]{2,1,0:T(8,128)S(1)} %get-tuple-element.46.u_ref, f32[12,64,256]{2,1,0:T(8,128)S(1)} %get-tuple-element.47.w_ref, ...), custom_call_target="tpu_custom_call" | custom-call | flops 1000000000 | bytes 10000000 | tf_op jit(solution)/shard_map/pallas_call | solution.py:675
  47.7 1.9 %collective-permute-start.6 = (f32[12,24,128]{2,1,0:T(8,128)S(1)}, f32[12,24,128]{2,1,0:T(8,128)S(1)}, u32[]{:S(2)}, u32[]{:S(2)}) collective-permute-start(f32[12,24,128]{2,1,0:T(8,128)S(1)} %get-tuple-element.60), channel_id=1, source_target_pairs={{0,1},{1,0},{2,3},{3,2},{4,5},{5,4},{6,7},{7,6},{8,9},{9,8},{10,11... | collective-permute-start | bytes 442376 | tf_op jit(solution)/shard_map/ppermute | solution.py:615
  49.6 4.1 %collective-permute-start.7 = (f32[12,24,128]{2,1,0:T(8,128)S(1)}, f32[12,24,128]{2,1,0:T(8,128)S(1)}, u32[]{:S(2)}, u32[]{:S(2)}) collective-permute-start(f32[12,24,128]{2,1,0:T(8,128)S(1)} %get-tuple-element.61), channel_id=1, source_target_pairs={{0,31},{1,2},{2,1},{3,4},{4,3},{5,6},{6,5},{7,8},{8,7},{9,10},{10,... | collective-permute-start | bytes 442376 | tf_op jit(solution)/shard_map/ppermute | solution.py:620
  53.7 1.7 %shard_map.62 = f32[32,128]{1,0:T(8,128)S(1)} custom-call(f32[12,12]{1,0:T(8,128)S(1)} %get-tuple-element.40.gram_ref, f32[12,96,256]{2,1,0:T(8,128)S(1)} %get-tuple-element.57.g_ref, bf16[768,128]{1,0:T(8,128)(2,1)S(1)} %get-tuple-element.58.by, bf16[64,384]{1,0:T(8,128)(2,1)S(1)} %get-tuple-element.59.bx), custom_call_target="tpu_custom_call" | custom-call | flops 1000000000 | bytes 10000000 | tf_op jit(solution)/shard_map/pallas_call | solution.py:677
  55.5 14.1 %all_to_all.20 = f32[32,1,128]{2,1,0:T(1,128)S(1)} all-to-all(f32[32,1,128]{2,1,0:T(1,128)S(1)} %bitcast.29), channel_id=1, replica_groups=mesh['y'=4,'x_hi'=2,'core'=2,'x_lo'=2,'z'=16] {'y','x_hi','core','x_lo'}, dimensions={0} | all-to-all | bytes 32768 | tf_op jit(solution)/shard_map/all_to_all | solution.py:624
  69.5 0.0 collective-permute-done.6.ya_ref
  69.5 0.0 collective-permute-done.7.yb_ref
  69.5 0.5 shard_map.63
  70.0 2.6 %collective-permute-start.9 = (f32[12,64,128]{2,1,0:T(8,128)S(1)}, f32[12,64,128]{2,1,0:T(8,128)S(1)}, u32[]{:S(2)}, u32[]{:S(2)}) collective-permute-start(f32[12,64,128]{2,1,0:T(8,128)S(1)} %get-tuple-element.65), channel_id=1, source_target_pairs={{0,32},{32,0},{64,96},{96,64},{128,160},{160,128},{192,224},{224,1... | collective-permute-start | bytes 1179656 | tf_op jit(solution)/shard_map/ppermute | solution.py:615
  72.6 2.7 %collective-permute-start.8 = (f32[12,64,128]{2,1,0:T(8,128)S(1)}, f32[12,64,128]{2,1,0:T(8,128)S(1)}, u32[]{:S(2)}, u32[]{:S(2)}) collective-permute-start(f32[12,64,128]{2,1,0:T(8,128)S(1)} %get-tuple-element.65), channel_id=1, source_target_pairs={{0,480},{32,64},{64,32},{96,128},{128,96},{160,192},{192,160},{224... | collective-permute-start | bytes 1179656 | tf_op jit(solution)/shard_map/ppermute | solution.py:620
  75.4 16.5 %all_to_all.21 = f32[16,1,128]{2,1,0:T(1,128)S(1)} all-to-all(f32[16,1,128]{2,1,0:T(1,128)S(1)} %bitcast.32), channel_id=1, replica_groups=mesh['y'=4,'x_hi'=2,'core'=2,'x_lo'=2,'z'=16] {'z'}, dimensions={0} | all-to-all | bytes 16384 | tf_op jit(solution)/shard_map/all_to_all | solution.py:624
  91.8 0.0 collective-permute-done.9.xa_ref
  91.8 0.0 collective-permute-done.8.xb_ref
  91.8 3.9 %shard_map.64 = (f32[12,64,128]{2,1,0:T(8,128)S(1)}, f32[12,64,128]{2,1,0:T(8,128)S(1)}, f32[32,128]{1,0:T(8,128)S(1)}) custom-call(f32[12,12]{1,0:T(8,128)S(1)} %get-tuple-element.40.gram_ref, f32[16,128]{1,0:T(8,128)S(1)} %bitcast.25, f32[12,64,128]{2,1,0:T(8,128)S(1)} %bitcast.22, f32[12,64,128]{2,1,0:T(8,128)S(1)} %get-tuple-element.41.side_ref, ...), custom_call_target="tpu_custom_call" | custom-call | flops 1000000000 | bytes 10000000 | tf_op jit(solution)/shard_map/pallas_call | solution.py:687
  95.8 13.0 %all_to_all.22 = f32[32,1,128]{2,1,0:T(1,128)S(1)} all-to-all(f32[32,1,128]{2,1,0:T(1,128)S(1)} %bitcast.28), channel_id=1, replica_groups=mesh['y'=4,'x_hi'=2,'core'=2,'x_lo'=2,'z'=16] {'y','x_hi','core','x_lo'}, dimensions={0} | all-to-all | bytes 32768 | tf_op jit(solution)/shard_map/all_to_all | solution.py:624
  108.7 13.8 %all_to_all.23 = f32[16,1,128]{2,1,0:T(1,128)S(1)} all-to-all(f32[16,1,128]{2,1,0:T(1,128)S(1)} %bitcast.27), channel_id=1, replica_groups=mesh['y'=4,'x_hi'=2,'core'=2,'x_lo'=2,'z'=16] {'z'}, dimensions={0} | all-to-all | bytes 16384 | tf_op jit(solution)/shard_map/all_to_all | solution.py:624
  122.5 0.9 shard_map.66
  (1 shorter events, 0.0 us)
Async XLA Ops:
  3.1 37.4 %collective-permute-start.2 = (f32[12,80,128]{2,1,0:T(8,128)}, f32[12,80,128]{2,1,0:T(8,128)S(1)}, u32[]{:S(2)}, u32[]{:S(2)}) collective-permute-start(f32[12,80,128]{2,1,0:T(8,128)} %get-tuple-element.43), channel_id=1, source_target_pairs={{0,480},{32,64},{64,32},{96,128},{128,96},{160,192},{192,160},{224... | collective-permute-start | bytes 1474568 | tf_op jit(solution)/shard_map/ppermute | solution.py:620
  9.2 22.0 %collective-permute-start = (f32[12,40,128]{2,1,0:T(8,128)}, f32[12,40,128]{2,1,0:T(8,128)S(1)}, u32[]{:S(2)}, u32[]{:S(2)}) collective-permute-start(f32[12,40,128]{2,1,0:T(8,128)} %get-tuple-element.37), channel_id=1, source_target_pairs={{0,1},{1,0},{2,3},{3,2},{4,5},{5,4},{6,7},{7,6},{8,9},{9,8},{10,11... | collective-permute-start | bytes 737288 | tf_op jit(solution)/shard_map/ppermute | solution.py:615
  12.7 18.5 %collective-permute-start.1 = (f32[12,40,128]{2,1,0:T(8,128)}, f32[12,40,128]{2,1,0:T(8,128)S(1)}, u32[]{:S(2)}, u32[]{:S(2)}) collective-permute-start(f32[12,40,128]{2,1,0:T(8,128)} %get-tuple-element.38), channel_id=1, source_target_pairs={{0,31},{1,2},{2,1},{3,4},{4,3},{5,6},{6,5},{7,8},{8,7},{9,10},{10,... | collective-permute-start | bytes 737288 | tf_op jit(solution)/shard_map/ppermute | solution.py:620
  23.0 14.8 %copy-start.1 = (f32[32,12]{0,1:T(8,128)S(1)}, f32[32,12]{0,1:T(8,128)}, u32[]{:S(2)}) copy-start(f32[32,12]{0,1:T(8,128)} %param.7) | copy-start | bytes 4612
  23.0 18.6 %collective-permute-start.3 = (f32[12,80,128]{2,1,0:T(8,128)}, f32[12,80,128]{2,1,0:T(8,128)S(1)}, u32[]{:S(2)}, u32[]{:S(2)}) collective-permute-start(f32[12,80,128]{2,1,0:T(8,128)} %get-tuple-element.48), channel_id=1, source_target_pairs={{0,32},{32,0},{64,96},{96,64},{128,160},{160,128},{192,224},{224,1... | collective-permute-start | bytes 1474568 | tf_op jit(solution)/shard_map/ppermute | solution.py:615
  27.8 0.7 copy-start.3
  28.4 9.3 %copy-start.4 = (f32[33]{0:T(128)S(1)}, f32[33]{0:T(128)}, u32[]{:S(2)}) copy-start(f32[33]{0:T(128)} %tx_ref.1) | copy-start | bytes 400
  31.8 12.7 %collective-permute-start.4 = (f32[624,128]{1,0:T(8,128)S(1)}, f32[624,128]{1,0:T(8,128)S(1)}, u32[]{:S(2)}, u32[]{:S(2)}) collective-permute-start(f32[624,128]{1,0:T(8,128)S(1)} %get-tuple-element.53), channel_id=1, source_target_pairs={{0,480},{32,64},{64,32},{96,128},{128,96},{160,192},{192,160},{224... | collective-permute-start | bytes 958472 | tf_op jit(solution)/shard_map/ppermute | solution.py:620
  34.0 10.5 %collective-permute-start.5 = (f32[624,128]{1,0:T(8,128)S(1)}, f32[624,128]{1,0:T(8,128)S(1)}, u32[]{:S(2)}, u32[]{:S(2)}) collective-permute-start(f32[624,128]{1,0:T(8,128)S(1)} %get-tuple-element.54), channel_id=1, source_target_pairs={{0,32},{32,0},{64,96},{96,64},{128,160},{160,128},{192,224},{224,1... | collective-permute-start | bytes 958472 | tf_op jit(solution)/shard_map/ppermute | solution.py:615
  37.8 2.8 %copy-start = (f32[1,12,64,128]{3,2,1,0:T(8,128)S(1)}, f32[1,12,64,128]{3,2,1,0:T(8,128)}, u32[]{:S(2)}) copy-start(f32[1,12,64,128]{3,2,1,0:T(8,128)} %param.5) | copy-start | bytes 1179652
  37.8 2.8 %copy-start.2 = (f32[12,64,128]{2,1,0:T(8,128)S(1)}, f32[12,64,128]{2,1,0:T(8,128)}, u32[]{:S(2)}) copy-start(f32[12,64,128]{2,1,0:T(8,128)} %get-tuple-element.42.p_ref) | copy-start | bytes 1179652
  47.7 21.8 %collective-permute-start.6 = (f32[12,24,128]{2,1,0:T(8,128)S(1)}, f32[12,24,128]{2,1,0:T(8,128)S(1)}, u32[]{:S(2)}, u32[]{:S(2)}) collective-permute-start(f32[12,24,128]{2,1,0:T(8,128)S(1)} %get-tuple-element.60), channel_id=1, source_target_pairs={{0,1},{1,0},{2,3},{3,2},{4,5},{5,4},{6,7},{7,6},{8,9},{9,8},{10,11... | collective-permute-start | bytes 442376 | tf_op jit(solution)/shard_map/ppermute | solution.py:615
  49.6 19.9 %collective-permute-start.7 = (f32[12,24,128]{2,1,0:T(8,128)S(1)}, f32[12,24,128]{2,1,0:T(8,128)S(1)}, u32[]{:S(2)}, u32[]{:S(2)}) collective-permute-start(f32[12,24,128]{2,1,0:T(8,128)S(1)} %get-tuple-element.61), channel_id=1, source_target_pairs={{0,31},{1,2},{2,1},{3,4},{4,3},{5,6},{6,5},{7,8},{8,7},{9,10},{10,... | collective-permute-start | bytes 442376 | tf_op jit(solution)/shard_map/ppermute | solution.py:620
  70.0 21.8 %collective-permute-start.9 = (f32[12,64,128]{2,1,0:T(8,128)S(1)}, f32[12,64,128]{2,1,0:T(8,128)S(1)}, u32[]{:S(2)}, u32[]{:S(2)}) collective-permute-start(f32[12,64,128]{2,1,0:T(8,128)S(1)} %get-tuple-element.65), channel_id=1, source_target_pairs={{0,32},{32,0},{64,96},{96,64},{128,160},{160,128},{192,224},{224,1... | collective-permute-start | bytes 1179656 | tf_op jit(solution)/shard_map/ppermute | solution.py:615
  72.6 19.2 %collective-permute-start.8 = (f32[12,64,128]{2,1,0:T(8,128)S(1)}, f32[12,64,128]{2,1,0:T(8,128)S(1)}, u32[]{:S(2)}, u32[]{:S(2)}) collective-permute-start(f32[12,64,128]{2,1,0:T(8,128)S(1)} %get-tuple-element.65), channel_id=1, source_target_pairs={{0,480},{32,64},{64,32},{96,128},{128,96},{160,192},{192,160},{224... | collective-permute-start | bytes 1179656 | tf_op jit(solution)/shard_map/ppermute | solution.py:620

commit v8 on v7

--- a/solution.py
+++ b/solution.py
@@ -376,14 +376,14 @@
     for start in range(0, ROWS, 8):
         part = [z_ref[f, start : start + 8, :] for f in range(FLUOR)]
         for f in range(FLUOR):
-            acc = gram_ref[f, 0] * part[0]
-            for k in range(1, FLUOR):
+            acc = 0.5 * gram_ref[f, f] * part[f]
+            for k in range(f):
                 acc = acc + gram_ref[f, k] * part[k]
             image = image + acc * part[f]
             g = g_ref[f, G_HALO + start : G_HALO + start + 8, :COLS]
             grad = grad + g * g
     grad = jnp.sum(grad, axis=0, keepdims=True)
-    image = jnp.sum(image, axis=0, keepdims=True)
+    image = 2.0 * jnp.sum(image, axis=0, keepdims=True)
     lane = lane_of((1, 128))
     row = jnp.where(lane < 64, grad + roll(grad, 64), image + roll(image, 64))
     sum_ref[...] = jnp.broadcast_to(row, sum_ref.shape)

time: 124 us -> 124 us (level)
  transfers between devices with their start and end apart: 10 -> 10, of which waited for: 1 -> 1; matrix products, arithmetic and copies ran while one was open for 0% -> 0% of each run, Pallas kernels for 8% -> 7%
where the time goes in v8:
time: 124 us; the launch traced here: 123 us
  blocking collectives  57.3 us (46%)
  starting transfers between devices  41.9 us (34%)
  Pallas kernels  20.6 us (17%)
  waiting for transfers between devices  2.48 us (2%)
    all_to_all x4, blocking collectives, spread(): lax.all_to_all(rows.reshape(rows.shape[0], 1, 128), axes, 0, 0, tiled=True)  57.3 us
    ppermute x5, starting transfers between devices, trade_second(): lax.ppermute(edge, axes, [(i, (i + (1 if i % 2 else -1)) % count) for i i...  25.3 us
    ppermute x5, starting transfers between devices, trade_first(): return lax.ppermute(edge, axes, [(i, i ^ 1) for i in range(length(axes))])  16.6 us
    pallas_call x1, Pallas kernels, local(): second_call(gram, total, a0, side, za, zb, ca, cb, d, g, g_side, xb, xa,...  3.77 us
    pallas_call x1, Pallas kernels, local(): first_call(gram, u, w, ua, ub, wa, wb, cb, ca, my, py, mx, px)  3.17 us
    pallas_call x1, Pallas kernels, local(): kernel(project_body, 'hhh', [(TILE, f32)] + [(edge, f32)] * 2 + [((FLUOR,...  3.14 us
    pallas_call x1, Pallas kernels, local(): kernel(functools.partial(y_matrices_body, sizes[1]), 's', [((768, 256), b...  2.76 us
    pallas_call x1, Pallas kernels, local(): kernel(functools.partial(x_matrices_body, sizes[0]), 'svv', [((FLUOR, FLU...  2.73 us
  transfers between devices with their start and end apart: 10, of which 1 were waited for; matrix products, arithmetic and copies ran while one was open for 0% of the time, Pallas kernels for 7%

profile of v8, /device:TPU:1, one launch (start us, length us, event | category | flops | bytes accessed | tf_op | source)
XLA Modules:
  0.0 123.3 jit_solution(15765923055825561559)
XLA Ops:
  0.0 3.1 %shard_map.55 = (f32[12,64,128]{2,1,0:T(8,128)}, f32[12,80,128]{2,1,0:T(8,128)}, f32[12,80,128]{2,1,0:T(8,128)}, f32[12,40,128]{2,1,0:T(8,128)}, f32[12,40,128]{2,1,0:T(8,128)}) custom-call(f32[12,32]{1,0:T(8,128)} %bitcast.30, f32[12,64,128]{2,1,0:T(8,128)} %bitcast.20, bf16[32,64,128]{2,1,0:T(8,128)(2,1)} %bitcast.33), custom_call_target="tpu_custom_call" | custom-call | flops 10000000 | bytes 100000 | tf_op jit(solution)/shard_map/pallas_call | solution.py:633
  3.1 6.0 %collective-permute-start.2 = (f32[12,80,128]{2,1,0:T(8,128)}, f32[12,80,128]{2,1,0:T(8,128)S(1)}, u32[]{:S(2)}, u32[]{:S(2)}) collective-permute-start(f32[12,80,128]{2,1,0:T(8,128)} %get-tuple-element.43), channel_id=1, source_target_pairs={{0,480},{32,64},{64,32},{96,128},{128,96},{160,192},{192,160},{224... | collective-permute-start | bytes 1474568 | tf_op jit(solution)/shard_map/ppermute | solution.py:620
  9.2 3.5 %collective-permute-start = (f32[12,40,128]{2,1,0:T(8,128)}, f32[12,40,128]{2,1,0:T(8,128)S(1)}, u32[]{:S(2)}, u32[]{:S(2)}) collective-permute-start(f32[12,40,128]{2,1,0:T(8,128)} %get-tuple-element.37), channel_id=1, source_target_pairs={{0,1},{1,0},{2,3},{3,2},{4,5},{5,4},{6,7},{7,6},{8,9},{9,8},{10,11... | collective-permute-start | bytes 737288 | tf_op jit(solution)/shard_map/ppermute | solution.py:615
  12.7 10.2 %collective-permute-start.1 = (f32[12,40,128]{2,1,0:T(8,128)}, f32[12,40,128]{2,1,0:T(8,128)S(1)}, u32[]{:S(2)}, u32[]{:S(2)}) collective-permute-start(f32[12,40,128]{2,1,0:T(8,128)} %get-tuple-element.38), channel_id=1, source_target_pairs={{0,31},{1,2},{2,1},{3,4},{4,3},{5,6},{6,5},{7,8},{8,7},{9,10},{10,... | collective-permute-start | bytes 737288 | tf_op jit(solution)/shard_map/ppermute | solution.py:620
  23.0 0.0 copy-start.1
  23.0 4.8 %collective-permute-start.3 = (f32[12,80,128]{2,1,0:T(8,128)}, f32[12,80,128]{2,1,0:T(8,128)S(1)}, u32[]{:S(2)}, u32[]{:S(2)}) collective-permute-start(f32[12,80,128]{2,1,0:T(8,128)} %get-tuple-element.48), channel_id=1, source_target_pairs={{0,32},{32,0},{64,96},{96,64},{128,160},{160,128},{192,224},{224,1... | collective-permute-start | bytes 1474568 | tf_op jit(solution)/shard_map/ppermute | solution.py:615
  27.8 0.0 copy-start.3
  27.8 0.6 copy-done.3
  28.4 0.0 copy-start.4
  28.4 2.8 %shard_map.58 = (bf16[768,256]{1,0:T(8,128)(2,1)S(1)}, bf16[768,256]{1,0:T(8,128)(2,1)S(1)}, bf16[768,128]{1,0:T(8,128)(2,1)S(1)}) custom-call(f32[33]{0:T(128)S(1)} %copy-done.3), custom_call_target="tpu_custom_call" | custom-call | flops 1000000000 | bytes 10000000 | tf_op jit(solution)/shard_map/pallas_call | solution.py:653
  31.2 0.0 collective-permute-done.ya_ref
  31.2 0.0 collective-permute-done.1.yb_ref
  31.2 0.6 shard_map.56
  31.8 2.2 %collective-permute-start.4 = (f32[624,128]{1,0:T(8,128)S(1)}, f32[624,128]{1,0:T(8,128)S(1)}, u32[]{:S(2)}, u32[]{:S(2)}) collective-permute-start(f32[624,128]{1,0:T(8,128)S(1)} %get-tuple-element.53), channel_id=1, source_target_pairs={{0,480},{32,64},{64,32},{96,128},{128,96},{160,192},{192,160},{224... | collective-permute-start | bytes 958472 | tf_op jit(solution)/shard_map/ppermute | solution.py:620
  34.0 3.7 %collective-permute-start.5 = (f32[624,128]{1,0:T(8,128)S(1)}, f32[624,128]{1,0:T(8,128)S(1)}, u32[]{:S(2)}, u32[]{:S(2)}) collective-permute-start(f32[624,128]{1,0:T(8,128)S(1)} %get-tuple-element.54), channel_id=1, source_target_pairs={{0,32},{32,0},{64,96},{96,64},{128,160},{160,128},{192,224},{224,1... | collective-permute-start | bytes 958472 | tf_op jit(solution)/shard_map/ppermute | solution.py:615
  37.8 0.0 copy-done.1
  37.8 0.0 copy-done.4
  37.8 0.0 copy-start
  37.8 0.0 copy-start.2
  37.8 2.7 %shard_map.57 = (f32[12,12]{1,0:T(8,128)S(1)}, bf16[96,512]{1,0:T(8,128)(2,1)S(1)}, bf16[96,384]{1,0:T(8,128)(2,1)S(1)}, bf16[64,384]{1,0:T(8,128)(2,1)S(1)}) custom-call(f32[33]{0:T(128)S(1)} %copy-done.4, f32[12,32]{1,0:T(8,128)S(1)} %bitcast.31, f32[12,64,128]{2,1,0:T(8,128)S(1)} %get-tuple-element.39.after_ref.ps_ref), custom_call_target="tpu_custom_call" | custom-call | flops 1000000000 | bytes 10000000 | tf_op jit(solution)/shard_map/pallas_call | solution.py:662
  40.5 0.0 collective-permute-done.2.xb_ref.zb_ref
  40.5 0.0 copy-done
  40.6 0.0 copy-done.2
  40.6 1.1 shard_map.59
  41.6 0.0 collective-permute-done.3.xa_ref.za_ref
  41.6 0.4 shard_map.60
  42.1 2.5 %collective-permute-done.4.cb_ref = f32[624,128]{1,0:T(8,128)S(1)} collective-permute-done((f32[624,128]{1,0:T(8,128)S(1)}, f32[624,128]{1,0:T(8,128)S(1)}, u32[]{:S(2)}, u32[]{:S(2)}) %collective-permute-start.4) | collective-permute-done | bytes 319520 | tf_op jit(solution)/shard_map/ppermute | solution.py:620
  44.5 0.0 collective-permute-done.5.ca_ref
  44.5 3.2 %shard_map.61 = (f32[12,96,256]{2,1,0:T(8,128)S(1)}, f32[12,96,256]{2,1,0:T(8,128)S(1)}, f32[12,24,128]{2,1,0:T(8,128)S(1)}, f32[12,24,128]{2,1,0:T(8,128)S(1)}) custom-call(f32[12,12]{1,0:T(8,128)S(1)} %get-tuple-element.40.gram_ref, f32[12,64,256]{2,1,0:T(8,128)S(1)} %get-tuple-element.46.u_ref, f32[12,64,256]{2,1,0:T(8,128)S(1)} %get-tuple-element.47.w_ref, ...), custom_call_target="tpu_custom_call" | custom-call | flops 1000000000 | bytes 10000000 | tf_op jit(solution)/shard_map/pallas_call | solution.py:675
  47.7 1.9 %collective-permute-start.6 = (f32[12,24,128]{2,1,0:T(8,128)S(1)}, f32[12,24,128]{2,1,0:T(8,128)S(1)}, u32[]{:S(2)}, u32[]{:S(2)}) collective-permute-start(f32[12,24,128]{2,1,0:T(8,128)S(1)} %get-tuple-element.60), channel_id=1, source_target_pairs={{0,1},{1,0},{2,3},{3,2},{4,5},{5,4},{6,7},{7,6},{8,9},{9,8},{10,11... | collective-permute-start | bytes 442376 | tf_op jit(solution)/shard_map/ppermute | solution.py:615
  49.6 4.1 %collective-permute-start.7 = (f32[12,24,128]{2,1,0:T(8,128)S(1)}, f32[12,24,128]{2,1,0:T(8,128)S(1)}, u32[]{:S(2)}, u32[]{:S(2)}) collective-permute-start(f32[12,24,128]{2,1,0:T(8,128)S(1)} %get-tuple-element.61), channel_id=1, source_target_pairs={{0,31},{1,2},{2,1},{3,4},{4,3},{5,6},{6,5},{7,8},{8,7},{9,10},{10,... | collective-permute-start | bytes 442376 | tf_op jit(solution)/shard_map/ppermute | solution.py:620
  53.7 1.6 %shard_map.62 = f32[32,128]{1,0:T(8,128)S(1)} custom-call(f32[12,12]{1,0:T(8,128)S(1)} %get-tuple-element.40.gram_ref, f32[12,96,256]{2,1,0:T(8,128)S(1)} %get-tuple-element.57.g_ref, bf16[768,128]{1,0:T(8,128)(2,1)S(1)} %get-tuple-element.58.by, bf16[64,384]{1,0:T(8,128)(2,1)S(1)} %get-tuple-element.59.bx), custom_call_target="tpu_custom_call" | custom-call | flops 1000000000 | bytes 10000000 | tf_op jit(solution)/shard_map/pallas_call | solution.py:677
  55.4 14.1 %all_to_all.20 = f32[32,1,128]{2,1,0:T(1,128)S(1)} all-to-all(f32[32,1,128]{2,1,0:T(1,128)S(1)} %bitcast.29), channel_id=1, replica_groups=mesh['y'=4,'x_hi'=2,'core'=2,'x_lo'=2,'z'=16] {'y','x_hi','core','x_lo'}, dimensions={0} | all-to-all | bytes 32768 | tf_op jit(solution)/shard_map/all_to_all | solution.py:624
  69.4 0.0 collective-permute-done.6.ya_ref
  69.4 0.0 collective-permute-done.7.yb_ref
  69.4 0.5 shard_map.63
  69.9 2.6 %collective-permute-start.9 = (f32[12,64,128]{2,1,0:T(8,128)S(1)}, f32[12,64,128]{2,1,0:T(8,128)S(1)}, u32[]{:S(2)}, u32[]{:S(2)}) collective-permute-start(f32[12,64,128]{2,1,0:T(8,128)S(1)} %get-tuple-element.65), channel_id=1, source_target_pairs={{0,32},{32,0},{64,96},{96,64},{128,160},{160,128},{192,224},{224,1... | collective-permute-start | bytes 1179656 | tf_op jit(solution)/shard_map/ppermute | solution.py:615
  72.5 2.7 %collective-permute-start.8 = (f32[12,64,128]{2,1,0:T(8,128)S(1)}, f32[12,64,128]{2,1,0:T(8,128)S(1)}, u32[]{:S(2)}, u32[]{:S(2)}) collective-permute-start(f32[12,64,128]{2,1,0:T(8,128)S(1)} %get-tuple-element.65), channel_id=1, source_target_pairs={{0,480},{32,64},{64,32},{96,128},{128,96},{160,192},{192,160},{224... | collective-permute-start | bytes 1179656 | tf_op jit(solution)/shard_map/ppermute | solution.py:620
  75.3 16.5 %all_to_all.21 = f32[16,1,128]{2,1,0:T(1,128)S(1)} all-to-all(f32[16,1,128]{2,1,0:T(1,128)S(1)} %bitcast.32), channel_id=1, replica_groups=mesh['y'=4,'x_hi'=2,'core'=2,'x_lo'=2,'z'=16] {'z'}, dimensions={0} | all-to-all | bytes 16384 | tf_op jit(solution)/shard_map/all_to_all | solution.py:624
  91.7 0.0 collective-permute-done.9.xa_ref
  91.7 0.0 collective-permute-done.8.xb_ref
  91.7 3.8 %shard_map.64 = (f32[12,64,128]{2,1,0:T(8,128)S(1)}, f32[12,64,128]{2,1,0:T(8,128)S(1)}, f32[32,128]{1,0:T(8,128)S(1)}) custom-call(f32[12,12]{1,0:T(8,128)S(1)} %get-tuple-element.40.gram_ref, f32[16,128]{1,0:T(8,128)S(1)} %bitcast.25, f32[12,64,128]{2,1,0:T(8,128)S(1)} %bitcast.22, f32[12,64,128]{2,1,0:T(8,128)S(1)} %get-tuple-element.41.side_ref, ...), custom_call_target="tpu_custom_call" | custom-call | flops 1000000000 | bytes 10000000 | tf_op jit(solution)/shard_map/pallas_call | solution.py:687
  95.5 13.0 %all_to_all.22 = f32[32,1,128]{2,1,0:T(1,128)S(1)} all-to-all(f32[32,1,128]{2,1,0:T(1,128)S(1)} %bitcast.28), channel_id=1, replica_groups=mesh['y'=4,'x_hi'=2,'core'=2,'x_lo'=2,'z'=16] {'y','x_hi','core','x_lo'}, dimensions={0} | all-to-all | bytes 32768 | tf_op jit(solution)/shard_map/all_to_all | solution.py:624
  108.5 13.8 %all_to_all.23 = f32[16,1,128]{2,1,0:T(1,128)S(1)} all-to-all(f32[16,1,128]{2,1,0:T(1,128)S(1)} %bitcast.27), channel_id=1, replica_groups=mesh['y'=4,'x_hi'=2,'core'=2,'x_lo'=2,'z'=16] {'z'}, dimensions={0} | all-to-all | bytes 16384 | tf_op jit(solution)/shard_map/all_to_all | solution.py:624
  122.3 0.9 shard_map.66
  (1 shorter events, 0.0 us)
Async XLA Ops:
  3.1 37.4 %collective-permute-start.2 = (f32[12,80,128]{2,1,0:T(8,128)}, f32[12,80,128]{2,1,0:T(8,128)S(1)}, u32[]{:S(2)}, u32[]{:S(2)}) collective-permute-start(f32[12,80,128]{2,1,0:T(8,128)} %get-tuple-element.43), channel_id=1, source_target_pairs={{0,480},{32,64},{64,32},{96,128},{128,96},{160,192},{192,160},{224... | collective-permute-start | bytes 1474568 | tf_op jit(solution)/shard_map/ppermute | solution.py:620
  9.2 22.0 %collective-permute-start = (f32[12,40,128]{2,1,0:T(8,128)}, f32[12,40,128]{2,1,0:T(8,128)S(1)}, u32[]{:S(2)}, u32[]{:S(2)}) collective-permute-start(f32[12,40,128]{2,1,0:T(8,128)} %get-tuple-element.37), channel_id=1, source_target_pairs={{0,1},{1,0},{2,3},{3,2},{4,5},{5,4},{6,7},{7,6},{8,9},{9,8},{10,11... | collective-permute-start | bytes 737288 | tf_op jit(solution)/shard_map/ppermute | solution.py:615
  12.7 18.5 %collective-permute-start.1 = (f32[12,40,128]{2,1,0:T(8,128)}, f32[12,40,128]{2,1,0:T(8,128)S(1)}, u32[]{:S(2)}, u32[]{:S(2)}) collective-permute-start(f32[12,40,128]{2,1,0:T(8,128)} %get-tuple-element.38), channel_id=1, source_target_pairs={{0,31},{1,2},{2,1},{3,4},{4,3},{5,6},{6,5},{7,8},{8,7},{9,10},{10,... | collective-permute-start | bytes 737288 | tf_op jit(solution)/shard_map/ppermute | solution.py:620
  23.0 14.8 %copy-start.1 = (f32[32,12]{0,1:T(8,128)S(1)}, f32[32,12]{0,1:T(8,128)}, u32[]{:S(2)}) copy-start(f32[32,12]{0,1:T(8,128)} %param.7) | copy-start | bytes 4612
  23.0 18.6 %collective-permute-start.3 = (f32[12,80,128]{2,1,0:T(8,128)}, f32[12,80,128]{2,1,0:T(8,128)S(1)}, u32[]{:S(2)}, u32[]{:S(2)}) collective-permute-start(f32[12,80,128]{2,1,0:T(8,128)} %get-tuple-element.48), channel_id=1, source_target_pairs={{0,32},{32,0},{64,96},{96,64},{128,160},{160,128},{192,224},{224,1... | collective-permute-start | bytes 1474568 | tf_op jit(solution)/shard_map/ppermute | solution.py:615
  27.8 0.7 copy-start.3
  28.4 9.3 %copy-start.4 = (f32[33]{0:T(128)S(1)}, f32[33]{0:T(128)}, u32[]{:S(2)}) copy-start(f32[33]{0:T(128)} %tx_ref.1) | copy-start | bytes 400
  31.8 12.7 %collective-permute-start.4 = (f32[624,128]{1,0:T(8,128)S(1)}, f32[624,128]{1,0:T(8,128)S(1)}, u32[]{:S(2)}, u32[]{:S(2)}) collective-permute-start(f32[624,128]{1,0:T(8,128)S(1)} %get-tuple-element.53), channel_id=1, source_target_pairs={{0,480},{32,64},{64,32},{96,128},{128,96},{160,192},{192,160},{224... | collective-permute-start | bytes 958472 | tf_op jit(solution)/shard_map/ppermute | solution.py:620
  34.0 10.5 %collective-permute-start.5 = (f32[624,128]{1,0:T(8,128)S(1)}, f32[624,128]{1,0:T(8,128)S(1)}, u32[]{:S(2)}, u32[]{:S(2)}) collective-permute-start(f32[624,128]{1,0:T(8,128)S(1)} %get-tuple-element.54), channel_id=1, source_target_pairs={{0,32},{32,0},{64,96},{96,64},{128,160},{160,128},{192,224},{224,1... | collective-permute-start | bytes 958472 | tf_op jit(solution)/shard_map/ppermute | solution.py:615
  37.8 2.8 %copy-start = (f32[1,12,64,128]{3,2,1,0:T(8,128)S(1)}, f32[1,12,64,128]{3,2,1,0:T(8,128)}, u32[]{:S(2)}) copy-start(f32[1,12,64,128]{3,2,1,0:T(8,128)} %param.5) | copy-start | bytes 1179652
  37.8 2.8 %copy-start.2 = (f32[12,64,128]{2,1,0:T(8,128)S(1)}, f32[12,64,128]{2,1,0:T(8,128)}, u32[]{:S(2)}) copy-start(f32[12,64,128]{2,1,0:T(8,128)} %get-tuple-element.42.p_ref) | copy-start | bytes 1179652
  47.7 21.7 %collective-permute-start.6 = (f32[12,24,128]{2,1,0:T(8,128)S(1)}, f32[12,24,128]{2,1,0:T(8,128)S(1)}, u32[]{:S(2)}, u32[]{:S(2)}) collective-permute-start(f32[12,24,128]{2,1,0:T(8,128)S(1)} %get-tuple-element.60), channel_id=1, source_target_pairs={{0,1},{1,0},{2,3},{3,2},{4,5},{5,4},{6,7},{7,6},{8,9},{9,8},{10,11... | collective-permute-start | bytes 442376 | tf_op jit(solution)/shard_map/ppermute | solution.py:615
  49.6 19.8 %collective-permute-start.7 = (f32[12,24,128]{2,1,0:T(8,128)S(1)}, f32[12,24,128]{2,1,0:T(8,128)S(1)}, u32[]{:S(2)}, u32[]{:S(2)}) collective-permute-start(f32[12,24,128]{2,1,0:T(8,128)S(1)} %get-tuple-element.61), channel_id=1, source_target_pairs={{0,31},{1,2},{2,1},{3,4},{4,3},{5,6},{6,5},{7,8},{8,7},{9,10},{10,... | collective-permute-start | bytes 442376 | tf_op jit(solution)/shard_map/ppermute | solution.py:620
  69.9 21.8 %collective-permute-start.9 = (f32[12,64,128]{2,1,0:T(8,128)S(1)}, f32[12,64,128]{2,1,0:T(8,128)S(1)}, u32[]{:S(2)}, u32[]{:S(2)}) collective-permute-start(f32[12,64,128]{2,1,0:T(8,128)S(1)} %get-tuple-element.65), channel_id=1, source_target_pairs={{0,32},{32,0},{64,96},{96,64},{128,160},{160,128},{192,224},{224,1... | collective-permute-start | bytes 1179656 | tf_op jit(solution)/shard_map/ppermute | solution.py:615
  72.5 19.2 %collective-permute-start.8 = (f32[12,64,128]{2,1,0:T(8,128)S(1)}, f32[12,64,128]{2,1,0:T(8,128)S(1)}, u32[]{:S(2)}, u32[]{:S(2)}) collective-permute-start(f32[12,64,128]{2,1,0:T(8,128)S(1)} %get-tuple-element.65), channel_id=1, source_target_pairs={{0,480},{32,64},{64,32},{96,128},{128,96},{160,192},{192,160},{224... | collective-permute-start | bytes 1179656 | tf_op jit(solution)/shard_map/ppermute | solution.py:620
